TPU v7x, 256 devices: a whole 4x4x8 slice. The times are simulated.
256 devices in a mesh: gx: 2 (over core), gy: 64 (over z, y, x_hi), rep: 2 (over x_lo).
Axes of the slice: x: 4 (x_hi: 2, x_lo: 2; x = x_hi * 2 + x_lo), y: 4, z: 8, core: 2. Of those that a mesh axis runs over, the one named last changes fastest.
Arguments:
- feats: bfloat16 [262144, 256], P(('gx', 'gy', 'rep')), may hold values from -6 to 6
- weight: bfloat16 [27, 256, 256], P(None, None, 'rep'), may hold values from -0.109375 to 0.109375
- cotan: bfloat16 [262144, 256], P(('gx', 'gy', 'rep')), may hold values from -24 to 24
- face_send: int32 [256, 4, 4], P(('gx', 'gy', 'rep')), may hold values from 0 to 7
- corner_send: int32 [256, 4, 1], P(('gx', 'gy', 'rep')), may hold values from 0 to 7
- pair_out: int32 [256, 27, 4], P(('gx', 'gy', 'rep')), may hold values from 0 to 7
- pair_in: int32 [256, 27, 4], P(('gx', 'gy', 'rep')), may hold values from 0 to 28
- row_map: int32 [256, 27, 4, 128], P(('gx', 'gy', 'rep')), may hold values from 0 to 128
Outputs:
- activation: bfloat16 [262144, 256], P(('gx', 'gy', 'rep'))
- input_grad: bfloat16 [262144, 256], P(('gx', 'gy', 'rep'))
- weight_grad: float32 [27, 256, 256], P(None, None, 'rep')
All inputs are finite; a program needn't handle non-finite values.
Results may differ from a plain program's by a relative error of at most 0.007.
Values may be sent and summed in bfloat16 or wider, within the bound.
No kernel may reach another device: no remote copies, remote signals or barrier semaphores. Data moves between devices by JAX's collectives and lax.ppermute only.
A program may use at most 128 MiB of HBM per device.

v0:
```python
import jax
import jax.numpy as jnp
from jax import lax
from jax.sharding import PartitionSpec as P


def from_behind(value, axis, steps):
    count = lax.axis_size(axis)
    initial, last = (max(0, -steps), min(count, count - steps))
    return lax.ppermute(value, axis, [(source, source + steps) for source in range(initial, last)])


def silu_grad(values):
    sigma = jax.nn.sigmoid(values)
    return sigma * (1.0 + values * (1.0 - sigma))


def gather_rows(flat_rows, ins_k, map_k, zero_row):
    source = ins_k[:, None] * 128 + map_k
    source = jnp.where(map_k == 128, zero_row, source)
    return (flat_rows[source], source)


def flatten_ext(ext_blocks):
    channels = ext_blocks.shape[2]
    flat_rows = jnp.concatenate(
        [ext_blocks.reshape(-1, channels), jnp.zeros((1, channels), ext_blocks.dtype)], 0
    )
    return (flat_rows, ext_blocks.shape[0] * 128)


def forward_local(ext_blocks, weight, outs_all, ins_all, maps_all, block_count):
    channels = ext_blocks.shape[2]
    flat_rows, zero_row = flatten_ext(ext_blocks)
    block_ids = jnp.arange(block_count, dtype=jnp.int32)

    def forward_one_offset(running, packed):
        weight_k, outs_k, ins_k, map_k = packed
        rows_k, source = gather_rows(flat_rows, ins_k, map_k, zero_row)
        pieces_count = rows_k.shape[0]
        product = jnp.dot(
            rows_k.reshape(-1, channels), weight_k, preferred_element_type=jnp.float32
        )
        product = product.reshape(pieces_count, 128, channels)
        select = (outs_k[None, :] == block_ids[:, None]).astype(jnp.float32)
        added = jnp.einsum("bp,prc->brc", select, product, precision=lax.Precision.HIGHEST)
        return (running + added, None)

    start_sum = jnp.zeros((block_count, 128, channels), jnp.float32)
    pre_act, unused_out = lax.scan(
        forward_one_offset, start_sum, (weight, outs_all, ins_all, maps_all)
    )
    return pre_act


def backward_local(ext_blocks, weight, outs_all, ins_all, maps_all, pre_grad):
    channels = ext_blocks.shape[2]
    flat_rows, zero_row = flatten_ext(ext_blocks)

    def backward_one_offset(grad_rows, packed):
        weight_k, outs_k, ins_k, map_k = packed
        rows_k, source = gather_rows(flat_rows, ins_k, map_k, zero_row)
        upstream = pre_grad[outs_k]
        flat_up = upstream.reshape(-1, channels)
        back_rows = lax.dot_general(
            flat_up, weight_k, (((1,), (1,)), ((), ())), preferred_element_type=jnp.float32
        )
        grad_rows = grad_rows.at[source.reshape(-1)].add(back_rows)
        weight_piece = lax.dot_general(
            rows_k.reshape(-1, channels),
            flat_up,
            (((0,), (0,)), ((), ())),
            preferred_element_type=jnp.float32,
        )
        return (grad_rows, weight_piece)

    start_rows = jnp.zeros((zero_row + 1, channels), jnp.float32)
    grad_rows, weight_part = lax.scan(
        backward_one_offset, start_rows, (weight, outs_all, ins_all, maps_all)
    )
    ext_grad = grad_rows[:zero_row].reshape(-1, 128, channels)
    return (ext_grad, weight_part)


def move_along_x(to_minus, to_plus):
    arrived = []
    for shift_by, payload in ((1, to_plus), (-1, to_minus)):
        arrived.append(from_behind(payload, "gx", shift_by))
    return (arrived[0], arrived[1])


def move_along_y(to_minus, to_plus):
    arrived = []
    for shift_by, payload in ((1, to_plus), (-1, to_minus)):
        arrived.append(from_behind(payload, "gy", shift_by))
    return (arrived[0], arrived[1])


def body(feats, weight, cotan, face_send, corner_send, pair_out, pair_in, row_map):
    channels = feats.shape[1]
    block_count = feats.shape[0] // 128
    local_blocks = feats.reshape(block_count, 128, channels)
    face_list = face_send[0]
    corner_list = corner_send[0]
    outs_all = pair_out[0]
    ins_all = pair_in[0]
    maps_all = row_map[0]
    face_end = face_list.shape[1]
    corner_end = face_end + corner_list.shape[1]
    corner_size = corner_list.shape[1]

    def take_blocks(listed):
        return jnp.take(local_blocks, listed, axis=0)

    full_weight = lax.all_gather(weight, "rep", axis=2, tiled=True)
    to_plus_x = jnp.concatenate(
        [take_blocks(face_list[1]), take_blocks(corner_list[2]), take_blocks(corner_list[3])], 0
    )
    to_minus_x = jnp.concatenate(
        [take_blocks(face_list[0]), take_blocks(corner_list[0]), take_blocks(corner_list[1])], 0
    )
    from_minus_x, from_plus_x = move_along_x(to_minus_x, to_plus_x)
    to_plus_y = jnp.concatenate(
        [take_blocks(face_list[3]), from_minus_x[corner_end:], from_plus_x[corner_end:]], 0
    )
    to_minus_y = jnp.concatenate(
        [
            take_blocks(face_list[2]),
            from_minus_x[face_end:corner_end],
            from_plus_x[face_end:corner_end],
        ],
        0,
    )
    from_minus_y, from_plus_y = move_along_y(to_minus_y, to_plus_y)
    ext_blocks = jnp.concatenate(
        [
            local_blocks,
            from_minus_x[:face_end],
            from_plus_x[:face_end],
            from_minus_y[:face_end],
            from_plus_y[:face_end],
            from_minus_y[face_end:corner_end],
            from_plus_y[face_end:corner_end],
            from_minus_y[corner_end:],
            from_plus_y[corner_end:],
            jnp.zeros((1, 128, channels), jnp.bfloat16),
        ],
        0,
    )
    pre_act = forward_local(ext_blocks, full_weight, outs_all, ins_all, maps_all, block_count)
    activation = jax.nn.silu(pre_act).astype(jnp.bfloat16)
    cot_blocks = cotan.reshape(block_count, 128, channels)
    pre_grad = (cot_blocks.astype(jnp.float32) * silu_grad(pre_act)).astype(jnp.bfloat16)
    ext_grad, weight_part = backward_local(
        ext_blocks, full_weight, outs_all, ins_all, maps_all, pre_grad
    )
    ext_count = ext_blocks.shape[0] - 1
    halo_grad = ext_grad[block_count:ext_count].astype(jnp.bfloat16)

    def face_grad(slot_id):
        return halo_grad[slot_id * face_end : (slot_id + 1) * face_end]

    def corner_grad(slot_id):
        first_row = 4 * face_end + slot_id * corner_size
        return halo_grad[first_row : first_row + corner_size]

    back_to_minus_y = jnp.concatenate([face_grad(2), corner_grad(0), corner_grad(2)], 0)
    back_to_plus_y = jnp.concatenate([face_grad(3), corner_grad(1), corner_grad(3)], 0)
    back_minus_y, back_plus_y = move_along_y(back_to_minus_y, back_to_plus_y)
    back_to_minus_x = jnp.concatenate(
        [face_grad(0), back_minus_y[face_end:corner_end], back_plus_y[face_end:corner_end]], 0
    )
    back_to_plus_x = jnp.concatenate(
        [face_grad(1), back_minus_y[corner_end:], back_plus_y[corner_end:]], 0
    )
    back_minus_x, back_plus_x = move_along_x(back_to_minus_x, back_to_plus_x)
    gathered = jnp.concatenate(
        [back_minus_x, back_plus_x, back_minus_y[:face_end], back_plus_y[:face_end]], 0
    )
    listed = jnp.concatenate(
        [
            face_list[0],
            corner_list[0],
            corner_list[1],
            face_list[1],
            corner_list[2],
            corner_list[3],
            face_list[2],
            face_list[3],
        ],
        0,
    )
    block_ids = jnp.arange(block_count, dtype=jnp.int32)
    select = (listed[None, :] == block_ids[:, None]).astype(jnp.bfloat16)
    returned = jnp.einsum("bn,nrc->brc", select, gathered, preferred_element_type=jnp.float32)
    input_grad = (ext_grad[:block_count] + returned).astype(jnp.bfloat16).reshape(-1, channels)
    part_grad = weight_part.astype(jnp.bfloat16)
    plane_count = lax.axis_size("gx") * lax.axis_size("gy")
    replicas = lax.axis_size("rep")
    replica_sum = lax.psum_scatter(part_grad, "rep", scatter_dimension=2, tiled=True).astype(
        jnp.float32
    )
    tile_sum = lax.psum(replica_sum, ("gx", "gy"))
    tile_total = plane_count * replicas
    scale_factor = (tile_total * outs_all.shape[1] * 128) ** (-0.5)
    return (activation.reshape(-1, channels), input_grad, tile_sum * scale_factor)


def solution(mesh):
    in_specs = (
        P(("gx", "gy", "rep"), None),
        P(None, None, "rep"),
        P(("gx", "gy", "rep"), None),
        P(("gx", "gy", "rep"), None, None),
        P(("gx", "gy", "rep"), None, None),
        P(("gx", "gy", "rep"), None, None),
        P(("gx", "gy", "rep"), None, None),
        P(("gx", "gy", "rep"), None, None, None),
    )
    out_specs = (P(("gx", "gy", "rep"), None), P(("gx", "gy", "rep"), None), P(None, None, "rep"))
    return jax.shard_map(body, mesh=mesh, in_specs=in_specs, out_specs=out_specs, check_vma=False)
```

profile of v0, /device:TPU:128, one launch (start us, length us, event | category | flops | bytes accessed | tf_op | source)
XLA Modules:
  0.0 1405.1 jit_solution(10028921954508962687)
XLA Ops:
  18.3 2.5 collective-permute-start
  26.4 4.9 collective-permute-start.2
  31.4 6.6 collective-permute-start.3
  40.0 17.4 %collective-permute-done.2 = bf16[6,128,256]{2,1,0:T(8,128)(2,1)S(1)} collective-permute-done((bf16[6,128,256]{2,1,0:T(8,128)(2,1)S(1)}, bf16[6,128,256]{2,1,0:T(8,128)(2,1)S(1)}, u32[]{:S(2)}, u32[]{:S(2)}) %collective-permute-start.2) | collective-permute-done | bytes 393248 | tf_op jit(solution)/shard_map/ppermute | solution.py:10
  57.4 10.4 collective-permute-done.3
  68.0 14.6 %all-gather.2.cloned.1.call-done = bf16[27,256,256]{2,1,0:T(8,128)(2,1)} async-done(((bf16[27,256,128]{2,1,0:T(8,128)(2,1)}), bf16[27,256,256]{2,1,0:T(8,128)(2,1)}) %all-gather.2.cloned.1.call-update) | async-done | bytes 3538960 | tf_op jit(solution)/shard_map/all_gather | solution.py:115
  82.6 137.3 %while.25 = (s32[]{:T(128)}, f32[8,128,256]{2,0,1:T(8,128)S(1)}, s32[27,4]{1,0:T(8,128)S(1)}, s32[27,4,128]{2,1,0:T(4,128)}, s32[27,4]{1,0:T(8,128)S(1)}, /*inde...) while((s32[]{:T(128)}, f32[8,128,256]{2,0,1:T(8,128)S(1)}, ...), condition=%wide.region_1.4_spmd.clone, body=%wide.region_0.3_spmd.clone.sunk | while | flops 80220200 | bytes 4075739 | solution.py:50
  219.9 2.4 fusion.40
  224.4 335.6 %while.24 = (s32[]{:T(128)}, f32[3713,256]{1,0:T(8,128)}, bf16[27,256,256]{2,1,0:T(8,128)(2,1)}, s32[27,4,128]{2,1,0:T(4,128)}, s32[27,4]{1,0:T(8,128)S(1)}, /*i...) while((s32[]{:T(128)}, f32[3713,256]{1,0:T(8,128)}, ...), condition=%wide.region_4.7_spmd, body=%wide.region_2.6_spmd.sunk | while | flops 134357008 | bytes 4354305 | solution.py:78
  229.9 6.9 scatter_fusion
  242.4 6.9 scatter_fusion
  254.8 6.9 scatter_fusion
  267.2 6.9 scatter_fusion
  279.7 6.9 scatter_fusion
  292.1 6.9 scatter_fusion
  304.5 6.9 scatter_fusion
  316.9 6.9 scatter_fusion
  329.4 6.9 scatter_fusion
  341.8 6.9 scatter_fusion
  354.2 6.9 scatter_fusion
  366.6 6.9 scatter_fusion
  379.1 6.9 scatter_fusion
  391.5 6.9 scatter_fusion
  403.9 6.9 scatter_fusion
  416.4 6.9 scatter_fusion
  428.8 6.9 scatter_fusion
  441.2 6.9 scatter_fusion
  453.6 6.9 scatter_fusion
  466.1 6.9 scatter_fusion
  478.5 6.9 scatter_fusion
  490.9 6.9 scatter_fusion
  503.4 6.9 scatter_fusion
  515.8 6.9 scatter_fusion
  528.2 6.9 scatter_fusion
  540.6 6.9 scatter_fusion
  553.1 6.9 scatter_fusion
  560.0 7.7 copy.132
  567.7 7.6 copy.134
  578.6 5.0 collective-permute-start.4
  584.5 6.8 collective-permute-start.5
  591.7 22.1 %collective-permute-done.4 = bf16[6,128,256]{2,0,1:T(8,128)(2,1)S(1)} collective-permute-done((bf16[6,128,256]{2,0,1:T(8,128)(2,1)S(1)}, bf16[6,128,256]{2,0,1:T(8,128)(2,1)S(1)}, u32[]{:S(2)}, u32[]{:S(2)}) %collective-permute-start.4) | collective-permute-done | bytes 393248 | tf_op jit(solution)/shard_map/ppermute | solution.py:10
  614.0 11.8 collective-permute-done.5
  628.3 3.1 collective-permute-start.6
  631.4 2.5 concatenate.43
  637.7 8.3 reduce-scatter.4.cloned.1.call-done
  646.0 2.8 reshape.420
  648.8 2.9 copy.133
  651.8 744.4 %all-reduce.2 = f32[27,256,128]{2,1,0:T(8,128)S(1)} all-reduce(bf16[27,256,128]{2,1,0:T(8,128)(2,1)} %copy.133), channel_id=1, replica_groups=mesh['gx'=2,'gy'=64,'rep'=2] {'gx','gy'}, use_global_device_ids=true, to_apply=%region_6.9 | all-reduce | flops 884736 | bytes 5308416 | tf_op jit(solution)/shard_map/psum | solution.py:203
  (538 shorter events, 310.3 us)
Async XLA Ops:
  7.2 10.4 copy-start
  7.2 75.4 %all-gather.2.cloned.1.call-start = ((), (), s32[]{:S(2)}) async-start(), calls=%async_computation.1 | async-start | bytes 5308416 | tf_op jit(solution)/shard_map/all_gather | solution.py:115
  7.9 638.1 %reduce-scatter.4.cloned.1.call-start = ((), (), s32[]{:S(2)}) async-start(), calls=%async_computation.2 | async-start | bytes 5308416
  18.3 6.2 collective-permute-start
  20.8 3.4 copy-start.2
  20.8 3.5 copy-start.3
  21.6 3.9 collective-permute-start.1
  26.4 31.0 %collective-permute-start.2 = (bf16[6,128,256]{2,1,0:T(8,128)(2,1)S(1)}, bf16[6,128,256]{2,1,0:T(8,128)(2,1)S(1)}, u32[]{:S(2)}, u32[]{:S(2)}) collective-permute-start(bf16[6,128,256]{2,1,0:T(8,128)(2,1)S(1)} %pad_maximum_fusion.6), channel_id=1, source_target_pairs={{0,2},{2,4},{4,6},{6,8},{8,10},{10,12},{12,14},{14,16},{16,18},{18... | collective-permute-start | bytes 1179656 | tf_op jit(solution)/shard_map/ppermute | solution.py:10
  31.4 36.4 %collective-permute-start.3 = (bf16[6,128,256]{2,1,0:T(8,128)(2,1)S(1)}, bf16[6,128,256]{2,1,0:T(8,128)(2,1)S(1)}, u32[]{:S(2)}, u32[]{:S(2)}) collective-permute-start(bf16[6,128,256]{2,1,0:T(8,128)(2,1)S(1)} %pad_maximum_fusion.7), channel_id=1, source_target_pairs={{2,0},{4,2},{6,4},{8,6},{10,8},{12,10},{14,12},{16,14},{18,16},{20... | collective-permute-start | bytes 1179656 | tf_op jit(solution)/shard_map/ppermute | solution.py:10
  578.6 35.2 %collective-permute-start.4 = (bf16[6,128,256]{2,0,1:T(8,128)(2,1)S(1)}, bf16[6,128,256]{2,0,1:T(8,128)(2,1)S(1)}, u32[]{:S(2)}, u32[]{:S(2)}) collective-permute-start(bf16[6,128,256]{2,0,1:T(8,128)(2,1)S(1)} %pad_maximum_fusion), channel_id=1, source_target_pairs={{0,2},{2,4},{4,6},{6,8},{8,10},{10,12},{12,14},{14,16},{16,18},{18... | collective-permute-start | bytes 1179656 | tf_op jit(solution)/shard_map/ppermute | solution.py:10
  584.5 41.4 %collective-permute-start.5 = (bf16[6,128,256]{2,0,1:T(8,128)(2,1)S(1)}, bf16[6,128,256]{2,0,1:T(8,128)(2,1)S(1)}, u32[]{:S(2)}, u32[]{:S(2)}) collective-permute-start(bf16[6,128,256]{2,0,1:T(8,128)(2,1)S(1)} %pad_maximum_fusion.1), channel_id=1, source_target_pairs={{2,0},{4,2},{6,4},{8,6},{10,8},{12,10},{14,12},{16,14},{18,16},{20... | collective-permute-start | bytes 1179656 | tf_op jit(solution)/shard_map/ppermute | solution.py:10
  591.5 39.9 %copy-start.1 = (s32[1,4,4]{2,1,0:T(4,128)S(1)}, s32[1,4,4]{2,1,0:T(4,128)}, u32[]{:S(2)}) copy-start(s32[1,4,4]{2,1,0:T(4,128)} %param.19) | copy-start | bytes 196
  626.6 8.9 collective-permute-start.7
  628.3 7.1 collective-permute-start.6
Sparse Core Ops, SparseCore 0:
  9.8 72.7 all-gather.1
  575.5 70.4 reduce-scatter.3
where the time goes:
time: 1410 us
  blocking collectives  744 us (53%)
  other arithmetic  239 us (17%)
  local copies, waits for them, and re-layouts  160 us (11%)
  matrix products  120 us (9%)
  waiting for transfers between devices  85.3 us (6%)
  starting transfers between devices  31.5 us (2%)
  between operations  21.8 us (2%)
    psum x1, blocking collectives, body(): tile_sum = lax.psum(replica_sum, ('gx', 'gy'))  744 us
    scatter-add x27, other arithmetic, backward_one_offset(): grad_rows = grad_rows.at[source.reshape(-1)].add(back_rows)  187 us
    gather x54, local copies, waits for them, and re-layouts, gather_rows(): return (flat_rows[source], source)  105 us
    ppermute x8, waiting for transfers between devices, from_behind(): lax.ppermute(value, axis, [(source, source + steps) for source in range(i...  61.7 us
    select_n x54, other arithmetic, gather_rows(): return (flat_rows[source], source)  40.8 us
    dot_general x27, matrix products, forward_one_offset(): jnp.einsum('bp,prc->brc', select, product, precision=lax.Precision.HIGHEST)  32 us
    ppermute x8, starting transfers between devices, from_behind(): lax.ppermute(value, axis, [(source, source + steps) for source in range(i...  31.5 us
    dot_general x27, matrix products, backward_one_offset(): lax.dot_general(flat_up, weight_k, (((1,), (1,)), ((), ())), preferred_el...  31.4 us
  transfers between devices with their start and end apart: 10, of which 6 were waited for; matrix products, arithmetic and copies ran while one was open for 2% of the time, Pallas kernels for 0%

commit v1 on v0

v1 whole, which is shorter than its diff:
```python
import functools

import jax
import jax.numpy as jnp
from jax import lax
from jax.experimental import pallas as pl
from jax.experimental.pallas import tpu as pltpu
from jax.sharding import PartitionSpec as P

ALL = ("gx", "gy", "rep")
K, C, NB, ROWS, PAIRS = 27, 256, 8, 128, 4
EXT = 29
KPAD = 32
BF, F32 = jnp.bfloat16, jnp.float32
VM = pl.BlockSpec(memory_space=pltpu.VMEM)
SM = pl.BlockSpec(memory_space=pltpu.SMEM)
PARAMS = pltpu.CompilerParams(vmem_limit_bytes=58 * 1024 * 1024)


def shape_of(*dims, dtype=BF):
    return jax.ShapeDtypeStruct(dims, dtype)


def call(kernel, ins, outs, scratch=(), cost=None):
    specs = [SM if kind == "s" else VM for kind, _ in ins]
    return pl.pallas_call(
        kernel,
        out_shape=outs,
        in_specs=specs,
        out_specs=[VM] * len(outs),
        scratch_shapes=list(scratch),
        compiler_params=PARAMS,
        cost_estimate=cost,
    )(*[value for _, value in ins])


def flat_id(core, x, y, z):
    return (core * 64 + ((z % 8) * 4 + y % 4) * 2 + (x % 4) // 2) * 2 + x % 2


def torus_perm(move):
    pairs = []
    for core in range(2):
        for z in range(8):
            for y in range(4):
                for x in range(4):
                    pairs.append((flat_id(core, x, y, z), flat_id(*move(core, x, y, z))))
    return pairs


def shift(value, **by):
    def move(core, x, y, z):
        return (
            (core + by.get("core", 0)) % 2,
            x + by.get("x", 0),
            y + by.get("y", 0),
            z + by.get("z", 0),
        )

    return lax.ppermute(value, ALL, torus_perm(move))


def grid_shift(value, step_x, step_y):
    pairs = []
    for i in range(2):
        for j in range(64):
            if 0 <= j + step_y < 64:
                for r in range(2):
                    to = ((i + step_x) % 2 * 64 + j + step_y) * 2 + r
                    pairs.append(((i * 64 + j) * 2 + r, to))
    return lax.ppermute(value, ALL, pairs)


def pick_kernel(core_ref, face_ref, corner_ref, feats, face_x, low_y, high_y, low_c, high_c):
    i = core_ref[0]
    for n in range(4):
        face_x[n] = feats[face_ref[(1 - i) * 4 + n]]
        low_y[n] = feats[face_ref[8 + n]]
        high_y[n] = feats[face_ref[12 + n]]
    low_c[...] = feats[corner_ref[2 * (1 - i)]]
    high_c[...] = feats[corner_ref[2 * (1 - i) + 1]]


def join_weight(core, rep, own, far, far_other, full):
    near_rows = pl.ds(pl.multiple_of(core * 128, 128), 128)
    other_rows = pl.ds(pl.multiple_of((1 - core) * 128, 128), 128)
    for side in range(2):

        @pl.when(rep == side)
        def _():
            mine = slice(side * 128, side * 128 + 128)
            theirs = slice(128 - side * 128, 256 - side * 128)

            def step(k, carry):
                full[k, :, mine] = own[k]
                full[k, near_rows, theirs] = far[k]
                full[k, other_rows, theirs] = far_other[k]
                return carry

            lax.fori_loop(0, K, step, 0)


def forward_kernel(
    meta, outs, ins, maps, feats, face_x, from_low, from_high, low_c, high_c,
    own, far, far_other, cotan,
    act, grad, keep, send,
    ext, full, rows, acc, flipped,
):
    core, rep = meta[0], meta[1]
    zeros = jnp.zeros((4, ROWS, C), BF)
    ext[0:8] = feats[...]
    ext[pl.ds(8 + 4 * (1 - core), 4)] = face_x[...]
    ext[pl.ds(8 + 4 * core, 4)] = zeros
    ext[16:20] = from_low[...]
    ext[20:24] = from_high[...]
    ext[24 + 2 * (1 - core)] = low_c[...]
    ext[25 + 2 * (1 - core)] = high_c[...]
    ext[pl.ds(24 + 2 * core, 2)] = zeros[:2]
    ext[28] = zeros[0]
    join_weight(core, rep, own, far, far_other, full)
    acc[...] = jnp.zeros_like(acc)
    places = lax.broadcasted_iota(jnp.int32, (ROWS, ROWS), 0)

    def gather_step(k, carry):
        map_k = maps[k]
        for p in range(PAIRS):
            hot = (places == map_k[p : p + 1, :]).astype(F32).astype(BF)
            picked = lax.dot_general(
                hot, ext[ins[k * PAIRS + p]], (((0,), (0,)), ((), ())), preferred_element_type=F32
            )
            rows[k, p * ROWS : (p + 1) * ROWS, :] = picked.astype(BF)
        product = jnp.dot(rows[k], full[k], preferred_element_type=F32)
        for p in range(PAIRS):
            acc[outs[k * PAIRS + p]] += product[p * ROWS : (p + 1) * ROWS]
        return carry

    lax.fori_loop(0, K, gather_step, 0)

    def grad_step(b, carry):
        value = acc[b]
        sigma = 1.0 / (1.0 + jnp.exp(-value))
        act[b] = (value * sigma).astype(BF)
        up = cotan[b].astype(F32) * (sigma * (1.0 + value * (1.0 - sigma)))
        grad[b] = up.astype(BF)
        flipped[b] = up.T.astype(BF)
        return carry

    lax.fori_loop(0, NB, grad_step, 0)

    def weight_step(k, carry):
        left = jnp.concatenate([flipped[outs[k * PAIRS + p]] for p in range(PAIRS)], axis=1)
        part = jnp.dot(left, rows[k], preferred_element_type=F32)
        for side in range(2):
            first = part[side * 128 : side * 128 + 64]
            second = part[side * 128 + 64 : side * 128 + 128]
            kept = jnp.where(core == 0, first, second).astype(BF)
            sent = jnp.where(core == 0, second, first).astype(BF)
            for y in range(4):
                keep[y, side, k] = kept[y * 16 : y * 16 + 16]
                send[y, side, k] = sent[y * 16 : y * 16 + 16]
        return carry

    lax.fori_loop(0, K, weight_step, 0)


def backward_kernel(
    meta, outs, ins, maps, grad, own, far, far_other,
    local, face_x, to_low, to_high, low_c, high_c,
    full, stack, acc,
):
    core, rep = meta[0], meta[1]
    join_weight(core, rep, own, far, far_other, full)
    acc[...] = jnp.zeros_like(acc)
    places = lax.broadcasted_iota(jnp.int32, (ROWS, ROWS), 0)

    def step(k, carry):
        map_k = maps[k]
        for p in range(PAIRS):
            hot = (places == map_k[p : p + 1, :]).astype(F32).astype(BF)
            spread = jnp.dot(hot, grad[outs[k * PAIRS + p]], preferred_element_type=F32)
            stack[p * ROWS : (p + 1) * ROWS, :] = spread.astype(BF)
        product = lax.dot_general(
            stack[...], full[k], (((1,), (1,)), ((), ())), preferred_element_type=F32
        )
        for p in range(PAIRS):
            acc[ins[k * PAIRS + p]] += product[p * ROWS : (p + 1) * ROWS]
        return carry

    lax.fori_loop(0, K, step, 0)
    local[...] = acc[0:8]
    face_x[...] = acc[pl.ds(8 + 4 * (1 - core), 4)].astype(BF)
    to_low[...] = acc[16:20].astype(BF)
    to_high[...] = acc[20:24].astype(BF)
    low_c[...] = acc[24 + 2 * (1 - core)].astype(BF)
    high_c[...] = acc[25 + 2 * (1 - core)].astype(BF)


def input_kernel(
    core_ref, face_ref, corner_ref, local, face_x, from_low, from_high, low_c, high_c, out, acc
):
    i = core_ref[0]
    acc[...] = local[...]
    for n in range(4):
        acc[face_ref[(1 - i) * 4 + n]] += face_x[n].astype(F32)
        acc[face_ref[8 + n]] += from_low[n].astype(F32)
        acc[face_ref[12 + n]] += from_high[n].astype(F32)
    acc[corner_ref[2 * (1 - i)]] += low_c[...].astype(F32)
    acc[corner_ref[2 * (1 - i) + 1]] += high_c[...].astype(F32)
    out[...] = acc[...].astype(BF)


def final_kernel(scale, meta, mine, other, out):
    core, half, y_at, z_at = meta[0], meta[2], meta[3], meta[4]

    def step(k, carry):
        z = (z_at - k // 4) & 7
        for side in range(2):
            source = (mine, other)[side]
            halves = []
            for x in range(2):
                pieces = [
                    source[(y_at - y) & 3, (half - x) & 1, z, k % 4].astype(F32) for y in range(4)
                ]
                halves.append(jnp.concatenate(pieces, 0))
            block = jnp.concatenate(halves, 1) * scale
            turned = block.T
            for first in range(2):

                @pl.when(core == first)
                def _():
                    at = 64 * (first ^ side)
                    out[k, :, at : at + 64] = turned

        return carry

    lax.fori_loop(0, K, step, 0)


def spread_ring(take, me, count, axis):
    total = take(me)
    arrived = [
        shift(take((me + s) % count).astype(BF), **{axis: s}) for s in range(1, count)
    ]
    for piece in arrived:
        total = total + piece.astype(F32)
    return total


def collect_ring(value, count, axis, stride=1):
    return jnp.stack(
        [value] + [shift(value, **{axis: s * stride}) for s in range(1, count)], 0
    )


def body(feats, weight, cotan, face_send, corner_send, pair_out, pair_in, row_map):
    core = lax.axis_index("gx")
    gy = lax.axis_index("gy")
    rep = lax.axis_index("rep")
    half, y_at, z_at = gy % 2, gy // 2 % 4, gy // 8
    x_at = half * 2 + rep
    meta = jnp.stack([core, rep, half, y_at, z_at]).astype(jnp.int32)
    blocks = feats.reshape(NB, ROWS, C)
    face = face_send.reshape(16)
    corner = corner_send.reshape(4)
    outs, ins = pair_out.reshape(-1), pair_in.reshape(-1)
    maps = row_map[0]
    four, one = shape_of(4, ROWS, C), shape_of(ROWS, C)

    face_x, low_y, high_y, low_c, high_c = call(
        pick_kernel,
        [("s", meta), ("s", face), ("s", corner), ("v", blocks)],
        [four, four, four, one, one],
    )
    from_high = grid_shift(low_y, 0, -1)
    from_low = grid_shift(high_y, 0, 1)
    from_high_c = grid_shift(low_c, 1, -1)
    from_low_c = grid_shift(high_c, 1, 1)
    from_x = grid_shift(face_x, 1, 0)
    wanted = lax.dynamic_slice_in_dim(weight, core * 128, 128, 1)
    far = lax.ppermute(
        wanted, ALL, torus_perm(lambda c, x, y, z: (c, x + (1 if c == 0 else -1), y, z))
    )
    far_other = shift(far, core=1)

    act, grad, keep, send = call(
        forward_kernel,
        [("s", meta), ("s", outs), ("s", ins), ("v", maps), ("v", blocks), ("v", from_x)]
        + [("v", v) for v in (from_low, from_high, from_low_c, from_high_c)]
        + [("v", v) for v in (weight, far, far_other, cotan.reshape(NB, ROWS, C))],
        [
            shape_of(NB, ROWS, C),
            shape_of(NB, ROWS, C),
            shape_of(4, 2, K, 16, C),
            shape_of(4, 2, K, 16, C),
        ],
        [
            pltpu.VMEM((EXT, ROWS, C), BF),
            pltpu.VMEM((K, C, C), BF),
            pltpu.VMEM((K, PAIRS * ROWS, C), BF),
            pltpu.VMEM((NB, ROWS, C), F32),
            pltpu.VMEM((NB, C, ROWS), BF),
        ],
        pl.CostEstimate(flops=7_000_000_000, bytes_accessed=12_000_000, transcendentals=0),
    )
    got = shift(send, core=1)
    local, back_x, to_low, to_high, back_low_c, back_high_c = call(
        backward_kernel,
        [("s", meta), ("s", outs), ("s", ins), ("v", maps), ("v", grad)]
        + [("v", v) for v in (weight, far, far_other)],
        [shape_of(NB, ROWS, C, dtype=F32), four, four, four, one, one],
        [
            pltpu.VMEM((K, C, C), BF),
            pltpu.VMEM((PAIRS * ROWS, C), BF),
            pltpu.VMEM((EXT, ROWS, C), F32),
        ],
        pl.CostEstimate(flops=5_000_000_000, bytes_accessed=10_000_000, transcendentals=0),
    )
    return_high = grid_shift(to_low, 0, -1)
    return_low = grid_shift(to_high, 0, 1)
    return_high_c = grid_shift(back_low_c, 1, -1)
    return_low_c = grid_shift(back_high_c, 1, 1)
    return_x = grid_shift(back_x, 1, 0)

    def take_y(n):
        return lax.dynamic_index_in_dim(keep, n, 0, False).astype(
            F32
        ) + lax.dynamic_index_in_dim(got, n, 0, False).astype(F32)

    sum_y = spread_ring(take_y, y_at, 4, "y")

    def take_x(n):
        return lax.dynamic_slice(sum_y, (n % 2, 0, 0, n // 2 * 128), (1, K, 16, 128))[0]

    sum_x = spread_ring(take_x, x_at, 4, "x")
    padded = jnp.concatenate([sum_x, jnp.zeros((KPAD - K, 16, 128), F32)], 0)

    def take_z(n):
        return lax.dynamic_slice_in_dim(padded, n * 4, 4, 0)

    sum_z = spread_ring(take_z, z_at, 8, "z")
    all_z = collect_ring(sum_z.astype(BF), 8, "z")
    all_x = collect_ring(all_z, 2, "x", 2)
    mine = collect_ring(all_x, 4, "y")
    other = shift(mine, core=1)

    input_grad = call(
        input_kernel,
        [("s", meta), ("s", face), ("s", corner), ("v", local), ("v", return_x)]
        + [("v", v) for v in (return_low, return_high, return_low_c, return_high_c)],
        [shape_of(NB, ROWS, C)],
        [pltpu.VMEM((NB, ROWS, C), F32)],
    )[0]
    tiles = lax.axis_size("gx") * lax.axis_size("gy") * lax.axis_size("rep")
    scale = float((tiles * PAIRS * ROWS) ** (-0.5))
    weight_grad = call(
        functools.partial(final_kernel, scale),
        [("s", meta), ("v", mine), ("v", other)],
        [shape_of(K, C, 128, dtype=F32)],
    )[0]
    return act.reshape(-1, C), input_grad.reshape(-1, C), weight_grad


def solution(mesh):
    tiles = ("gx", "gy", "rep")
    in_specs = (
        P(tiles, None),
        P(None, None, "rep"),
        P(tiles, None),
        P(tiles, None, None),
        P(tiles, None, None),
        P(tiles, None, None),
        P(tiles, None, None),
        P(tiles, None, None, None),
    )
    out_specs = (P(tiles, None), P(tiles, None), P(None, None, "rep"))
    return jax.shard_map(body, mesh=mesh, in_specs=in_specs, out_specs=out_specs, check_vma=False)
```

time: 1410 us -> 234 us (0.17)
  the two profiles are of different devices: /device:TPU:128 before, /device:TPU:1 now
where the time goes in v1:
time: 234 us; the launch traced here: 232 us
  waiting for transfers between devices  90 us (38%)
  starting transfers between devices  74.9 us (32%)
  Pallas kernels  55.4 us (24%)
  local copies, waits for them, and re-layouts  7.16 us (3%)
  other arithmetic  3.45 us (1%)
    pallas_call x5, Pallas kernels, call(): pl.pallas_call(kernel, out_shape=outs, in_specs=specs, out_specs=[VM] * l...  55.4 us
    ppermute x27, waiting for transfers between devices, shift(): return lax.ppermute(value, ALL, torus_perm(move))  52.9 us
    ppermute x27, starting transfers between devices, shift(): return lax.ppermute(value, ALL, torus_perm(move))  49.4 us
    ppermute x10, waiting for transfers between devices, grid_shift(): return lax.ppermute(value, ALL, pairs)  27.1 us
    ppermute x10, starting transfers between devices, grid_shift(): return lax.ppermute(value, ALL, pairs)  22.1 us
    ppermute x1, waiting for transfers between devices, body(): lax.ppermute(wanted, ALL, torus_perm(lambda c, x, y, z: (c, x + (1 if c =...  9.99 us
  transfers between devices with their start and end apart: 38, of which 19 were waited for; matrix products, arithmetic and copies ran while one was open for 1% of the time, Pallas kernels for 8%

profile of v1, /device:TPU:1, one launch (start us, length us, event | category | flops | bytes accessed | tf_op | source)
XLA Modules:
  0.0 231.9 jit_solution(16646693121480051580)
XLA Ops:
  0.7 1.2 constant_dynamic-slice_fusion
  1.9 3.4 %collective-permute-start.5 = (bf16[27,128,128]{2,1,0:T(8,128)(2,1)S(1)}, bf16[27,128,128]{2,1,0:T(8,128)(2,1)S(1)}, u32[]{:S(2)}, u32[]{:S(2)}) collective-permute-start(bf16[27,128,128]{2,1,0:T(8,128)(2,1)S(1)} %constant_dynamic-slice_fusion), channel_id=1, source_target_pairs={{0,1},{1,2},{2,3},{3,0},{4,5},{5,6},{6,7},{7,4},{8,9},{9,10},{10,1... | collective-permute-start | bytes 2654216 | tf_op jit(solution)/shard_map/ppermute | solution.py:280
  5.3 10.0 %collective-permute-done.5.far = bf16[27,128,128]{2,1,0:T(8,128)(2,1)S(1)} collective-permute-done((bf16[27,128,128]{2,1,0:T(8,128)(2,1)S(1)}, bf16[27,128,128]{2,1,0:T(8,128)(2,1)S(1)}, u32[]{:S(2)}, u32[]{:S(2)}) %collective-permute-start.5) | collective-permute-done | bytes 884768 | tf_op jit(solution)/shard_map/ppermute | solution.py:280
  15.3 4.2 %collective-permute-start.6 = (bf16[27,128,128]{2,1,0:T(8,128)(2,1)S(1)}, bf16[27,128,128]{2,1,0:T(8,128)(2,1)S(1)}, u32[]{:S(2)}, u32[]{:S(2)}) collective-permute-start(bf16[27,128,128]{2,1,0:T(8,128)(2,1)S(1)} %collective-permute-done.5.far), channel_id=1, source_target_pairs={{0,128},{1,129},{2,130},{3,131},{4,132},{5,133},{6,134},{7,135},{8... | collective-permute-start | bytes 2654216 | tf_op jit(solution)/shard_map/ppermute | solution.py:60
  20.7 2.0 shard_map.103
  22.8 1.7 collective-permute-start.1
  24.5 1.3 collective-permute-start.2
  25.8 6.3 %collective-permute-start.3 = (bf16[128,256]{1,0:T(8,128)(2,1)}, bf16[128,256]{1,0:T(8,128)(2,1)S(1)}, u32[]{:S(2)}, u32[]{:S(2)}) collective-permute-start(bf16[128,256]{1,0:T(8,128)(2,1)} %get-tuple-element.21), channel_id=1, source_target_pairs={{0,130},{1,131},{2,132},{3,133},{4,134},{5,135},{6,136},{7,137},{8... | collective-permute-start | bytes 196616 | tf_op jit(solution)/shard_map/ppermute | solution.py:71
  32.2 7.5 %collective-permute-done.3.low_c = bf16[128,256]{1,0:T(8,128)(2,1)S(1)} collective-permute-done((bf16[128,256]{1,0:T(8,128)(2,1)}, bf16[128,256]{1,0:T(8,128)(2,1)S(1)}, u32[]{:S(2)}, u32[]{:S(2)}) %collective-permute-start.3) | collective-permute-done | bytes 65568 | tf_op jit(solution)/shard_map/ppermute | solution.py:71
  39.7 1.3 collective-permute-start.4
  42.5 5.1 %collective-permute-done.4.high_c = bf16[128,256]{1,0:T(8,128)(2,1)S(1)} collective-permute-done((bf16[128,256]{1,0:T(8,128)(2,1)}, bf16[128,256]{1,0:T(8,128)(2,1)S(1)}, u32[]{:S(2)}, u32[]{:S(2)}) %collective-permute-start.4) | collective-permute-done | bytes 65568 | tf_op jit(solution)/shard_map/ppermute | solution.py:71
  48.8 24.1 %shard_map.104 = (bf16[8,128,256]{2,1,0:T(8,128)(2,1)}, bf16[8,128,256]{2,1,0:T(8,128)(2,1)}, bf16[4,2,27,16,256]{4,3,2,1,0:T(8,128)(2,1)}, bf16[4,2,27,16,256]{4,3,2,1,0:T(8,128)(2,1)}) custom-call(s32[5]{0:T(128)} %stack.74.core_ref.meta, s32[108]{0:T(128)} %reshape.48.outs, s32[108]{0:T(128)} %reshape.49.ins, s32[27,4,128]{2,1,0:T(4,128)} %bitcast.69, ...), custom_call_target="tpu_custom_call" | custom-call | flops 7000000000 | bytes 12000000 | tf_op jit(solution)/shard_map/pallas_call | solution.py:26
  73.0 3.8 %collective-permute-done.12 = bf16[4,2,27,16,256]{4,3,2,1,0:T(8,128)(2,1)S(1)} collective-permute-done((bf16[4,2,27,16,256]{4,3,2,1,0:T(8,128)(2,1)}, bf16[4,2,27,16,256]{4,3,2,1,0:T(8,128)(2,1)S(1)}, u32[]{:S(2)}, u32[]{:S(2)}) %collective-permute-start.12) | collective-permute-done | bytes 1769504 | tf_op jit(solution)/shard_map/ppermute | solution.py:60
  76.8 1.7 fusion.2
  78.5 3.1 %collective-permute-start.15 = (bf16[2,27,16,256]{3,2,1,0:T(8,128)(2,1)S(1)}, bf16[2,27,16,256]{3,2,1,0:T(8,128)(2,1)S(1)}, u32[]{:S(2)}, u32[]{:S(2)}) collective-permute-start(bf16[2,27,16,256]{3,2,1,0:T(8,128)(2,1)S(1)} %get-tuple-element.36), channel_id=1, source_target_pairs={{0,12},{1,13},{2,14},{3,15},{4,0},{5,1},{6,2},{7,3},{8,4},{9,5},{1... | collective-permute-start | bytes 1327112 | tf_op jit(solution)/shard_map/ppermute | solution.py:60
  82.6 17.7 %collective-permute-done.15 = bf16[2,27,16,256]{3,2,1,0:T(8,128)(2,1)S(1)} collective-permute-done((bf16[2,27,16,256]{3,2,1,0:T(8,128)(2,1)S(1)}, bf16[2,27,16,256]{3,2,1,0:T(8,128)(2,1)S(1)}, u32[]{:S(2)}, u32[]{:S(2)}) %collective-permute-start.15) | collective-permute-done | bytes 442400 | tf_op jit(solution)/shard_map/ppermute | solution.py:60
  100.3 4.4 %collective-permute-done.13 = bf16[2,27,16,256]{3,2,1,0:T(8,128)(2,1)} collective-permute-done((bf16[2,27,16,256]{3,2,1,0:T(8,128)(2,1)S(1)}, bf16[2,27,16,256]{3,2,1,0:T(8,128)(2,1)}, u32[]{:S(2)}, u32[]{:S(2)}) %collective-permute-start.13) | collective-permute-done | bytes 442400 | tf_op jit(solution)/shard_map/ppermute | solution.py:60
  104.7 1.5 fusion.1
  106.4 3.2 %collective-permute-start.18 = (bf16[27,16,128]{2,1,0:T(8,128)(2,1)S(1)}, bf16[27,16,128]{2,1,0:T(8,128)(2,1)S(1)}, u32[]{:S(2)}, u32[]{:S(2)}) collective-permute-start(bf16[27,16,128]{2,1,0:T(8,128)(2,1)S(1)} %get-tuple-element.39), channel_id=1, source_target_pairs={{0,3},{1,0},{2,1},{3,2},{4,7},{5,4},{6,5},{7,6},{8,11},{9,8},{10,9... | collective-permute-start | bytes 331784 | tf_op jit(solution)/shard_map/ppermute | solution.py:60
  110.7 1.8 collective-permute-done.18
  112.5 2.3 collective-permute-done.17
  114.8 3.3 %collective-permute-done.16 = bf16[27,16,128]{2,1,0:T(8,128)(2,1)S(1)} collective-permute-done((bf16[27,16,128]{2,1,0:T(8,128)(2,1)S(1)}, bf16[27,16,128]{2,1,0:T(8,128)(2,1)S(1)}, u32[]{:S(2)}, u32[]{:S(2)}) %collective-permute-start.16) | collective-permute-done | bytes 110624 | tf_op jit(solution)/shard_map/ppermute | solution.py:60
  118.2 2.5 %collective-permute-start.25 = (bf16[4,16,128]{2,1,0:T(8,128)(2,1)S(1)}, bf16[4,16,128]{2,1,0:T(8,128)(2,1)S(1)}, u32[]{:S(2)}, u32[]{:S(2)}) collective-permute-start(bf16[4,16,128]{2,1,0:T(8,128)(2,1)S(1)} %get-tuple-element.49), channel_id=1, source_target_pairs={{0,112},{1,113},{2,114},{3,115},{4,116},{5,117},{6,118},{7,119},{8... | collective-permute-start | bytes 49160 | tf_op jit(solution)/shard_map/ppermute | solution.py:60
  120.7 4.1 %collective-permute-start.24 = (bf16[4,16,128]{2,1,0:T(8,128)(2,1)S(1)}, bf16[4,16,128]{2,1,0:T(8,128)(2,1)S(1)}, u32[]{:S(2)}, u32[]{:S(2)}) collective-permute-start(bf16[4,16,128]{2,1,0:T(8,128)(2,1)S(1)} %get-tuple-element.48), channel_id=1, source_target_pairs={{0,96},{1,97},{2,98},{3,99},{4,100},{5,101},{6,102},{7,103},{8,104... | collective-permute-start | bytes 49160 | tf_op jit(solution)/shard_map/ppermute | solution.py:60
  124.7 2.2 collective-permute-start.23
  126.9 2.7 %collective-permute-start.22 = (bf16[4,16,128]{2,1,0:T(8,128)(2,1)S(1)}, bf16[4,16,128]{2,1,0:T(8,128)(2,1)S(1)}, u32[]{:S(2)}, u32[]{:S(2)}) collective-permute-start(bf16[4,16,128]{2,1,0:T(8,128)(2,1)S(1)} %get-tuple-element.46), channel_id=1, source_target_pairs={{0,64},{1,65},{2,66},{3,67},{4,68},{5,69},{6,70},{7,71},{8,72},{9,... | collective-permute-start | bytes 49160 | tf_op jit(solution)/shard_map/ppermute | solution.py:60
  130.1 3.6 %collective-permute-start.20 = (bf16[4,16,128]{2,1,0:T(8,128)(2,1)S(1)}, bf16[4,16,128]{2,1,0:T(8,128)(2,1)S(1)}, u32[]{:S(2)}, u32[]{:S(2)}) collective-permute-start(bf16[4,16,128]{2,1,0:T(8,128)(2,1)S(1)} %get-tuple-element.44), channel_id=1, source_target_pairs={{0,32},{1,33},{2,34},{3,35},{4,36},{5,37},{6,38},{7,39},{8,40},{9,... | collective-permute-start | bytes 49160 | tf_op jit(solution)/shard_map/ppermute | solution.py:60
  133.7 1.9 collective-permute-done.21
  135.5 2.4 %collective-permute-done.19 = bf16[4,16,128]{2,1,0:T(8,128)(2,1)S(1)} collective-permute-done((bf16[4,16,128]{2,1,0:T(8,128)(2,1)S(1)}, bf16[4,16,128]{2,1,0:T(8,128)(2,1)S(1)}, u32[]{:S(2)}, u32[]{:S(2)}) %collective-permute-start.19) | collective-permute-done | bytes 16416 | tf_op jit(solution)/shard_map/ppermute | solution.py:60
  138.3 2.0 collective-permute-start.28
  140.3 3.4 %collective-permute-start.29 = (bf16[4,16,128]{2,1,0:T(8,128)(2,1)S(1)}, bf16[4,16,128]{2,1,0:T(8,128)(2,1)S(1)}, u32[]{:S(2)}, u32[]{:S(2)}) collective-permute-start(bf16[4,16,128]{2,1,0:T(8,128)(2,1)S(1)} %get-tuple-element.34), channel_id=1, source_target_pairs={{0,64},{1,65},{2,66},{3,67},{4,68},{5,69},{6,70},{7,71},{8,72},{9,... | collective-permute-start | bytes 49160 | tf_op jit(solution)/shard_map/ppermute | solution.py:60
  143.7 1.7 collective-permute-start.30
  145.5 2.8 %collective-permute-start.31 = (bf16[4,16,128]{2,1,0:T(8,128)(2,1)S(1)}, bf16[4,16,128]{2,1,0:T(8,128)(2,1)S(1)}, u32[]{:S(2)}, u32[]{:S(2)}) collective-permute-start(bf16[4,16,128]{2,1,0:T(8,128)(2,1)S(1)} %get-tuple-element.34), channel_id=1, source_target_pairs={{0,96},{1,97},{2,98},{3,99},{4,100},{5,101},{6,102},{7,103},{8,104... | collective-permute-start | bytes 49160 | tf_op jit(solution)/shard_map/ppermute | solution.py:60
  149.7 1.5 collective-permute-done.32
  151.4 5.1 %collective-permute-done.33 = bf16[8,4,16,128]{3,2,1,0:T(8,128)(2,1)S(1)} collective-permute-done((bf16[8,4,16,128]{3,2,1,0:T(8,128)(2,1)S(1)}, bf16[8,4,16,128]{3,2,1,0:T(8,128)(2,1)S(1)}, u32[]{:S(2)}, u32[]{:S(2)}) %collective-permute-start.33) | collective-permute-done | bytes 131104 | tf_op jit(solution)/shard_map/ppermute | solution.py:60
  158.4 3.7 %collective-permute-done.36 = bf16[2,8,4,16,128]{4,3,2,1,0:T(8,128)(2,1)S(1)} collective-permute-done((bf16[2,8,4,16,128]{4,3,2,1,0:T(8,128)(2,1)S(1)}, bf16[2,8,4,16,128]{4,3,2,1,0:T(8,128)(2,1)S(1)}, u32[]{:S(2)}, u32[]{:S(2)}) %collective-permute-start.36) | collective-permute-done | bytes 262176 | tf_op jit(solution)/shard_map/ppermute | solution.py:60
  162.1 1.4 collective-permute-done.35
  163.6 2.7 %collective-permute-done.34 = bf16[2,8,4,16,128]{4,3,2,1,0:T(8,128)(2,1)S(1)} collective-permute-done((bf16[2,8,4,16,128]{4,3,2,1,0:T(8,128)(2,1)S(1)}, bf16[2,8,4,16,128]{4,3,2,1,0:T(8,128)(2,1)S(1)}, u32[]{:S(2)}, u32[]{:S(2)}) %collective-permute-start.34) | collective-permute-done | bytes 262176 | tf_op jit(solution)/shard_map/ppermute | solution.py:60
  166.4 8.5 %collective-permute-start.37 = (bf16[4,2,8,4,16,128]{5,4,3,2,1,0:T(8,128)(2,1)S(1)}, bf16[4,2,8,4,16,128]{5,4,3,2,1,0:T(8,128)(2,1)S(1)}, u32[]{:S(2)}, u32[]{:S(2)}) collective-permute-start(bf16[4,2,8,4,16,128]{5,4,3,2,1,0:T(8,128)(2,1)S(1)} %pad_maximum_fusion.mine), channel_id=1, source_target_pairs={{0,128},{1,129},{2,130},{3,131},{4,132},{5,133},{6,134},{7,135},{8... | collective-permute-start | bytes 3145736 | tf_op jit(solution)/shard_map/ppermute | solution.py:60
  174.9 14.6 %shard_map.105 = (f32[8,128,256]{2,1,0:T(8,128)}, bf16[4,128,256]{2,1,0:T(8,128)(2,1)}, bf16[4,128,256]{2,1,0:T(8,128)(2,1)}, bf16[4,128,256]{2,1,0:T(8,128)(2,1...) custom-call(s32[5]{0:T(128)} %stack.74.core_ref.meta, s32[108]{0:T(128)} %reshape.48.outs, s32[108]{0:T(128)} %reshape.49.ins, ...), custom_call_target="tpu_custom_call" | custom-call | flops 5000000000 | bytes 10000000 | tf_op jit(solution)/shard_map/pallas_call | solution.py:26
  189.9 2.3 collective-permute-start.8
  192.2 1.3 collective-permute-start.9
  193.5 6.2 %collective-permute-start.10 = (bf16[128,256]{1,0:T(8,128)(2,1)}, bf16[128,256]{1,0:T(8,128)(2,1)S(1)}, u32[]{:S(2)}, u32[]{:S(2)}) collective-permute-start(bf16[128,256]{1,0:T(8,128)(2,1)} %get-tuple-element.29), channel_id=1, source_target_pairs={{0,130},{1,131},{2,132},{3,133},{4,134},{5,135},{6,136},{7,137},{8... | collective-permute-start | bytes 196616 | tf_op jit(solution)/shard_map/ppermute | solution.py:71
  199.6 7.8 %collective-permute-done.10.low_c = bf16[128,256]{1,0:T(8,128)(2,1)S(1)} collective-permute-done((bf16[128,256]{1,0:T(8,128)(2,1)}, bf16[128,256]{1,0:T(8,128)(2,1)S(1)}, u32[]{:S(2)}, u32[]{:S(2)}) %collective-permute-start.10) | collective-permute-done | bytes 65568 | tf_op jit(solution)/shard_map/ppermute | solution.py:71
  207.4 1.3 collective-permute-start.11
  208.7 6.6 %collective-permute-done.11.high_c = bf16[128,256]{1,0:T(8,128)(2,1)S(1)} collective-permute-done((bf16[128,256]{1,0:T(8,128)(2,1)}, bf16[128,256]{1,0:T(8,128)(2,1)S(1)}, u32[]{:S(2)}, u32[]{:S(2)}) %collective-permute-start.11) | collective-permute-done | bytes 65568 | tf_op jit(solution)/shard_map/ppermute | solution.py:71
  216.3 2.5 %shard_map.106 = bf16[8,128,256]{2,1,0:T(8,128)(2,1)} custom-call(s32[5]{0:T(128)} %stack.74.core_ref.meta, s32[16]{0:T(128)} %reshape.51.face_ref, s32[4]{0:T(128)} %bitcast.67, f32[8,128,256]{2,1,0:T(8,128)} %get-tuple-element.25.local, bf16[4,128,256]{2,1,0:T(8,128)(2,1)} %copy-done.2, bf16[4,128,256]{2,1,0:T(8,128)(2,1)} %copy-done.3, ...), custom_call_target="tpu_custom_call" | custom-call | tf_op jit(solution)/shard_map/pallas_call | solution.py:26
  219.8 12.2 %shard_map.107 = f32[27,256,128]{2,1,0:T(8,128)} custom-call(s32[5]{0:T(128)} %stack.74.core_ref.meta, bf16[4,2,8,4,16,128]{5,4,3,2,1,0:T(8,128)(2,1)} %copy-done, bf16[4,2,8,4,16,128]{5,4,3,2,1,0:T(8,128)(2,1)} %copy-done.1), custom_call_target="tpu_custom_call" | custom-call | tf_op jit(solution)/shard_map/pallas_call | solution.py:26
  (89 shorter events, 13.0 us)
Async XLA Ops:
  0.6 18.9 %copy-start.9 = (s32[1,4,4]{2,1,0:T(4,128)S(1)}, s32[1,4,4]{2,1,0:T(4,128)}, u32[]{:S(2)}) copy-start(s32[1,4,4]{2,1,0:T(4,128)} %param.11) | copy-start | bytes 196
  0.6 40.4 %copy-start.7 = (s32[1,27,4]{1,2,0:T(4,128)S(1)}, s32[1,27,4]{1,2,0:T(4,128)}, u32[]{:S(2)}) copy-start(s32[1,27,4]{1,2,0:T(4,128)} %param.13) | copy-start | bytes 1300
  0.7 41.1 %copy-start.8 = (s32[1,27,4]{1,2,0:T(4,128)S(1)}, s32[1,27,4]{1,2,0:T(4,128)}, u32[]{:S(2)}) copy-start(s32[1,27,4]{1,2,0:T(4,128)} %param.14) | copy-start | bytes 1300
  1.9 13.4 %collective-permute-start.5 = (bf16[27,128,128]{2,1,0:T(8,128)(2,1)S(1)}, bf16[27,128,128]{2,1,0:T(8,128)(2,1)S(1)}, u32[]{:S(2)}, u32[]{:S(2)}) collective-permute-start(bf16[27,128,128]{2,1,0:T(8,128)(2,1)S(1)} %constant_dynamic-slice_fusion), channel_id=1, source_target_pairs={{0,1},{1,2},{2,3},{3,0},{4,5},{5,6},{6,7},{7,4},{8,9},{9,10},{10,1... | collective-permute-start | bytes 2654216 | tf_op jit(solution)/shard_map/ppermute | solution.py:280
  15.3 32.4 %copy-start.10 = (bf16[27,128,128]{2,1,0:T(8,128)(2,1)}, bf16[27,128,128]{2,1,0:T(8,128)(2,1)S(1)}, u32[]{:S(2)}) copy-start(bf16[27,128,128]{2,1,0:T(8,128)(2,1)S(1)} %collective-permute-done.5.far) | copy-start | bytes 2654212
  15.3 32.4 %collective-permute-start.6 = (bf16[27,128,128]{2,1,0:T(8,128)(2,1)S(1)}, bf16[27,128,128]{2,1,0:T(8,128)(2,1)S(1)}, u32[]{:S(2)}, u32[]{:S(2)}) collective-permute-start(bf16[27,128,128]{2,1,0:T(8,128)(2,1)S(1)} %collective-permute-done.5.far), channel_id=1, source_target_pairs={{0,128},{1,129},{2,130},{3,131},{4,132},{5,133},{6,134},{7,135},{8... | collective-permute-start | bytes 2654216 | tf_op jit(solution)/shard_map/ppermute | solution.py:60
  22.7 25.0 %collective-permute-start = (bf16[4,128,256]{2,1,0:T(8,128)(2,1)}, bf16[4,128,256]{2,1,0:T(8,128)(2,1)S(1)}, u32[]{:S(2)}, u32[]{:S(2)}) collective-permute-start(bf16[4,128,256]{2,1,0:T(8,128)(2,1)} %get-tuple-element.18), channel_id=1, source_target_pairs={{0,128},{1,129},{2,130},{3,131},{4,132},{5,133},{6,134},{7,135},{8... | collective-permute-start | bytes 786440 | tf_op jit(solution)/shard_map/ppermute | solution.py:71
  22.8 24.9 %collective-permute-start.1 = (bf16[4,128,256]{2,1,0:T(8,128)(2,1)}, bf16[4,128,256]{2,1,0:T(8,128)(2,1)S(1)}, u32[]{:S(2)}, u32[]{:S(2)}) collective-permute-start(bf16[4,128,256]{2,1,0:T(8,128)(2,1)} %get-tuple-element.19), channel_id=1, source_target_pairs={{0,2},{1,3},{2,4},{3,5},{4,6},{5,7},{6,8},{7,9},{8,10},{9,11},{10,... | collective-permute-start | bytes 786440 | tf_op jit(solution)/shard_map/ppermute | solution.py:71
  24.5 23.2 %collective-permute-start.2 = (bf16[4,128,256]{2,1,0:T(8,128)(2,1)}, bf16[4,128,256]{2,1,0:T(8,128)(2,1)S(1)}, u32[]{:S(2)}, u32[]{:S(2)}) collective-permute-start(bf16[4,128,256]{2,1,0:T(8,128)(2,1)} %get-tuple-element.20), channel_id=1, source_target_pairs={{2,0},{3,1},{4,2},{5,3},{6,4},{7,5},{8,6},{9,7},{10,8},{11,9},{12,... | collective-permute-start | bytes 786440 | tf_op jit(solution)/shard_map/ppermute | solution.py:71
  25.8 13.9 %collective-permute-start.3 = (bf16[128,256]{1,0:T(8,128)(2,1)}, bf16[128,256]{1,0:T(8,128)(2,1)S(1)}, u32[]{:S(2)}, u32[]{:S(2)}) collective-permute-start(bf16[128,256]{1,0:T(8,128)(2,1)} %get-tuple-element.21), channel_id=1, source_target_pairs={{0,130},{1,131},{2,132},{3,133},{4,134},{5,135},{6,136},{7,137},{8... | collective-permute-start | bytes 196616 | tf_op jit(solution)/shard_map/ppermute | solution.py:71
  39.7 8.0 %copy-start.15 = (bf16[128,256]{1,0:T(8,128)(2,1)}, bf16[128,256]{1,0:T(8,128)(2,1)S(1)}, u32[]{:S(2)}) copy-start(bf16[128,256]{1,0:T(8,128)(2,1)S(1)} %collective-permute-done.3.low_c) | copy-start | bytes 196612
  39.7 7.9 %collective-permute-start.4 = (bf16[128,256]{1,0:T(8,128)(2,1)}, bf16[128,256]{1,0:T(8,128)(2,1)S(1)}, u32[]{:S(2)}, u32[]{:S(2)}) collective-permute-start(bf16[128,256]{1,0:T(8,128)(2,1)} %get-tuple-element.22), channel_id=1, source_target_pairs={{2,128},{3,129},{4,130},{5,131},{6,132},{7,133},{8,134},{9,135},{1... | collective-permute-start | bytes 196616 | tf_op jit(solution)/shard_map/ppermute | solution.py:71
  47.7 1.2 copy-start.11
  72.9 3.9 %collective-permute-start.12 = (bf16[4,2,27,16,256]{4,3,2,1,0:T(8,128)(2,1)}, bf16[4,2,27,16,256]{4,3,2,1,0:T(8,128)(2,1)S(1)}, u32[]{:S(2)}, u32[]{:S(2)}) collective-permute-start(bf16[4,2,27,16,256]{4,3,2,1,0:T(8,128)(2,1)} %get-tuple-element.32), channel_id=1, source_target_pairs={{0,128},{1,129},{2,130},{3,131},{4,132},{5,133},{6,134},{7,135},{8... | collective-permute-start | bytes 5308424 | tf_op jit(solution)/shard_map/ppermute | solution.py:60
  78.5 21.8 %collective-permute-start.15 = (bf16[2,27,16,256]{3,2,1,0:T(8,128)(2,1)S(1)}, bf16[2,27,16,256]{3,2,1,0:T(8,128)(2,1)S(1)}, u32[]{:S(2)}, u32[]{:S(2)}) collective-permute-start(bf16[2,27,16,256]{3,2,1,0:T(8,128)(2,1)S(1)} %get-tuple-element.36), channel_id=1, source_target_pairs={{0,12},{1,13},{2,14},{3,15},{4,0},{5,1},{6,2},{7,3},{8,4},{9,5},{1... | collective-permute-start | bytes 1327112 | tf_op jit(solution)/shard_map/ppermute | solution.py:60
  81.5 18.8 %collective-permute-start.14 = (bf16[2,27,16,256]{3,2,1,0:T(8,128)(2,1)S(1)}, bf16[2,27,16,256]{3,2,1,0:T(8,128)(2,1)}, u32[]{:S(2)}, u32[]{:S(2)}) collective-permute-start(bf16[2,27,16,256]{3,2,1,0:T(8,128)(2,1)S(1)} %get-tuple-element.37), channel_id=1, source_target_pairs={{0,8},{1,9},{2,10},{3,11},{4,12},{5,13},{6,14},{7,15},{8,0},{9,1},... | collective-permute-start | bytes 1327112 | tf_op jit(solution)/shard_map/ppermute | solution.py:60
  81.9 22.8 %collective-permute-start.13 = (bf16[2,27,16,256]{3,2,1,0:T(8,128)(2,1)S(1)}, bf16[2,27,16,256]{3,2,1,0:T(8,128)(2,1)}, u32[]{:S(2)}, u32[]{:S(2)}) collective-permute-start(bf16[2,27,16,256]{3,2,1,0:T(8,128)(2,1)S(1)} %get-tuple-element.35), channel_id=1, source_target_pairs={{0,4},{1,5},{2,6},{3,7},{4,8},{5,9},{6,10},{7,11},{8,12},{9,13},{1... | collective-permute-start | bytes 1327112 | tf_op jit(solution)/shard_map/ppermute | solution.py:60
  106.4 6.1 %collective-permute-start.18 = (bf16[27,16,128]{2,1,0:T(8,128)(2,1)S(1)}, bf16[27,16,128]{2,1,0:T(8,128)(2,1)S(1)}, u32[]{:S(2)}, u32[]{:S(2)}) collective-permute-start(bf16[27,16,128]{2,1,0:T(8,128)(2,1)S(1)} %get-tuple-element.39), channel_id=1, source_target_pairs={{0,3},{1,0},{2,1},{3,2},{4,7},{5,4},{6,5},{7,6},{8,11},{9,8},{10,9... | collective-permute-start | bytes 331784 | tf_op jit(solution)/shard_map/ppermute | solution.py:60
  109.5 5.2 %collective-permute-start.17 = (bf16[27,16,128]{2,1,0:T(8,128)(2,1)S(1)}, bf16[27,16,128]{2,1,0:T(8,128)(2,1)S(1)}, u32[]{:S(2)}, u32[]{:S(2)}) collective-permute-start(bf16[27,16,128]{2,1,0:T(8,128)(2,1)S(1)} %get-tuple-element.40), channel_id=1, source_target_pairs={{0,2},{1,3},{2,0},{3,1},{4,6},{5,7},{6,4},{7,5},{8,10},{9,11},{10,... | collective-permute-start | bytes 331784 | tf_op jit(solution)/shard_map/ppermute | solution.py:60
  109.9 8.1 %collective-permute-start.16 = (bf16[27,16,128]{2,1,0:T(8,128)(2,1)S(1)}, bf16[27,16,128]{2,1,0:T(8,128)(2,1)S(1)}, u32[]{:S(2)}, u32[]{:S(2)}) collective-permute-start(bf16[27,16,128]{2,1,0:T(8,128)(2,1)S(1)} %get-tuple-element.38), channel_id=1, source_target_pairs={{0,1},{1,2},{2,3},{3,0},{4,5},{5,6},{6,7},{7,4},{8,9},{9,10},{10,1... | collective-permute-start | bytes 331784 | tf_op jit(solution)/shard_map/ppermute | solution.py:60
  118.2 11.9 %collective-permute-start.25 = (bf16[4,16,128]{2,1,0:T(8,128)(2,1)S(1)}, bf16[4,16,128]{2,1,0:T(8,128)(2,1)S(1)}, u32[]{:S(2)}, u32[]{:S(2)}) collective-permute-start(bf16[4,16,128]{2,1,0:T(8,128)(2,1)S(1)} %get-tuple-element.49), channel_id=1, source_target_pairs={{0,112},{1,113},{2,114},{3,115},{4,116},{5,117},{6,118},{7,119},{8... | collective-permute-start | bytes 49160 | tf_op jit(solution)/shard_map/ppermute | solution.py:60
  120.7 13.0 %collective-permute-start.24 = (bf16[4,16,128]{2,1,0:T(8,128)(2,1)S(1)}, bf16[4,16,128]{2,1,0:T(8,128)(2,1)S(1)}, u32[]{:S(2)}, u32[]{:S(2)}) collective-permute-start(bf16[4,16,128]{2,1,0:T(8,128)(2,1)S(1)} %get-tuple-element.48), channel_id=1, source_target_pairs={{0,96},{1,97},{2,98},{3,99},{4,100},{5,101},{6,102},{7,103},{8,104... | collective-permute-start | bytes 49160 | tf_op jit(solution)/shard_map/ppermute | solution.py:60
  124.7 8.9 %collective-permute-start.23 = (bf16[4,16,128]{2,1,0:T(8,128)(2,1)S(1)}, bf16[4,16,128]{2,1,0:T(8,128)(2,1)S(1)}, u32[]{:S(2)}, u32[]{:S(2)}) collective-permute-start(bf16[4,16,128]{2,1,0:T(8,128)(2,1)S(1)} %get-tuple-element.47), channel_id=1, source_target_pairs={{0,80},{1,81},{2,82},{3,83},{4,84},{5,85},{6,86},{7,87},{8,88},{9,... | collective-permute-start | bytes 49160 | tf_op jit(solution)/shard_map/ppermute | solution.py:60
  126.9 6.8 %collective-permute-start.22 = (bf16[4,16,128]{2,1,0:T(8,128)(2,1)S(1)}, bf16[4,16,128]{2,1,0:T(8,128)(2,1)S(1)}, u32[]{:S(2)}, u32[]{:S(2)}) collective-permute-start(bf16[4,16,128]{2,1,0:T(8,128)(2,1)S(1)} %get-tuple-element.46), channel_id=1, source_target_pairs={{0,64},{1,65},{2,66},{3,67},{4,68},{5,69},{6,70},{7,71},{8,72},{9,... | collective-permute-start | bytes 49160 | tf_op jit(solution)/shard_map/ppermute | solution.py:60
  129.6 5.9 %collective-permute-start.21 = (bf16[4,16,128]{2,1,0:T(8,128)(2,1)S(1)}, bf16[4,16,128]{2,1,0:T(8,128)(2,1)S(1)}, u32[]{:S(2)}, u32[]{:S(2)}) collective-permute-start(bf16[4,16,128]{2,1,0:T(8,128)(2,1)S(1)} %get-tuple-element.45), channel_id=1, source_target_pairs={{0,48},{1,49},{2,50},{3,51},{4,52},{5,53},{6,54},{7,55},{8,56},{9,... | collective-permute-start | bytes 49160 | tf_op jit(solution)/shard_map/ppermute | solution.py:60
  130.1 5.5 %collective-permute-start.20 = (bf16[4,16,128]{2,1,0:T(8,128)(2,1)S(1)}, bf16[4,16,128]{2,1,0:T(8,128)(2,1)S(1)}, u32[]{:S(2)}, u32[]{:S(2)}) collective-permute-start(bf16[4,16,128]{2,1,0:T(8,128)(2,1)S(1)} %get-tuple-element.44), channel_id=1, source_target_pairs={{0,32},{1,33},{2,34},{3,35},{4,36},{5,37},{6,38},{7,39},{8,40},{9,... | collective-permute-start | bytes 49160 | tf_op jit(solution)/shard_map/ppermute | solution.py:60
  133.6 4.3 %collective-permute-start.19 = (bf16[4,16,128]{2,1,0:T(8,128)(2,1)S(1)}, bf16[4,16,128]{2,1,0:T(8,128)(2,1)S(1)}, u32[]{:S(2)}, u32[]{:S(2)}) collective-permute-start(bf16[4,16,128]{2,1,0:T(8,128)(2,1)S(1)} %get-tuple-element.43), channel_id=1, source_target_pairs={{0,16},{1,17},{2,18},{3,19},{4,20},{5,21},{6,22},{7,23},{8,24},{9,... | collective-permute-start | bytes 49160 | tf_op jit(solution)/shard_map/ppermute | solution.py:60
  138.0 7.5 %collective-permute-start.26 = (bf16[4,16,128]{2,1,0:T(8,128)(2,1)S(1)}, bf16[4,16,128]{2,1,0:T(8,128)(2,1)S(1)}, u32[]{:S(2)}, u32[]{:S(2)}) collective-permute-start(bf16[4,16,128]{2,1,0:T(8,128)(2,1)S(1)} %get-tuple-element.34), channel_id=1, source_target_pairs={{0,16},{1,17},{2,18},{3,19},{4,20},{5,21},{6,22},{7,23},{8,24},{9,... | collective-permute-start | bytes 49160 | tf_op jit(solution)/shard_map/ppermute | solution.py:60
  138.1 10.2 %collective-permute-start.27 = (bf16[4,16,128]{2,1,0:T(8,128)(2,1)S(1)}, bf16[4,16,128]{2,1,0:T(8,128)(2,1)S(1)}, u32[]{:S(2)}, u32[]{:S(2)}) collective-permute-start(bf16[4,16,128]{2,1,0:T(8,128)(2,1)S(1)} %get-tuple-element.34), channel_id=1, source_target_pairs={{0,32},{1,33},{2,34},{3,35},{4,36},{5,37},{6,38},{7,39},{8,40},{9,... | collective-permute-start | bytes 49160 | tf_op jit(solution)/shard_map/ppermute | solution.py:60
  138.3 10.5 %collective-permute-start.28 = (bf16[4,16,128]{2,1,0:T(8,128)(2,1)S(1)}, bf16[4,16,128]{2,1,0:T(8,128)(2,1)S(1)}, u32[]{:S(2)}, u32[]{:S(2)}) collective-permute-start(bf16[4,16,128]{2,1,0:T(8,128)(2,1)S(1)} %get-tuple-element.34), channel_id=1, source_target_pairs={{0,48},{1,49},{2,50},{3,51},{4,52},{5,53},{6,54},{7,55},{8,56},{9,... | collective-permute-start | bytes 49160 | tf_op jit(solution)/shard_map/ppermute | solution.py:60
  140.3 8.5 %collective-permute-start.29 = (bf16[4,16,128]{2,1,0:T(8,128)(2,1)S(1)}, bf16[4,16,128]{2,1,0:T(8,128)(2,1)S(1)}, u32[]{:S(2)}, u32[]{:S(2)}) collective-permute-start(bf16[4,16,128]{2,1,0:T(8,128)(2,1)S(1)} %get-tuple-element.34), channel_id=1, source_target_pairs={{0,64},{1,65},{2,66},{3,67},{4,68},{5,69},{6,70},{7,71},{8,72},{9,... | collective-permute-start | bytes 49160 | tf_op jit(solution)/shard_map/ppermute | solution.py:60
  143.7 5.1 %collective-permute-start.30 = (bf16[4,16,128]{2,1,0:T(8,128)(2,1)S(1)}, bf16[4,16,128]{2,1,0:T(8,128)(2,1)S(1)}, u32[]{:S(2)}, u32[]{:S(2)}) collective-permute-start(bf16[4,16,128]{2,1,0:T(8,128)(2,1)S(1)} %get-tuple-element.34), channel_id=1, source_target_pairs={{0,80},{1,81},{2,82},{3,83},{4,84},{5,85},{6,86},{7,87},{8,88},{9,... | collective-permute-start | bytes 49160 | tf_op jit(solution)/shard_map/ppermute | solution.py:60
  145.5 4.2 %collective-permute-start.31 = (bf16[4,16,128]{2,1,0:T(8,128)(2,1)S(1)}, bf16[4,16,128]{2,1,0:T(8,128)(2,1)S(1)}, u32[]{:S(2)}, u32[]{:S(2)}) collective-permute-start(bf16[4,16,128]{2,1,0:T(8,128)(2,1)S(1)} %get-tuple-element.34), channel_id=1, source_target_pairs={{0,96},{1,97},{2,98},{3,99},{4,100},{5,101},{6,102},{7,103},{8,104... | collective-permute-start | bytes 49160 | tf_op jit(solution)/shard_map/ppermute | solution.py:60
  148.3 2.9 %collective-permute-start.32 = (bf16[4,16,128]{2,1,0:T(8,128)(2,1)S(1)}, bf16[4,16,128]{2,1,0:T(8,128)(2,1)S(1)}, u32[]{:S(2)}, u32[]{:S(2)}) collective-permute-start(bf16[4,16,128]{2,1,0:T(8,128)(2,1)S(1)} %get-tuple-element.34), channel_id=1, source_target_pairs={{0,112},{1,113},{2,114},{3,115},{4,116},{5,117},{6,118},{7,119},{8... | collective-permute-start | bytes 49160 | tf_op jit(solution)/shard_map/ppermute | solution.py:60
  151.2 5.3 %collective-permute-start.33 = (bf16[8,4,16,128]{3,2,1,0:T(8,128)(2,1)S(1)}, bf16[8,4,16,128]{3,2,1,0:T(8,128)(2,1)S(1)}, u32[]{:S(2)}, u32[]{:S(2)}) collective-permute-start(bf16[8,4,16,128]{3,2,1,0:T(8,128)(2,1)S(1)} %constant_dynamic-update-slice_fusion), channel_id=1, source_target_pairs={{0,2},{1,3},{2,0},{3,1},{4,6},{5,7},{6,4},{7,5},{8,10},{9,11},{10,... | collective-permute-start | bytes 393224 | tf_op jit(solution)/shard_map/ppermute | solution.py:60
  156.5 5.6 %collective-permute-start.36 = (bf16[2,8,4,16,128]{4,3,2,1,0:T(8,128)(2,1)S(1)}, bf16[2,8,4,16,128]{4,3,2,1,0:T(8,128)(2,1)S(1)}, u32[]{:S(2)}, u32[]{:S(2)}) collective-permute-start(bf16[2,8,4,16,128]{4,3,2,1,0:T(8,128)(2,1)S(1)} %get-tuple-element.42), channel_id=1, source_target_pairs={{0,12},{1,13},{2,14},{3,15},{4,0},{5,1},{6,2},{7,3},{8,4},{9,5},{1... | collective-permute-start | bytes 786440 | tf_op jit(solution)/shard_map/ppermute | solution.py:60
  156.6 6.9 %collective-permute-start.35 = (bf16[2,8,4,16,128]{4,3,2,1,0:T(8,128)(2,1)S(1)}, bf16[2,8,4,16,128]{4,3,2,1,0:T(8,128)(2,1)S(1)}, u32[]{:S(2)}, u32[]{:S(2)}) collective-permute-start(bf16[2,8,4,16,128]{4,3,2,1,0:T(8,128)(2,1)S(1)} %get-tuple-element.42), channel_id=1, source_target_pairs={{0,8},{1,9},{2,10},{3,11},{4,12},{5,13},{6,14},{7,15},{8,0},{9,1},... | collective-permute-start | bytes 786440 | tf_op jit(solution)/shard_map/ppermute | solution.py:60
  157.6 8.6 %collective-permute-start.34 = (bf16[2,8,4,16,128]{4,3,2,1,0:T(8,128)(2,1)S(1)}, bf16[2,8,4,16,128]{4,3,2,1,0:T(8,128)(2,1)S(1)}, u32[]{:S(2)}, u32[]{:S(2)}) collective-permute-start(bf16[2,8,4,16,128]{4,3,2,1,0:T(8,128)(2,1)S(1)} %get-tuple-element.42), channel_id=1, source_target_pairs={{0,4},{1,5},{2,6},{3,7},{4,8},{5,9},{6,10},{7,11},{8,12},{9,13},{1... | collective-permute-start | bytes 786440 | tf_op jit(solution)/shard_map/ppermute | solution.py:60
  166.4 23.1 %copy-start = (bf16[4,2,8,4,16,128]{5,4,3,2,1,0:T(8,128)(2,1)}, bf16[4,2,8,4,16,128]{5,4,3,2,1,0:T(8,128)(2,1)S(1)}, u32[]{:S(2)}) copy-start(bf16[4,2,8,4,16,128]{5,4,3,2,1,0:T(8,128)(2,1)S(1)} %pad_maximum_fusion.mine) | copy-start | bytes 3145732
  166.4 52.4 %collective-permute-start.37 = (bf16[4,2,8,4,16,128]{5,4,3,2,1,0:T(8,128)(2,1)S(1)}, bf16[4,2,8,4,16,128]{5,4,3,2,1,0:T(8,128)(2,1)S(1)}, u32[]{:S(2)}, u32[]{:S(2)}) collective-permute-start(bf16[4,2,8,4,16,128]{5,4,3,2,1,0:T(8,128)(2,1)S(1)} %pad_maximum_fusion.mine), channel_id=1, source_target_pairs={{0,128},{1,129},{2,130},{3,131},{4,132},{5,133},{6,134},{7,135},{8... | collective-permute-start | bytes 3145736 | tf_op jit(solution)/shard_map/ppermute | solution.py:60
  189.5 25.8 %collective-permute-start.7 = (bf16[4,128,256]{2,1,0:T(8,128)(2,1)}, bf16[4,128,256]{2,1,0:T(8,128)(2,1)S(1)}, u32[]{:S(2)}, u32[]{:S(2)}) collective-permute-start(bf16[4,128,256]{2,1,0:T(8,128)(2,1)} %get-tuple-element.26), channel_id=1, source_target_pairs={{0,128},{1,129},{2,130},{3,131},{4,132},{5,133},{6,134},{7,135},{8... | collective-permute-start | bytes 786440 | tf_op jit(solution)/shard_map/ppermute | solution.py:71
  189.9 25.5 %collective-permute-start.8 = (bf16[4,128,256]{2,1,0:T(8,128)(2,1)}, bf16[4,128,256]{2,1,0:T(8,128)(2,1)S(1)}, u32[]{:S(2)}, u32[]{:S(2)}) collective-permute-start(bf16[4,128,256]{2,1,0:T(8,128)(2,1)} %get-tuple-element.27), channel_id=1, source_target_pairs={{0,2},{1,3},{2,4},{3,5},{4,6},{5,7},{6,8},{7,9},{8,10},{9,11},{10,... | collective-permute-start | bytes 786440 | tf_op jit(solution)/shard_map/ppermute | solution.py:71
  192.2 23.2 %collective-permute-start.9 = (bf16[4,128,256]{2,1,0:T(8,128)(2,1)}, bf16[4,128,256]{2,1,0:T(8,128)(2,1)S(1)}, u32[]{:S(2)}, u32[]{:S(2)}) collective-permute-start(bf16[4,128,256]{2,1,0:T(8,128)(2,1)} %get-tuple-element.28), channel_id=1, source_target_pairs={{2,0},{3,1},{4,2},{5,3},{6,4},{7,5},{8,6},{9,7},{10,8},{11,9},{12,... | collective-permute-start | bytes 786440 | tf_op jit(solution)/shard_map/ppermute | solution.py:71
  193.5 13.9 %collective-permute-start.10 = (bf16[128,256]{1,0:T(8,128)(2,1)}, bf16[128,256]{1,0:T(8,128)(2,1)S(1)}, u32[]{:S(2)}, u32[]{:S(2)}) collective-permute-start(bf16[128,256]{1,0:T(8,128)(2,1)} %get-tuple-element.29), channel_id=1, source_target_pairs={{0,130},{1,131},{2,132},{3,133},{4,134},{5,135},{6,136},{7,137},{8... | collective-permute-start | bytes 196616 | tf_op jit(solution)/shard_map/ppermute | solution.py:71
  207.4 8.0 %copy-start.5 = (bf16[128,256]{1,0:T(8,128)(2,1)}, bf16[128,256]{1,0:T(8,128)(2,1)S(1)}, u32[]{:S(2)}) copy-start(bf16[128,256]{1,0:T(8,128)(2,1)S(1)} %collective-permute-done.10.low_c) | copy-start | bytes 196612
  207.4 7.9 %collective-permute-start.11 = (bf16[128,256]{1,0:T(8,128)(2,1)}, bf16[128,256]{1,0:T(8,128)(2,1)S(1)}, u32[]{:S(2)}, u32[]{:S(2)}) collective-permute-start(bf16[128,256]{1,0:T(8,128)(2,1)} %get-tuple-element.30), channel_id=1, source_target_pairs={{2,128},{3,129},{4,130},{5,131},{6,132},{7,133},{8,134},{9,135},{1... | collective-permute-start | bytes 196616 | tf_op jit(solution)/shard_map/ppermute | solution.py:71
  215.4 0.9 copy-start.4
  218.8 1.0 copy-start.1
  (7 other events, 5.2 us)

commit v2 on v1

v2 whole, which is shorter than its diff:
```python
import functools

import jax
import jax.numpy as jnp
from jax import lax
from jax.experimental import pallas as pl
from jax.experimental.pallas import tpu as pltpu
from jax.sharding import PartitionSpec as P

ALL = ("gx", "gy", "rep")
K, C, NB, ROWS, PAIRS = 27, 256, 8, 128, 4
EXT = 29
KPAD = 32
BF, F32 = jnp.bfloat16, jnp.float32
VM = pl.BlockSpec(memory_space=pltpu.VMEM)
SM = pl.BlockSpec(memory_space=pltpu.SMEM)
PARAMS = pltpu.CompilerParams(vmem_limit_bytes=58 * 1024 * 1024)


def shape_of(*dims, dtype=BF):
    return jax.ShapeDtypeStruct(dims, dtype)


def call(kernel, ins, outs, scratch=(), cost=None):
    place = {"s": SM, "v": VM, "a": pl.BlockSpec(memory_space=pl.ANY)}
    outs = [out if isinstance(out, tuple) else ("v", out) for out in outs]
    return pl.pallas_call(
        kernel,
        out_shape=[out for _, out in outs],
        in_specs=[place[kind] for kind, _ in ins],
        out_specs=[place[kind] for kind, _ in outs],
        scratch_shapes=list(scratch),
        compiler_params=PARAMS,
        cost_estimate=cost,
    )(*[value for _, value in ins])


def flat_id(core, x, y, z):
    return (core * 64 + ((z % 8) * 4 + y % 4) * 2 + (x % 4) // 2) * 2 + x % 2


def torus_perm(move):
    pairs = []
    for core in range(2):
        for z in range(8):
            for y in range(4):
                for x in range(4):
                    pairs.append((flat_id(core, x, y, z), flat_id(*move(core, x, y, z))))
    return pairs


def shift(value, **by):
    def move(core, x, y, z):
        return (
            (core + by.get("core", 0)) % 2,
            x + by.get("x", 0),
            y + by.get("y", 0),
            z + by.get("z", 0),
        )

    return lax.ppermute(value, ALL, torus_perm(move))


def grid_shift(value, step_x, step_y):
    pairs = []
    for i in range(2):
        for j in range(64):
            if 0 <= j + step_y < 64:
                for r in range(2):
                    to = ((i + step_x) % 2 * 64 + j + step_y) * 2 + r
                    pairs.append(((i * 64 + j) * 2 + r, to))
    return lax.ppermute(value, ALL, pairs)


def pick_kernel(core_ref, face_ref, corner_ref, feats, weight, face_x, low_y, high_y, part, sem):
    i = core_ref[0]
    rows = pl.ds(pl.multiple_of(i * 128, 128), 128)
    copy = pltpu.make_async_copy(weight.at[:, rows, :], part, sem)
    copy.start()
    for n in range(4):
        face_x[n] = feats[face_ref[(1 - i) * 4 + n]]
        low_y[n] = feats[face_ref[8 + n]]
        high_y[n] = feats[face_ref[12 + n]]
    for n in range(2):
        face_x[4 + n] = feats[corner_ref[2 * (1 - i) + n]]
    low_y[4] = face_x[4]
    high_y[4] = face_x[5]
    copy.wait()


def weight_copies(core, side, own, far, far_other, full, sems):
    near_rows = pl.ds(pl.multiple_of(core * 128, 128), 128)
    other_rows = pl.ds(pl.multiple_of((1 - core) * 128, 128), 128)
    mine = slice(side * 128, side * 128 + 128)
    theirs = slice(128 - side * 128, 256 - side * 128)
    return (
        pltpu.make_async_copy(own, full.at[:, :, mine], sems.at[0]),
        pltpu.make_async_copy(far, full.at[:, near_rows, theirs], sems.at[1]),
        pltpu.make_async_copy(far_other, full.at[:, other_rows, theirs], sems.at[2]),
    )


def on_weights(act, core, rep, *refs):
    for side in range(2):

        @pl.when(rep == side)
        def _():
            for copy in weight_copies(core, side, *refs):
                getattr(copy, act)()


def forward_kernel(
    meta, outs, ins, maps, feats, from_x, from_low, from_high, own, far, far_other, cotan,
    act, grad, keep, send,
    ext, full, rows, acc, flipped, sems,
):
    core, rep = meta[0], meta[1]
    weights = (own, far, far_other, full, sems)
    on_weights("start", core, rep, *weights)
    ext[8:16] = jnp.zeros((8, ROWS, C), BF)
    ext[24:29] = jnp.zeros((5, ROWS, C), BF)
    copies = [
        pltpu.make_async_copy(feats, ext.at[0:8], sems.at[3]),
        pltpu.make_async_copy(from_x.at[0:4], ext.at[pl.ds(8 + 4 * (1 - core), 4)], sems.at[4]),
        pltpu.make_async_copy(from_low.at[0:4], ext.at[16:20], sems.at[5]),
        pltpu.make_async_copy(from_high.at[0:4], ext.at[20:24], sems.at[6]),
        pltpu.make_async_copy(from_low.at[4], ext.at[24 + 2 * (1 - core)], sems.at[7]),
        pltpu.make_async_copy(from_high.at[4], ext.at[25 + 2 * (1 - core)], sems.at[8]),
    ]
    for copy in copies:
        copy.start()
    acc[...] = jnp.zeros_like(acc)
    places = lax.broadcasted_iota(jnp.int32, (ROWS, ROWS), 0)
    for copy in copies:
        copy.wait()
    on_weights("wait", core, rep, *weights)

    def gather_step(k, carry):
        map_k = maps[k]
        for p in range(PAIRS):
            hot = (places == map_k[p : p + 1, :]).astype(F32).astype(BF)
            picked = lax.dot_general(
                hot, ext[ins[k * PAIRS + p]], (((0,), (0,)), ((), ())), preferred_element_type=F32
            )
            rows[k, p * ROWS : (p + 1) * ROWS, :] = picked.astype(BF)
        product = jnp.dot(rows[k], full[k], preferred_element_type=F32)
        for p in range(PAIRS):
            acc[outs[k * PAIRS + p]] += product[p * ROWS : (p + 1) * ROWS]
        return carry

    lax.fori_loop(0, K, gather_step, 0, unroll=3)

    def grad_step(b, carry):
        value = acc[b]
        sigma = 1.0 / (1.0 + jnp.exp(-value))
        act[b] = (value * sigma).astype(BF)
        up = cotan[b].astype(F32) * (sigma * (1.0 + value * (1.0 - sigma)))
        grad[b] = up.astype(BF)
        flipped[b] = up.T.astype(BF)
        return carry

    lax.fori_loop(0, NB, grad_step, 0)

    def weight_step(k, carry):
        left = jnp.concatenate([flipped[outs[k * PAIRS + p]] for p in range(PAIRS)], axis=1)
        part = jnp.dot(left, rows[k], preferred_element_type=F32)
        for side in range(2):
            first = part[side * 128 : side * 128 + 64]
            second = part[side * 128 + 64 : side * 128 + 128]
            kept = jnp.where(core == 0, first, second).astype(BF)
            sent = jnp.where(core == 0, second, first).astype(BF)
            for y in range(4):
                for x in range(2):
                    at = (slice(y * 16, y * 16 + 16), slice(x * 128, x * 128 + 128))
                    keep[y * 4 + side * 2 + x, k] = kept[at]
                    send[y * 4 + side * 2 + x, k] = sent[at]
        return carry

    lax.fori_loop(0, K, weight_step, 0, unroll=3)


def backward_kernel(
    meta, outs, ins, maps, grad, own, far, far_other,
    local, face_x, to_low, to_high,
    full, acc, sems,
):
    core, rep = meta[0], meta[1]
    weights = (own, far, far_other, full, sems)
    on_weights("start", core, rep, *weights)
    acc[...] = jnp.zeros_like(acc)
    places = lax.broadcasted_iota(jnp.int32, (ROWS, ROWS), 0)
    on_weights("wait", core, rep, *weights)

    def step(k, carry):
        map_k = maps[k]
        parts = []
        for p in range(PAIRS):
            hot = (places == map_k[p : p + 1, :]).astype(F32).astype(BF)
            spread = jnp.dot(hot, grad[outs[k * PAIRS + p]], preferred_element_type=F32)
            parts.append(spread.astype(BF))
        product = lax.dot_general(
            jnp.concatenate(parts, 0), full[k], (((1,), (1,)), ((), ())), preferred_element_type=F32
        )
        for p in range(PAIRS):
            acc[ins[k * PAIRS + p]] += product[p * ROWS : (p + 1) * ROWS]
        return carry

    lax.fori_loop(0, K, step, 0, unroll=3)
    local[...] = acc[0:8]
    face_x[0:4] = acc[pl.ds(8 + 4 * (1 - core), 4)].astype(BF)
    face_x[4:6] = jnp.zeros((2, ROWS, C), BF)
    to_low[0:4] = acc[16:20].astype(BF)
    to_low[4] = acc[24 + 2 * (1 - core)].astype(BF)
    to_high[0:4] = acc[20:24].astype(BF)
    to_high[4] = acc[25 + 2 * (1 - core)].astype(BF)


def input_kernel(core_ref, face_ref, corner_ref, local, from_x, from_low, from_high, out, acc):
    i = core_ref[0]
    acc[...] = local[...]
    for n in range(4):
        acc[face_ref[(1 - i) * 4 + n]] += from_x[n].astype(F32)
        acc[face_ref[8 + n]] += from_low[n].astype(F32)
        acc[face_ref[12 + n]] += from_high[n].astype(F32)
    for n in range(2):
        acc[corner_ref[2 * (1 - i) + n]] += from_x[4 + n].astype(F32)
    out[...] = acc[...].astype(BF)


def pair_kernel(keep, got, after, out):
    def step(n, carry):
        out[n] = (keep[n].astype(F32) + got[n].astype(F32)).astype(BF)
        return carry

    lax.fori_loop(0, 16, step, 0)


def final_kernel(scale, meta, mine, other, out):
    core, half, y_at = meta[0], meta[2], meta[3]

    def step(k, carry):
        sides = []
        for source in (mine, other):
            halves = []
            for x in range(2):
                pieces = [
                    source[(y_at - y) & 3, (half - x) & 1, k // 4, k % 4].astype(F32)
                    for y in range(4)
                ]
                halves.append(jnp.concatenate(pieces, 0))
            sides.append(jnp.concatenate(halves, 1) * scale)
        first = jnp.where(core == 0, sides[0], sides[1])
        second = jnp.where(core == 0, sides[1], sides[0])
        out[k] = jnp.concatenate([first, second], 0).T
        return carry

    lax.fori_loop(0, K, step, 0, unroll=3)


def members(key):
    found = {}
    for y in range(4):
        for rep in range(2):
            for half in range(2):
                for z in range(8):
                    for core in range(2):
                        x = half * 2 + rep
                        found.setdefault(key(core, x, y, z), []).append(flat_id(core, x, y, z))
    return list(found.values())


def exchange(value, key):
    return lax.all_to_all(
        value, ALL, split_axis=0, concat_axis=0, axis_index_groups=members(key), tiled=False
    )


def collect_ring(value, count, axis, stride=1):
    return jnp.stack(
        [value] + [shift(value, **{axis: s * stride}) for s in range(1, count)], 0
    )


def body(feats, weight, cotan, face_send, corner_send, pair_out, pair_in, row_map):
    core = lax.axis_index("gx")
    gy = lax.axis_index("gy")
    rep = lax.axis_index("rep")
    half, y_at, z_at = gy % 2, gy // 2 % 4, gy // 8
    meta = jnp.stack([core, rep, half, y_at, z_at]).astype(jnp.int32)
    blocks = feats.reshape(NB, ROWS, C)
    face = face_send.reshape(16)
    corner = corner_send.reshape(4)
    outs, ins = pair_out.reshape(-1), pair_in.reshape(-1)
    maps = row_map[0]
    five, six = shape_of(5, ROWS, C), shape_of(6, ROWS, C)

    face_x, low_y, high_y, part = call(
        pick_kernel,
        [("s", meta), ("s", face), ("s", corner), ("v", blocks), ("a", weight)],
        [six, five, five, shape_of(K, 128, 128)],
        [pltpu.SemaphoreType.DMA],
    )
    from_x = grid_shift(face_x, 1, 0)
    low_y = lax.dynamic_update_slice(low_y, from_x[4:5], (4, 0, 0))
    high_y = lax.dynamic_update_slice(high_y, from_x[5:6], (4, 0, 0))
    from_high = grid_shift(low_y, 0, -1)
    from_low = grid_shift(high_y, 0, 1)
    far = lax.ppermute(
        part, ALL, torus_perm(lambda c, x, y, z: (c, x + (1 if c == 0 else -1), y, z))
    )
    far_other = shift(far, core=1)

    act, grad, keep, send = call(
        forward_kernel,
        [("s", meta), ("s", outs), ("s", ins), ("v", maps)]
        + [("a", v) for v in (blocks, from_x, from_low, from_high, weight, far, far_other)]
        + [("v", cotan.reshape(NB, ROWS, C))],
        [
            shape_of(NB, ROWS, C),
            shape_of(NB, ROWS, C),
            shape_of(16, K, 16, 128),
            shape_of(16, K, 16, 128),
        ],
        [
            pltpu.VMEM((EXT, ROWS, C), BF),
            pltpu.VMEM((K, C, C), BF),
            pltpu.VMEM((K, PAIRS * ROWS, C), BF),
            pltpu.VMEM((NB, ROWS, C), F32),
            pltpu.VMEM((NB, C, ROWS), BF),
            pltpu.SemaphoreType.DMA((9,)),
        ],
        pl.CostEstimate(flops=7_000_000_000, bytes_accessed=12_000_000, transcendentals=0),
    )
    got = shift(send, core=1)
    local, back_x, to_low, to_high = call(
        backward_kernel,
        [("s", meta), ("s", outs), ("s", ins), ("v", maps), ("v", grad)]
        + [("a", v) for v in (weight, far, far_other)],
        [shape_of(NB, ROWS, C, dtype=F32), six, five, five],
        [
            pltpu.VMEM((K, C, C), BF),
            pltpu.VMEM((EXT, ROWS, C), F32),
            pltpu.SemaphoreType.DMA((3,)),
        ],
        pl.CostEstimate(flops=5_000_000_000, bytes_accessed=10_000_000, transcendentals=0),
    )
    return_high = grid_shift(to_low, 0, -1)
    return_low = grid_shift(to_high, 0, 1)
    back_x = lax.dynamic_update_slice(back_x, return_low[4:5], (4, 0, 0))
    back_x = lax.dynamic_update_slice(back_x, return_high[4:5], (5, 0, 0))
    return_x = grid_shift(back_x, 1, 0)

    paired = call(
        pair_kernel,
        [("v", keep), ("v", got), ("a", to_low)],
        [shape_of(16, K, 16, 128)],
    )[0]
    spread = exchange(paired, lambda c, x, y, z: (c, z))
    sum_xy = jnp.sum(spread.astype(F32), 0)
    padded = jnp.concatenate([sum_xy, jnp.zeros((KPAD - K, 16, 128), F32)], 0)
    spread = exchange(padded.astype(BF).reshape(8, 4, 16, 128), lambda c, x, y, z: (c, x, y))
    sum_z = jnp.sum(spread.astype(F32), 0).astype(BF)
    all_z = exchange(jnp.broadcast_to(sum_z, (8, 4, 16, 128)), lambda c, x, y, z: (c, x, y))
    all_x = collect_ring(all_z, 2, "x", 2)
    mine = collect_ring(all_x, 4, "y")
    other = shift(mine, core=1)

    input_grad = call(
        input_kernel,
        [("s", meta), ("s", face), ("s", corner), ("v", local), ("v", return_x)]
        + [("v", v) for v in (return_low, return_high)],
        [shape_of(NB, ROWS, C)],
        [pltpu.VMEM((NB, ROWS, C), F32)],
    )[0]
    tiles = lax.axis_size("gx") * lax.axis_size("gy") * lax.axis_size("rep")
    scale = float((tiles * PAIRS * ROWS) ** (-0.5))
    weight_grad = call(
        functools.partial(final_kernel, scale),
        [("s", meta), ("v", mine), ("v", other)],
        [shape_of(K, C, 128, dtype=F32)],
    )[0]
    return act.reshape(-1, C), input_grad.reshape(-1, C), weight_grad


def solution(mesh):
    tiles = ("gx", "gy", "rep")
    in_specs = (
        P(tiles, None),
        P(None, None, "rep"),
        P(tiles, None),
        P(tiles, None, None),
        P(tiles, None, None),
        P(tiles, None, None),
        P(tiles, None, None),
        P(tiles, None, None, None),
    )
    out_specs = (P(tiles, None), P(tiles, None), P(None, None, "rep"))
    return jax.shard_map(body, mesh=mesh, in_specs=in_specs, out_specs=out_specs, check_vma=False)
```

time: 234 us -> 187 us (0.80)
  blocking collectives: 0 us -> 55.6 us
  waiting for transfers between devices: 90 us -> 41 us
  starting transfers between devices: 74.9 us -> 36.6 us
  Pallas kernels: 55.4 us -> 43.4 us
  other arithmetic: 3.45 us -> 0.44 us
    all_to_all x0 -> x3, blocking collectives: none -> 55.6 us  [exchange(): lax.all_to_all(value, ALL, split_axis=0, concat_axis=0, axis_index_groups...]
    ppermute x27 -> x7, waiting for transfers between devices: 52.9 us -> 6.43 us  [shift(): return lax.ppermute(value, ALL, torus_perm(move))]
    ppermute x27 -> x7, starting transfers between devices: 49.4 us -> 21.4 us  [shift(): return lax.ppermute(value, ALL, torus_perm(move))]
    pallas_call x5 -> x6, Pallas kernels: 55.4 us -> 43.4 us  [call(): pl.pallas_call(kernel, out_shape=[out for _, out in outs], in_specs=[plac...]
    ppermute x10 -> x6, starting transfers between devices: 22.1 us -> 11.8 us  [grid_shift(): return lax.ppermute(value, ALL, pairs)]
    ppermute x10 -> x6, waiting for transfers between devices: 27.1 us -> 24.3 us  [grid_shift(): return lax.ppermute(value, ALL, pairs)]
  transfers between devices with their start and end apart: 38 -> 14, of which waited for: 19 -> 8; matrix products, arithmetic and copies ran while one was open for 1% -> 1% of each run, Pallas kernels for 8% -> 8%
where the time goes in v2:
time: 187 us; the launch traced here: 186 us
  blocking collectives  55.6 us (30%)
  Pallas kernels  43.4 us (23%)
  waiting for transfers between devices  41 us (22%)
  starting transfers between devices  36.6 us (20%)
  local copies, waits for them, and re-layouts  8.08 us (4%)
    all_to_all x3, blocking collectives, exchange(): lax.all_to_all(value, ALL, split_axis=0, concat_axis=0, axis_index_groups...  55.6 us
    pallas_call x6, Pallas kernels, call(): pl.pallas_call(kernel, out_shape=[out for _, out in outs], in_specs=[plac...  43.4 us
    ppermute x6, waiting for transfers between devices, grid_shift(): return lax.ppermute(value, ALL, pairs)  24.3 us
    ppermute x7, starting transfers between devices, shift(): return lax.ppermute(value, ALL, torus_perm(move))  21.4 us
    ppermute x6, starting transfers between devices, grid_shift(): return lax.ppermute(value, ALL, pairs)  11.8 us
    ppermute x1, waiting for transfers between devices, body(): lax.ppermute(part, ALL, torus_perm(lambda c, x, y, z: (c, x + (1 if c ==...  10.3 us
    ppermute x7, waiting for transfers between devices, shift(): return lax.ppermute(value, ALL, torus_perm(move))  6.43 us
    unnamed x34, local copies, waits for them, and re-layouts  4.15 us
  transfers between devices with their start and end apart: 14, of which 8 were waited for; matrix products, arithmetic and copies ran while one was open for 1% of the time, Pallas kernels for 8%

profile of v2, /device:TPU:1, one launch (start us, length us, event | category | flops | bytes accessed | tf_op | source)
XLA Modules:
  0.0 186.0 jit_solution(13059254356014355348)
XLA Ops:
  0.7 1.3 reshape.36.face_ref
  2.0 0.7 stack.47.core_ref.meta
  2.7 3.5 %shard_map.103 = (bf16[6,128,256]{2,1,0:T(8,128)(2,1)}, bf16[5,128,256]{2,1,0:T(8,128)(2,1)}, bf16[5,128,256]{2,1,0:T(8,128)(2,1)}, bf16[27,128,128]{2,1,0:T(8,128)(2,1)}) custom-call(s32[5]{0:T(128)} %stack.47.core_ref.meta, s32[16]{0:T(128)} %reshape.36.face_ref, s32[4]{0:T(128)} %bitcast.28, bf16[8,128,256]{2,1,0:T(8,128)(2,1)} %bitcast.21, ...), custom_call_target="tpu_custom_call" | custom-call | tf_op jit(solution)/shard_map/pallas_call | solution.py:27
  6.1 3.4 %collective-permute-start.3 = (bf16[27,128,128]{2,1,0:T(8,128)(2,1)}, bf16[27,128,128]{2,1,0:T(8,128)(2,1)S(1)}, u32[]{:S(2)}, u32[]{:S(2)}) collective-permute-start(bf16[27,128,128]{2,1,0:T(8,128)(2,1)} %get-tuple-element.18), channel_id=1, source_target_pairs={{0,1},{1,2},{2,3},{3,0},{4,5},{5,6},{6,7},{7,4},{8,9},{9,10},{10,1... | collective-permute-start | bytes 2654216 | tf_op jit(solution)/shard_map/ppermute | solution.py:308
  9.5 0.0 collective-permute-start
  9.6 10.3 %collective-permute-done.3.far = bf16[27,128,128]{2,1,0:T(8,128)(2,1)S(1)} collective-permute-done((bf16[27,128,128]{2,1,0:T(8,128)(2,1)}, bf16[27,128,128]{2,1,0:T(8,128)(2,1)S(1)}, u32[]{:S(2)}, u32[]{:S(2)}) %collective-permute-start.3) | collective-permute-done | bytes 884768 | tf_op jit(solution)/shard_map/ppermute | solution.py:308
  19.8 4.1 %collective-permute-start.4 = (bf16[27,128,128]{2,1,0:T(8,128)(2,1)S(1)}, bf16[27,128,128]{2,1,0:T(8,128)(2,1)S(1)}, u32[]{:S(2)}, u32[]{:S(2)}) collective-permute-start(bf16[27,128,128]{2,1,0:T(8,128)(2,1)S(1)} %collective-permute-done.3.far), channel_id=1, source_target_pairs={{0,128},{1,129},{2,130},{3,131},{4,132},{5,133},{6,134},{7,135},{8... | collective-permute-start | bytes 2654216 | tf_op jit(solution)/shard_map/ppermute | solution.py:61
  23.9 0.7 slice_dynamic-update-slice_fusion.2
  24.6 1.3 collective-permute-start.2
  25.9 5.5 %collective-permute-start.1 = (bf16[5,128,256]{2,1,0:T(8,128)(2,1)}, bf16[5,128,256]{2,1,0:T(8,128)(2,1)S(1)}, u32[]{:S(2)}, u32[]{:S(2)}) collective-permute-start(bf16[5,128,256]{2,1,0:T(8,128)(2,1)} %get-tuple-element.28), channel_id=1, source_target_pairs={{0,2},{1,3},{2,4},{3,5},{4,6},{5,7},{6,8},{7,9},{8,10},{9,11},{10,... | collective-permute-start | bytes 983048 | tf_op jit(solution)/shard_map/ppermute | solution.py:72
  31.4 0.1 copy.15
  31.5 0.6 reshape.33.outs
  32.2 0.1 copy.16
  32.3 0.6 reshape.34.ins
  32.9 4.6 %collective-permute-done.2.from_high = bf16[5,128,256]{2,1,0:T(8,128)(2,1)S(1)} collective-permute-done((bf16[5,128,256]{2,1,0:T(8,128)(2,1)}, bf16[5,128,256]{2,1,0:T(8,128)(2,1)S(1)}, u32[]{:S(2)}, u32[]{:S(2)}) %collective-permute-start.2) | collective-permute-done | bytes 327712 | tf_op jit(solution)/shard_map/ppermute | solution.py:72
  37.5 6.9 %collective-permute-done.1.from_low = bf16[5,128,256]{2,1,0:T(8,128)(2,1)S(1)} collective-permute-done((bf16[5,128,256]{2,1,0:T(8,128)(2,1)}, bf16[5,128,256]{2,1,0:T(8,128)(2,1)S(1)}, u32[]{:S(2)}, u32[]{:S(2)}) %collective-permute-start.1) | collective-permute-done | bytes 327712 | tf_op jit(solution)/shard_map/ppermute | solution.py:72
  44.5 0.0 collective-permute-done.4.far_other
  44.5 0.7 copy-done.15
  45.2 0.3 copy-done.11
  45.5 17.3 %shard_map.104 = (bf16[8,128,256]{2,1,0:T(8,128)(2,1)}, bf16[8,128,256]{2,1,0:T(8,128)(2,1)}, bf16[16,27,16,128]{3,2,1,0:T(8,128)(2,1)}, bf16[16,27,16,128]{3,2,1,0:T(8,128)(2,1)}) custom-call(s32[5]{0:T(128)} %stack.47.core_ref.meta, s32[108]{0:T(128)} %reshape.33.outs, s32[108]{0:T(128)} %reshape.34.ins, s32[27,4,128]{2,1,0:T(4,128)} %bitcast.31, ...), custom_call_target="tpu_custom_call" | custom-call | flops 7000000000 | bytes 12000000 | tf_op jit(solution)/shard_map/pallas_call | solution.py:27
  62.8 0.6 collective-permute-start.8
  63.3 11.5 %shard_map.105 = (f32[8,128,256]{2,1,0:T(8,128)}, bf16[6,128,256]{2,1,0:T(8,128)(2,1)}, bf16[5,128,256]{2,1,0:T(8,128)(2,1)}, bf16[5,128,256]{2,1,0:T(8,128)(2,1)}) custom-call(s32[5]{0:T(128)} %stack.47.core_ref.meta, s32[108]{0:T(128)} %reshape.33.outs, s32[108]{0:T(128)} %reshape.34.ins, s32[27,4,128]{2,1,0:T(4,128)} %bitcast.32, ...), custom_call_target="tpu_custom_call" | custom-call | flops 5000000000 | bytes 10000000 | tf_op jit(solution)/shard_map/pallas_call | solution.py:27
  74.8 0.0 collective-permute-done.8.got
  74.8 1.2 copy-done.1
  76.0 3.7 %shard_map.107 = bf16[16,27,16,128]{3,2,1,0:T(8,128)(2,1)} custom-call(bf16[16,27,16,128]{3,2,1,0:T(8,128)(2,1)} %get-tuple-element.25.keep, bf16[16,27,16,128]{3,2,1,0:T(8,128)(2,1)} %copy-done.1, bf16[5,128,256]{2,1,0:T(8,128)(2,1)} %get-tuple-element.24.after), custom_call_target="tpu_custom_call" | custom-call | tf_op jit(solution)/shard_map/pallas_call | solution.py:27
  79.7 29.1 %all_to_all.15 = bf16[16,27,16,128]{3,2,1,0:T(8,128)(2,1)S(1)} all-to-all(bf16[16,27,16,128]{3,2,1,0:T(8,128)(2,1)} %shard_map.107), channel_id=1, replica_groups={{0,2,1,3,4,6,5,7,8,10,9,11,12,14,13,15},{128,130,129,131,132,134,133,13..., dimensions={0} | all-to-all | bytes 3538944 | tf_op jit(solution)/shard_map/all_to_all | solution.py:273
  108.8 0.2 reduce.1
  109.1 16.0 %all_to_all.16 = bf16[8,4,16,128]{3,2,1,0:T(8,128)(2,1)S(1)} all-to-all(bf16[8,4,16,128]{3,2,1,0:T(8,128)(2,1)S(1)} %bitcast.19), channel_id=1, replica_groups={{0,16,32,48,64,80,96,112},{128,144,160,176,192,208,224,240},{2,18,34,50..., dimensions={0} | all-to-all | bytes 262144 | tf_op jit(solution)/shard_map/all_to_all | solution.py:273
  125.1 10.5 %all_to_all.17 = bf16[8,4,16,128]{3,2,1,0:T(8,128)(2,1)S(1)} all-to-all(bf16[8,4,16,128]{3,2,1,0:T(8,128)(2,1)S(1)} %broadcast_in_dim.4), channel_id=1, replica_groups={{0,16,32,48,64,80,96,112},{128,144,160,176,192,208,224,240},{2,18,34,50..., dimensions={0} | all-to-all | bytes 262144 | tf_op jit(solution)/shard_map/all_to_all | solution.py:273
  135.6 1.7 collective-permute-start.9
  137.3 3.6 %collective-permute-done.9 = bf16[8,4,16,128]{3,2,1,0:T(8,128)(2,1)S(1)} collective-permute-done((bf16[8,4,16,128]{3,2,1,0:T(8,128)(2,1)S(1)}, bf16[8,4,16,128]{3,2,1,0:T(8,128)(2,1)S(1)}, u32[]{:S(2)}, u32[]{:S(2)}) %collective-permute-start.9) | collective-permute-done | bytes 131104 | tf_op jit(solution)/shard_map/ppermute | solution.py:61
  141.0 1.3 collective-permute-start.11
  142.3 0.1 collective-permute-start.10
  142.5 2.5 %collective-permute-start.12 = (bf16[2,8,4,16,128]{4,3,2,1,0:T(8,128)(2,1)S(1)}, bf16[2,8,4,16,128]{4,3,2,1,0:T(8,128)(2,1)S(1)}, u32[]{:S(2)}, u32[]{:S(2)}) collective-permute-start(bf16[2,8,4,16,128]{4,3,2,1,0:T(8,128)(2,1)S(1)} %get-tuple-element.30), channel_id=1, source_target_pairs={{0,12},{1,13},{2,14},{3,15},{4,0},{5,1},{6,2},{7,3},{8,4},{9,5},{1... | collective-permute-start | bytes 786440 | tf_op jit(solution)/shard_map/ppermute | solution.py:61
  145.0 2.8 %collective-permute-start.5 = (bf16[5,128,256]{2,1,0:T(8,128)(2,1)S(1)}, bf16[5,128,256]{2,1,0:T(8,128)(2,1)S(1)}, u32[]{:S(2)}, u32[]{:S(2)}) collective-permute-start(bf16[5,128,256]{2,1,0:T(8,128)(2,1)S(1)} %copy-done.13), channel_id=1, source_target_pairs={{0,2},{1,3},{2,4},{3,5},{4,6},{5,7},{6,8},{7,9},{8,10},{9,11},{10,... | collective-permute-start | bytes 983048 | tf_op jit(solution)/shard_map/ppermute | solution.py:72
  147.8 0.1 collective-permute-done.11
  147.9 2.7 %collective-permute-done.10 = bf16[2,8,4,16,128]{4,3,2,1,0:T(8,128)(2,1)S(1)} collective-permute-done((bf16[2,8,4,16,128]{4,3,2,1,0:T(8,128)(2,1)S(1)}, bf16[2,8,4,16,128]{4,3,2,1,0:T(8,128)(2,1)S(1)}, u32[]{:S(2)}, u32[]{:S(2)}) %collective-permute-start.10) | collective-permute-done | bytes 262176 | tf_op jit(solution)/shard_map/ppermute | solution.py:61
  150.6 0.0 collective-permute-done.12
  150.6 0.1 pad_maximum_fusion.mine
  150.8 11.0 %collective-permute-start.13 = (bf16[4,2,8,4,16,128]{5,4,3,2,1,0:T(8,128)(2,1)S(1)}, bf16[4,2,8,4,16,128]{5,4,3,2,1,0:T(8,128)(2,1)S(1)}, u32[]{:S(2)}, u32[]{:S(2)}) collective-permute-start(bf16[4,2,8,4,16,128]{5,4,3,2,1,0:T(8,128)(2,1)S(1)} %pad_maximum_fusion.mine), channel_id=1, source_target_pairs={{0,128},{1,129},{2,130},{3,131},{4,132},{5,133},{6,134},{7,135},{8... | collective-permute-start | bytes 3145736 | tf_op jit(solution)/shard_map/ppermute | solution.py:61
  161.8 1.3 collective-permute-start.6
  163.2 11.4 %collective-permute-done.6.from_high = bf16[5,128,256]{2,1,0:T(8,128)(2,1)S(1)} collective-permute-done((bf16[5,128,256]{2,1,0:T(8,128)(2,1)S(1)}, bf16[5,128,256]{2,1,0:T(8,128)(2,1)S(1)}, u32[]{:S(2)}, u32[]{:S(2)}) %collective-permute-start.6) | collective-permute-done | bytes 327712 | tf_op jit(solution)/shard_map/ppermute | solution.py:72
  174.5 0.9 collective-permute-start.7
  175.4 1.3 collective-permute-done.7.from_x
  176.8 0.7 copy-done.5
  177.5 2.6 %shard_map.106 = bf16[8,128,256]{2,1,0:T(8,128)(2,1)} custom-call(s32[5]{0:T(128)} %stack.47.core_ref.meta, s32[16]{0:T(128)} %reshape.36.face_ref, s32[4]{0:T(128)} %bitcast.29, f32[8,128,256]{2,1,0:T(8,128)} %get-tuple-element.21.local, bf16[6,128,256]{2,1,0:T(8,128)(2,1)} %copy-done.5, bf16[5,128,256]{2,1,0:T(8,128)(2,1)} %copy-done.3, ...), custom_call_target="tpu_custom_call" | custom-call | tf_op jit(solution)/shard_map/pallas_call | solution.py:27
  180.1 0.9 copy-done.2
  181.1 4.9 %shard_map.108 = f32[27,256,128]{2,1,0:T(8,128)} custom-call(s32[5]{0:T(128)} %stack.47.core_ref.meta, bf16[4,2,8,4,16,128]{5,4,3,2,1,0:T(8,128)(2,1)} %copy-done, bf16[4,2,8,4,16,128]{5,4,3,2,1,0:T(8,128)(2,1)} %copy-done.2), custom_call_target="tpu_custom_call" | custom-call | tf_op jit(solution)/shard_map/pallas_call | solution.py:27
  (36 shorter events, 0.2 us)
Async XLA Ops:
  0.6 30.8 %copy-start.8 = (s32[1,27,4]{1,2,0:T(4,128)S(1)}, s32[1,27,4]{1,2,0:T(4,128)}, u32[]{:S(2)}) copy-start(s32[1,27,4]{1,2,0:T(4,128)} %param.13) | copy-start | bytes 1300
  0.6 31.5 %copy-start.9 = (s32[1,27,4]{1,2,0:T(4,128)S(1)}, s32[1,27,4]{1,2,0:T(4,128)}, u32[]{:S(2)}) copy-start(s32[1,27,4]{1,2,0:T(4,128)} %param.14) | copy-start | bytes 1300
  6.1 13.7 %collective-permute-start.3 = (bf16[27,128,128]{2,1,0:T(8,128)(2,1)}, bf16[27,128,128]{2,1,0:T(8,128)(2,1)S(1)}, u32[]{:S(2)}, u32[]{:S(2)}) collective-permute-start(bf16[27,128,128]{2,1,0:T(8,128)(2,1)} %get-tuple-element.18), channel_id=1, source_target_pairs={{0,1},{1,2},{2,3},{3,0},{4,5},{5,6},{6,7},{7,4},{8,9},{9,10},{10,1... | collective-permute-start | bytes 2654216 | tf_op jit(solution)/shard_map/ppermute | solution.py:308
  9.5 14.4 %collective-permute-start = (bf16[6,128,256]{2,1,0:T(8,128)(2,1)}, bf16[6,128,256]{2,1,0:T(8,128)(2,1)S(1)}, u32[]{:S(2)}, u32[]{:S(2)}) collective-permute-start(bf16[6,128,256]{2,1,0:T(8,128)(2,1)} %get-tuple-element.15), channel_id=1, source_target_pairs={{0,128},{1,129},{2,130},{3,131},{4,132},{5,133},{6,134},{7,135},{8... | collective-permute-start | bytes 1179656 | tf_op jit(solution)/shard_map/ppermute | solution.py:72
  19.8 24.6 %copy-start.10 = (bf16[27,128,128]{2,1,0:T(8,128)(2,1)}, bf16[27,128,128]{2,1,0:T(8,128)(2,1)S(1)}, u32[]{:S(2)}) copy-start(bf16[27,128,128]{2,1,0:T(8,128)(2,1)S(1)} %collective-permute-done.3.far) | copy-start | bytes 2654212
  19.8 24.6 %collective-permute-start.4 = (bf16[27,128,128]{2,1,0:T(8,128)(2,1)S(1)}, bf16[27,128,128]{2,1,0:T(8,128)(2,1)S(1)}, u32[]{:S(2)}, u32[]{:S(2)}) collective-permute-start(bf16[27,128,128]{2,1,0:T(8,128)(2,1)S(1)} %collective-permute-done.3.far), channel_id=1, source_target_pairs={{0,128},{1,129},{2,130},{3,131},{4,132},{5,133},{6,134},{7,135},{8... | collective-permute-start | bytes 2654216 | tf_op jit(solution)/shard_map/ppermute | solution.py:61
  23.9 20.5 %copy-start.7 = (bf16[6,128,256]{2,1,0:T(8,128)(2,1)}, bf16[6,128,256]{2,1,0:T(8,128)(2,1)S(1)}, u32[]{:S(2)}) copy-start(bf16[6,128,256]{2,1,0:T(8,128)(2,1)S(1)} %collective-permute-done.from_x) | copy-start | bytes 1179652
  24.6 12.9 %collective-permute-start.2 = (bf16[5,128,256]{2,1,0:T(8,128)(2,1)}, bf16[5,128,256]{2,1,0:T(8,128)(2,1)S(1)}, u32[]{:S(2)}, u32[]{:S(2)}) collective-permute-start(bf16[5,128,256]{2,1,0:T(8,128)(2,1)} %get-tuple-element.27), channel_id=1, source_target_pairs={{2,0},{3,1},{4,2},{5,3},{6,4},{7,5},{8,6},{9,7},{10,8},{11,9},{12,... | collective-permute-start | bytes 983048 | tf_op jit(solution)/shard_map/ppermute | solution.py:72
  25.9 18.5 %collective-permute-start.1 = (bf16[5,128,256]{2,1,0:T(8,128)(2,1)}, bf16[5,128,256]{2,1,0:T(8,128)(2,1)S(1)}, u32[]{:S(2)}, u32[]{:S(2)}) collective-permute-start(bf16[5,128,256]{2,1,0:T(8,128)(2,1)} %get-tuple-element.28), channel_id=1, source_target_pairs={{0,2},{1,3},{2,4},{3,5},{4,6},{5,7},{6,8},{7,9},{8,10},{9,11},{10,... | collective-permute-start | bytes 983048 | tf_op jit(solution)/shard_map/ppermute | solution.py:72
  37.5 7.0 %copy-start.14 = (bf16[5,128,256]{2,1,0:T(8,128)(2,1)}, bf16[5,128,256]{2,1,0:T(8,128)(2,1)S(1)}, u32[]{:S(2)}) copy-start(bf16[5,128,256]{2,1,0:T(8,128)(2,1)S(1)} %collective-permute-done.2.from_high) | copy-start | bytes 983044
  44.5 0.7 copy-start.15
  44.5 1.0 copy-start.11
  62.8 12.0 %collective-permute-start.8 = (bf16[16,27,16,128]{3,2,1,0:T(8,128)(2,1)}, bf16[16,27,16,128]{3,2,1,0:T(8,128)(2,1)S(1)}, u32[]{:S(2)}, u32[]{:S(2)}) collective-permute-start(bf16[16,27,16,128]{3,2,1,0:T(8,128)(2,1)} %get-tuple-element.26), channel_id=1, source_target_pairs={{0,128},{1,129},{2,130},{3,131},{4,132},{5,133},{6,134},{7,135},{8... | collective-permute-start | bytes 5308424 | tf_op jit(solution)/shard_map/ppermute | solution.py:61
  74.8 1.2 copy-start.1
  108.8 36.2 %copy-start.13 = (bf16[5,128,256]{2,1,0:T(8,128)(2,1)S(1)}, bf16[5,128,256]{2,1,0:T(8,128)(2,1)}, u32[]{:S(2)}) copy-start(bf16[5,128,256]{2,1,0:T(8,128)(2,1)} %get-tuple-element.23) | copy-start | bytes 983044
  125.0 36.8 %copy-start.6 = (bf16[5,128,256]{2,1,0:T(8,128)(2,1)S(1)}, bf16[5,128,256]{2,1,0:T(8,128)(2,1)}, u32[]{:S(2)}) copy-start(bf16[5,128,256]{2,1,0:T(8,128)(2,1)} %get-tuple-element.24.after) | copy-start | bytes 983044
  125.0 38.1 %copy-start.12 = (bf16[6,128,256]{2,1,0:T(8,128)(2,1)S(1)}, bf16[6,128,256]{2,1,0:T(8,128)(2,1)}, u32[]{:S(2)}) copy-start(bf16[6,128,256]{2,1,0:T(8,128)(2,1)} %get-tuple-element.22) | copy-start | bytes 1179652
  135.6 5.3 %collective-permute-start.9 = (bf16[8,4,16,128]{3,2,1,0:T(8,128)(2,1)S(1)}, bf16[8,4,16,128]{3,2,1,0:T(8,128)(2,1)S(1)}, u32[]{:S(2)}, u32[]{:S(2)}) collective-permute-start(bf16[8,4,16,128]{3,2,1,0:T(8,128)(2,1)S(1)} %all_to_all.17), channel_id=1, source_target_pairs={{0,2},{1,3},{2,0},{3,1},{4,6},{5,7},{6,4},{7,5},{8,10},{9,11},{10,... | collective-permute-start | bytes 393224 | tf_op jit(solution)/shard_map/ppermute | solution.py:61
  141.0 6.9 %collective-permute-start.11 = (bf16[2,8,4,16,128]{4,3,2,1,0:T(8,128)(2,1)S(1)}, bf16[2,8,4,16,128]{4,3,2,1,0:T(8,128)(2,1)S(1)}, u32[]{:S(2)}, u32[]{:S(2)}) collective-permute-start(bf16[2,8,4,16,128]{4,3,2,1,0:T(8,128)(2,1)S(1)} %get-tuple-element.30), channel_id=1, source_target_pairs={{0,8},{1,9},{2,10},{3,11},{4,12},{5,13},{6,14},{7,15},{8,0},{9,1},... | collective-permute-start | bytes 786440 | tf_op jit(solution)/shard_map/ppermute | solution.py:61
  142.3 8.3 %collective-permute-start.10 = (bf16[2,8,4,16,128]{4,3,2,1,0:T(8,128)(2,1)S(1)}, bf16[2,8,4,16,128]{4,3,2,1,0:T(8,128)(2,1)S(1)}, u32[]{:S(2)}, u32[]{:S(2)}) collective-permute-start(bf16[2,8,4,16,128]{4,3,2,1,0:T(8,128)(2,1)S(1)} %get-tuple-element.30), channel_id=1, source_target_pairs={{0,4},{1,5},{2,6},{3,7},{4,8},{5,9},{6,10},{7,11},{8,12},{9,13},{1... | collective-permute-start | bytes 786440 | tf_op jit(solution)/shard_map/ppermute | solution.py:61
  142.5 8.2 %collective-permute-start.12 = (bf16[2,8,4,16,128]{4,3,2,1,0:T(8,128)(2,1)S(1)}, bf16[2,8,4,16,128]{4,3,2,1,0:T(8,128)(2,1)S(1)}, u32[]{:S(2)}, u32[]{:S(2)}) collective-permute-start(bf16[2,8,4,16,128]{4,3,2,1,0:T(8,128)(2,1)S(1)} %get-tuple-element.30), channel_id=1, source_target_pairs={{0,12},{1,13},{2,14},{3,15},{4,0},{5,1},{6,2},{7,3},{8,4},{9,5},{1... | collective-permute-start | bytes 786440 | tf_op jit(solution)/shard_map/ppermute | solution.py:61
  145.0 18.1 %collective-permute-start.5 = (bf16[5,128,256]{2,1,0:T(8,128)(2,1)S(1)}, bf16[5,128,256]{2,1,0:T(8,128)(2,1)S(1)}, u32[]{:S(2)}, u32[]{:S(2)}) collective-permute-start(bf16[5,128,256]{2,1,0:T(8,128)(2,1)S(1)} %copy-done.13), channel_id=1, source_target_pairs={{0,2},{1,3},{2,4},{3,5},{4,6},{5,7},{6,8},{7,9},{8,10},{9,11},{10,... | collective-permute-start | bytes 983048 | tf_op jit(solution)/shard_map/ppermute | solution.py:72
  150.8 29.4 %copy-start = (bf16[4,2,8,4,16,128]{5,4,3,2,1,0:T(8,128)(2,1)}, bf16[4,2,8,4,16,128]{5,4,3,2,1,0:T(8,128)(2,1)S(1)}, u32[]{:S(2)}) copy-start(bf16[4,2,8,4,16,128]{5,4,3,2,1,0:T(8,128)(2,1)S(1)} %pad_maximum_fusion.mine) | copy-start | bytes 3145732
  150.8 29.3 %collective-permute-start.13 = (bf16[4,2,8,4,16,128]{5,4,3,2,1,0:T(8,128)(2,1)S(1)}, bf16[4,2,8,4,16,128]{5,4,3,2,1,0:T(8,128)(2,1)S(1)}, u32[]{:S(2)}, u32[]{:S(2)}) collective-permute-start(bf16[4,2,8,4,16,128]{5,4,3,2,1,0:T(8,128)(2,1)S(1)} %pad_maximum_fusion.mine), channel_id=1, source_target_pairs={{0,128},{1,129},{2,130},{3,131},{4,132},{5,133},{6,134},{7,135},{8... | collective-permute-start | bytes 3145736 | tf_op jit(solution)/shard_map/ppermute | solution.py:61
  161.8 12.7 %collective-permute-start.6 = (bf16[5,128,256]{2,1,0:T(8,128)(2,1)S(1)}, bf16[5,128,256]{2,1,0:T(8,128)(2,1)S(1)}, u32[]{:S(2)}, u32[]{:S(2)}) collective-permute-start(bf16[5,128,256]{2,1,0:T(8,128)(2,1)S(1)} %copy-done.6), channel_id=1, source_target_pairs={{2,0},{3,1},{4,2},{5,3},{6,4},{7,5},{8,6},{9,7},{10,8},{11,9},{12,... | collective-permute-start | bytes 983048 | tf_op jit(solution)/shard_map/ppermute | solution.py:72
  163.1 13.7 %copy-start.3 = (bf16[5,128,256]{2,1,0:T(8,128)(2,1)}, bf16[5,128,256]{2,1,0:T(8,128)(2,1)S(1)}, u32[]{:S(2)}) copy-start(bf16[5,128,256]{2,1,0:T(8,128)(2,1)S(1)} %collective-permute-done.5.from_low) | copy-start | bytes 983044
  174.5 2.3 %copy-start.4 = (bf16[5,128,256]{2,1,0:T(8,128)(2,1)}, bf16[5,128,256]{2,1,0:T(8,128)(2,1)S(1)}, u32[]{:S(2)}) copy-start(bf16[5,128,256]{2,1,0:T(8,128)(2,1)S(1)} %collective-permute-done.6.from_high) | copy-start | bytes 983044
  174.5 2.3 %collective-permute-start.7 = (bf16[6,128,256]{2,1,0:T(8,128)(2,1)S(1)}, bf16[6,128,256]{2,1,0:T(8,128)(2,1)S(1)}, u32[]{:S(2)}, u32[]{:S(2)}) collective-permute-start(bf16[6,128,256]{2,1,0:T(8,128)(2,1)S(1)} %slice_dynamic-update-slice_fusion), channel_id=1, source_target_pairs={{0,128},{1,129},{2,130},{3,131},{4,132},{5,133},{6,134},{7,135},{8... | collective-permute-start | bytes 1179656 | tf_op jit(solution)/shard_map/ppermute | solution.py:72
  176.8 0.7 copy-start.5
  180.1 1.0 copy-start.2

commit v3 on v2

v3 whole, which is shorter than its diff:
```python
import functools

import jax
import jax.numpy as jnp
from jax import lax
from jax.experimental import pallas as pl
from jax.experimental.pallas import tpu as pltpu
from jax.sharding import PartitionSpec as P

ALL = ("gx", "gy", "rep")
K, C, NB, ROWS, PAIRS = 27, 256, 8, 128, 4
EXT = 29
KPAD = 32
BF, F32 = jnp.bfloat16, jnp.float32
VM = pl.BlockSpec(memory_space=pltpu.VMEM)
SM = pl.BlockSpec(memory_space=pltpu.SMEM)
PARAMS = pltpu.CompilerParams(vmem_limit_bytes=26 * 1024 * 1024)


def shape_of(*dims, dtype=BF):
    return jax.ShapeDtypeStruct(dims, dtype)


def call(kernel, ins, outs, scratch=(), cost=None):
    place = {"s": SM, "v": VM, "a": pl.BlockSpec(memory_space=pl.ANY)}
    outs = [out if isinstance(out, tuple) else ("v", out) for out in outs]
    return pl.pallas_call(
        kernel,
        out_shape=[out for _, out in outs],
        in_specs=[place[kind] for kind, _ in ins],
        out_specs=[place[kind] for kind, _ in outs],
        scratch_shapes=list(scratch),
        compiler_params=PARAMS,
        cost_estimate=cost,
    )(*[value for _, value in ins])


def tie(value, *after):
    return lax.optimization_barrier((value, *after))[0]


def places():
    gy = lax.axis_index("gy")
    return lax.axis_index("gx"), lax.axis_index("rep"), gy % 2, gy // 2 % 4, gy // 8


def flat_id(core, x, y, z):
    return (core * 64 + ((z % 8) * 4 + y % 4) * 2 + (x % 4) // 2) * 2 + x % 2


def torus_perm(move):
    pairs = []
    for core in range(2):
        for z in range(8):
            for y in range(4):
                for x in range(4):
                    pairs.append((flat_id(core, x, y, z), flat_id(*move(core, x, y, z))))
    return pairs


def shift(value, **by):
    def move(core, x, y, z):
        return (
            (core + by.get("core", 0)) % 2,
            x + by.get("x", 0),
            y + by.get("y", 0),
            z + by.get("z", 0),
        )

    return lax.ppermute(value, ALL, torus_perm(move))


def grid_shift(value, step_x, step_y):
    pairs = []
    for i in range(2):
        for j in range(64):
            if 0 <= j + step_y < 64:
                for r in range(2):
                    to = ((i + step_x) % 2 * 64 + j + step_y) * 2 + r
                    pairs.append(((i * 64 + j) * 2 + r, to))
    return lax.ppermute(value, ALL, pairs)


def pick_kernel(face, corner, feats, face_x, low_y, high_y):
    i = lax.axis_index("gx")
    for n in range(4):
        face_x[n] = feats[face[0, 1 - i, n]]
        low_y[n] = feats[face[0, 2, n]]
        high_y[n] = feats[face[0, 3, n]]
    for n in range(2):
        face_x[4 + n] = feats[corner[0, 0, 2 * (1 - i) + n]]
    low_y[4] = face_x[4]
    high_y[4] = face_x[5]


def weight_copies(core, side, own, far, far_other, full, sems):
    near_rows = pl.ds(pl.multiple_of(core * 128, 128), 128)
    other_rows = pl.ds(pl.multiple_of((1 - core) * 128, 128), 128)
    mine = slice(side * 128, side * 128 + 128)
    theirs = slice(128 - side * 128, 256 - side * 128)
    return (
        pltpu.make_async_copy(own, full.at[:, :, mine], sems.at[0]),
        pltpu.make_async_copy(far, full.at[:, near_rows, theirs], sems.at[1]),
        pltpu.make_async_copy(far_other, full.at[:, other_rows, theirs], sems.at[2]),
    )


def on_weights(act, core, rep, *refs):
    for side in range(2):

        @pl.when(rep == side)
        def _():
            for copy in weight_copies(core, side, *refs):
                getattr(copy, act)()


def forward_kernel(
    outs, ins, maps, feats, from_x, from_low, from_high, own, far, far_other, cotan,
    act, grad, keep, send,
    ext, full, rows, acc, flipped, sems,
):
    core, rep = places()[:2]
    weights = (own, far, far_other, full, sems)
    on_weights("start", core, rep, *weights)
    ext[8:16] = jnp.zeros((8, ROWS, C), BF)
    ext[24:29] = jnp.zeros((5, ROWS, C), BF)
    copies = [
        pltpu.make_async_copy(feats, ext.at[0:8], sems.at[3]),
        pltpu.make_async_copy(from_x.at[0:4], ext.at[pl.ds(8 + 4 * (1 - core), 4)], sems.at[4]),
        pltpu.make_async_copy(from_low.at[0:4], ext.at[16:20], sems.at[5]),
        pltpu.make_async_copy(from_high.at[0:4], ext.at[20:24], sems.at[6]),
        pltpu.make_async_copy(from_low.at[4], ext.at[24 + 2 * (1 - core)], sems.at[7]),
        pltpu.make_async_copy(from_high.at[4], ext.at[25 + 2 * (1 - core)], sems.at[8]),
    ]
    for copy in copies:
        copy.start()
    acc[...] = jnp.zeros_like(acc)
    lanes = lax.broadcasted_iota(jnp.int32, (ROWS, ROWS), 0)
    for copy in copies:
        copy.wait()

    def gather_step(k, carry):
        map_k = maps[k]
        for p in range(PAIRS):
            hot = (lanes == map_k[p : p + 1, :]).astype(F32).astype(BF)
            picked = lax.dot_general(
                hot, ext[ins[0, p, k]], (((0,), (0,)), ((), ())), preferred_element_type=F32
            )
            rows[k, p * ROWS : (p + 1) * ROWS, :] = picked.astype(BF)
        return carry

    lax.fori_loop(0, K, gather_step, 0, unroll=27)
    on_weights("wait", core, rep, *weights)

    def product_step(k, carry):
        product = jnp.dot(rows[k], full[k], preferred_element_type=F32)
        for p in range(PAIRS):
            acc[outs[0, p, k]] += product[p * ROWS : (p + 1) * ROWS]
        return carry

    lax.fori_loop(0, K, product_step, 0, unroll=27)

    def grad_step(b, carry):
        value = acc[b]
        sigma = 1.0 / (1.0 + jnp.exp(-value))
        act[b] = (value * sigma).astype(BF)
        up = cotan[b].astype(F32) * (sigma * (1.0 + value * (1.0 - sigma)))
        grad[b] = up.astype(BF)
        flipped[b] = up.T.astype(BF)
        return carry

    lax.fori_loop(0, NB, grad_step, 0, unroll=4)

    def weight_step(k, carry):
        left = jnp.concatenate([flipped[outs[0, p, k]] for p in range(PAIRS)], axis=1)
        part = jnp.dot(left, rows[k], preferred_element_type=F32)
        for side in range(2):
            first = part[side * 128 : side * 128 + 64]
            second = part[side * 128 + 64 : side * 128 + 128]
            kept = jnp.where(core == 0, first, second).astype(BF)
            sent = jnp.where(core == 0, second, first).astype(BF)
            for y in range(4):
                for x in range(2):
                    at = (slice(y * 16, y * 16 + 16), slice(x * 128, x * 128 + 128))
                    keep[y * 4 + side * 2 + x, k] = kept[at]
                    send[y * 4 + side * 2 + x, k] = sent[at]
        return carry

    lax.fori_loop(0, K, weight_step, 0, unroll=27)


def backward_kernel(
    outs, ins, maps, grad, own, far, far_other,
    local, face_x, to_low, to_high,
    full, rows, acc, sems,
):
    core, rep = places()[:2]
    weights = (own, far, far_other, full, sems)
    on_weights("start", core, rep, *weights)
    acc[...] = jnp.zeros_like(acc)
    lanes = lax.broadcasted_iota(jnp.int32, (ROWS, ROWS), 0)

    def spread_step(k, carry):
        map_k = maps[k]
        for p in range(PAIRS):
            hot = (lanes == map_k[p : p + 1, :]).astype(F32).astype(BF)
            spread = jnp.dot(hot, grad[outs[0, p, k]], preferred_element_type=F32)
            rows[k, p * ROWS : (p + 1) * ROWS, :] = spread.astype(BF)
        return carry

    lax.fori_loop(0, K, spread_step, 0, unroll=27)
    on_weights("wait", core, rep, *weights)

    def step(k, carry):
        product = lax.dot_general(
            rows[k], full[k], (((1,), (1,)), ((), ())), preferred_element_type=F32
        )
        for p in range(PAIRS):
            acc[ins[0, p, k]] += product[p * ROWS : (p + 1) * ROWS]
        return carry

    lax.fori_loop(0, K, step, 0, unroll=27)
    local[...] = acc[0:8]
    face_x[0:4] = acc[pl.ds(8 + 4 * (1 - core), 4)].astype(BF)
    face_x[4:6] = jnp.zeros((2, ROWS, C), BF)
    to_low[0:4] = acc[16:20].astype(BF)
    to_low[4] = acc[24 + 2 * (1 - core)].astype(BF)
    to_high[0:4] = acc[20:24].astype(BF)
    to_high[4] = acc[25 + 2 * (1 - core)].astype(BF)


def input_kernel(face, corner, local, from_x, from_low, from_high, out, acc):
    i = lax.axis_index("gx")
    acc[...] = local[...]
    for n in range(4):
        acc[face[0, 1 - i, n]] += from_x[n].astype(F32)
        acc[face[0, 2, n]] += from_low[n].astype(F32)
        acc[face[0, 3, n]] += from_high[n].astype(F32)
    for n in range(2):
        acc[corner[0, 0, 2 * (1 - i) + n]] += from_x[4 + n].astype(F32)
    out[...] = acc[...].astype(BF)


def final_kernel(scale, *refs):
    core, _, _, y_at, _ = places()
    out = refs[8]
    first = pl.program_id(0) * 9

    def run(turn):
        def step(n, carry):
            k = first + n
            sides = []
            for side in range(2):
                halves = []
                for x in range(2):
                    pieces = [refs[side * 4 + (turn - y) % 4][x, k].astype(F32) for y in range(4)]
                    halves.append(jnp.concatenate(pieces, 0))
                sides.append(jnp.concatenate(halves, 1) * scale)
            low = jnp.where(core == 0, sides[0], sides[1])
            high = jnp.where(core == 0, sides[1], sides[0])
            out[n] = jnp.concatenate([low, high], 0).T
            return carry

        lax.fori_loop(0, 9, step, 0, unroll=3)

    for turn in range(4):
        pl.when(y_at == turn)(functools.partial(run, turn))


def members(key):
    found = {}
    for y in range(4):
        for rep in range(2):
            for half in range(2):
                for z in range(8):
                    for core in range(2):
                        x = half * 2 + rep
                        found.setdefault(key(core, x, y, z), []).append(flat_id(core, x, y, z))
    return list(found.values())


def exchange(value, key):
    return lax.all_to_all(
        value, ALL, split_axis=0, concat_axis=0, axis_index_groups=members(key), tiled=False
    )


def body(feats, weight, cotan, face_send, corner_send, pair_out, pair_in, row_map):
    blocks = feats.reshape(NB, ROWS, C)
    lists = [("s", face_send), ("s", corner_send.swapaxes(1, 2))]
    pairs = [("s", v.swapaxes(1, 2)) for v in (pair_out, pair_in)] + [("v", row_map[0])]
    five, six = shape_of(5, ROWS, C), shape_of(6, ROWS, C)

    face_x, low_y, high_y = call(pick_kernel, lists + [("v", blocks)], [six, five, five])
    from_x = grid_shift(face_x, 1, 0)
    low_y = lax.dynamic_update_slice(low_y, from_x[4:5], (4, 0, 0))
    high_y = lax.dynamic_update_slice(high_y, from_x[5:6], (4, 0, 0))
    from_high = grid_shift(low_y, 0, -1)
    from_low = grid_shift(high_y, 0, 1)
    part = lax.dynamic_slice_in_dim(weight, lax.axis_index("gx") * 128, 128, 1)
    far = lax.ppermute(
        tie(part, from_x), ALL, torus_perm(lambda c, x, y, z: (c, x + (1 if c == 0 else -1), y, z))
    )
    far = tie(far, from_high, from_low)
    far_other = shift(far, core=1)

    act, grad, keep, send = call(
        forward_kernel,
        pairs
        + [("a", v) for v in (blocks, from_x, from_low, from_high, weight, far, far_other)]
        + [("v", cotan.reshape(NB, ROWS, C))],
        [
            shape_of(NB, ROWS, C),
            shape_of(NB, ROWS, C),
            shape_of(16, K, 16, 128),
            shape_of(16, K, 16, 128),
        ],
        [
            pltpu.VMEM((EXT, ROWS, C), BF),
            pltpu.VMEM((K, C, C), BF),
            pltpu.VMEM((K, PAIRS * ROWS, C), BF),
            pltpu.VMEM((NB, ROWS, C), F32),
            pltpu.VMEM((NB, C, ROWS), BF),
            pltpu.SemaphoreType.DMA((9,)),
        ],
        pl.CostEstimate(flops=7_000_000_000, bytes_accessed=12_000_000, transcendentals=0),
    )
    got = shift(send, core=1)
    local, back_x, to_low, to_high = call(
        backward_kernel,
        pairs
        + [("v", grad)]
        + [("a", v) for v in (weight, far, far_other)],
        [shape_of(NB, ROWS, C, dtype=F32), six, five, five],
        [
            pltpu.VMEM((K, C, C), BF),
            pltpu.VMEM((K, PAIRS * ROWS, C), BF),
            pltpu.VMEM((EXT, ROWS, C), F32),
            pltpu.SemaphoreType.DMA((3,)),
        ],
        pl.CostEstimate(flops=5_000_000_000, bytes_accessed=10_000_000, transcendentals=0),
    )
    paired = (tie(keep, to_low).astype(F32) + got.astype(F32)).astype(BF)
    spread = exchange(paired, lambda c, x, y, z: (c, z))
    return_high = grid_shift(tie(to_low, spread), 0, -1)
    return_low = grid_shift(tie(to_high, spread), 0, 1)
    sum_xy = jnp.sum(spread.astype(F32), 0)
    padded = jnp.concatenate([sum_xy, jnp.zeros((KPAD - K, 16, 128), F32)], 0)
    spread = exchange(padded.astype(BF).reshape(8, 4, 16, 128), lambda c, x, y, z: (c, x, y))
    sum_z = jnp.sum(spread.astype(F32), 0).astype(BF)
    all_x = exchange(jnp.broadcast_to(sum_z, (16, 4, 16, 128)), lambda c, x, y, z: (c, x % 2, y))
    all_x = all_x.reshape(2, KPAD, 16, 128)[:, :K]
    back_x = lax.dynamic_update_slice(back_x, return_low[4:5], (4, 0, 0))
    back_x = lax.dynamic_update_slice(back_x, return_high[4:5], (5, 0, 0))
    return_x = grid_shift(back_x, 1, 0)
    mine = [all_x] + [shift(all_x, y=s) for s in range(1, 4)]
    other = [shift(tie(piece, return_low, return_high), core=1) for piece in mine]

    input_grad = call(
        input_kernel,
        lists + [("v", v) for v in (local, return_x, return_low, return_high)],
        [shape_of(NB, ROWS, C)],
        [pltpu.VMEM((NB, ROWS, C), F32)],
    )[0]
    tiles = lax.axis_size("gx") * lax.axis_size("gy") * lax.axis_size("rep")
    scale = float((tiles * PAIRS * ROWS) ** (-0.5))
    pieces = mine + other
    weight_grad = pl.pallas_call(
        functools.partial(final_kernel, scale),
        grid=(3,),
        out_shape=shape_of(K, C, 128, dtype=F32),
        in_specs=[pl.BlockSpec((2, K, 16, 128), lambda n: (0, 0, 0, 0))] * 8,
        out_specs=pl.BlockSpec((9, C, 128), lambda n: (n, 0, 0)),
        compiler_params=PARAMS,
    )(*pieces)
    return act.reshape(-1, C), input_grad.reshape(-1, C), weight_grad


def solution(mesh):
    tiles = ("gx", "gy", "rep")
    in_specs = (
        P(tiles, None),
        P(None, None, "rep"),
        P(tiles, None),
        P(tiles, None, None),
        P(tiles, None, None),
        P(tiles, None, None),
        P(tiles, None, None),
        P(tiles, None, None, None),
    )
    out_specs = (P(tiles, None), P(tiles, None), P(None, None, "rep"))
    return jax.shard_map(body, mesh=mesh, in_specs=in_specs, out_specs=out_specs, check_vma=False)
```

time: 187 us -> 140 us (0.75)
  blocking collectives: 55.6 us -> 27.7 us
  Pallas kernels: 43.4 us -> 20.9 us
  starting transfers between devices: 36.6 us -> 47.4 us
  waiting for transfers between devices: 41 us -> 32.5 us
    all_to_all x3 -> x1, blocking collectives: 55.6 us -> 27.7 us  [exchange(): lax.all_to_all(value, ALL, split_axis=0, concat_axis=0, axis_index_groups...]
    pallas_call x6 -> x4, Pallas kernels: 43.4 us -> 17.8 us  [call(): pl.pallas_call(kernel, out_shape=[out for _, out in outs], in_specs=[plac...]
    all_to_all x0 -> x2, waiting for transfers between devices: none -> 12.4 us  [exchange(): lax.all_to_all(value, ALL, split_axis=0, concat_axis=0, axis_index_groups...]
    all_to_all x0 -> x2, starting transfers between devices: none -> 11.6 us  [exchange(): lax.all_to_all(value, ALL, split_axis=0, concat_axis=0, axis_index_groups...]
    ppermute x1, waiting for transfers between devices: 10.3 us -> 0.3 us  [body(): lax.ppermute(tie(part, from_x), ALL, torus_perm(lambda c, x, y, z: (c, x...]
    ppermute x6, waiting for transfers between devices: 24.3 us -> 15 us  [grid_shift(): return lax.ppermute(value, ALL, pairs)]
    ppermute x6, starting transfers between devices: 11.8 us -> 18.8 us  [grid_shift(): return lax.ppermute(value, ALL, pairs)]
    ppermute x7 -> x9, starting transfers between devices: 21.4 us -> 16.3 us  [shift(): return lax.ppermute(value, ALL, torus_perm(move))]
  transfers between devices with their start and end apart: 14 -> 18, of which waited for: 8 -> 10; matrix products, arithmetic and copies ran while one was open for 1% -> 2% of each run, Pallas kernels for 8% -> 6%
where the time goes in v3:
time: 140 us; the launch traced here: 139 us
  starting transfers between devices  47.4 us (34%)
  waiting for transfers between devices  32.5 us (23%)
  blocking collectives  27.7 us (20%)
  Pallas kernels  20.9 us (15%)
  local copies, waits for them, and re-layouts  7.75 us (6%)
  other arithmetic  2.26 us (2%)
    all_to_all x1, blocking collectives, exchange(): lax.all_to_all(value, ALL, split_axis=0, concat_axis=0, axis_index_groups...  27.7 us
    ppermute x6, starting transfers between devices, grid_shift(): return lax.ppermute(value, ALL, pairs)  18.8 us
    pallas_call x4, Pallas kernels, call(): pl.pallas_call(kernel, out_shape=[out for _, out in outs], in_specs=[plac...  17.8 us
    ppermute x9, starting transfers between devices, shift(): return lax.ppermute(value, ALL, torus_perm(move))  16.3 us
    ppermute x6, waiting for transfers between devices, grid_shift(): return lax.ppermute(value, ALL, pairs)  15 us
    all_to_all x2, waiting for transfers between devices, exchange(): lax.all_to_all(value, ALL, split_axis=0, concat_axis=0, axis_index_groups...  12.4 us
    all_to_all x2, starting transfers between devices, exchange(): lax.all_to_all(value, ALL, split_axis=0, concat_axis=0, axis_index_groups...  11.6 us
    ppermute x9, waiting for transfers between devices, shift(): return lax.ppermute(value, ALL, torus_perm(move))  4.92 us
  transfers between devices with their start and end apart: 18, of which 10 were waited for; matrix products, arithmetic and copies ran while one was open for 2% of the time, Pallas kernels for 6%

profile of v3, /device:TPU:1, one launch (start us, length us, event | category | flops | bytes accessed | tf_op | source)
XLA Modules:
  0.0 139.4 jit_solution(13511413480484493087)
XLA Ops:
  0.7 1.0 copy-done
  1.7 0.7 copy-done.3
  2.4 0.7 copy-done.5
  3.0 0.6 shard_map.103
  3.7 0.0 copy-start.10
  3.7 0.7 copy-done.10
  4.4 3.2 %collective-permute-start = (bf16[6,128,256]{2,1,0:T(8,128)(2,1)S(1)}, bf16[6,128,256]{2,1,0:T(8,128)(2,1)S(1)}, u32[]{:S(2)}, u32[]{:S(2)}) collective-permute-start(bf16[6,128,256]{2,1,0:T(8,128)(2,1)S(1)} %get-tuple-element.23), channel_id=1, source_target_pairs={{0,128},{1,129},{2,130},{3,131},{4,132},{5,133},{6,134},{7,135},{8... | collective-permute-start | bytes 1179656 | tf_op jit(solution)/shard_map/ppermute | solution.py:81
  7.7 1.3 constant_dynamic-slice_fusion
  8.9 0.1 collective-permute-done.from_x
  9.0 0.7 collective-permute-start.3
  9.8 0.6 slice_dynamic-update-slice_fusion.2
  10.4 1.3 collective-permute-start.2
  11.7 5.5 %collective-permute-start.1 = (bf16[5,128,256]{2,1,0:T(8,128)(2,1)}, bf16[5,128,256]{2,1,0:T(8,128)(2,1)S(1)}, u32[]{:S(2)}, u32[]{:S(2)}) collective-permute-start(bf16[5,128,256]{2,1,0:T(8,128)(2,1)} %get-tuple-element.44), channel_id=1, source_target_pairs={{0,2},{1,3},{2,4},{3,5},{4,6},{5,7},{6,8},{7,9},{8,10},{9,11},{10,... | collective-permute-start | bytes 983048 | tf_op jit(solution)/shard_map/ppermute | solution.py:81
  17.2 6.1 %collective-permute-done.2.from_high = bf16[5,128,256]{2,1,0:T(8,128)(2,1)S(1)} collective-permute-done((bf16[5,128,256]{2,1,0:T(8,128)(2,1)S(1)}, bf16[5,128,256]{2,1,0:T(8,128)(2,1)S(1)}, u32[]{:S(2)}, u32[]{:S(2)}) %collective-permute-start.2) | collective-permute-done | bytes 327712 | tf_op jit(solution)/shard_map/ppermute | solution.py:81
  23.3 7.7 %collective-permute-done.1.from_low = bf16[5,128,256]{2,1,0:T(8,128)(2,1)S(1)} collective-permute-done((bf16[5,128,256]{2,1,0:T(8,128)(2,1)}, bf16[5,128,256]{2,1,0:T(8,128)(2,1)S(1)}, u32[]{:S(2)}, u32[]{:S(2)}) %collective-permute-start.1) | collective-permute-done | bytes 327712 | tf_op jit(solution)/shard_map/ppermute | solution.py:81
  31.0 0.3 collective-permute-done.3.far
  31.3 6.4 %collective-permute-start.4 = (bf16[27,128,128]{2,1,0:T(8,128)(2,1)S(1)}, bf16[27,128,128]{2,1,0:T(8,128)(2,1)S(1)}, u32[]{:S(2)}, u32[]{:S(2)}) collective-permute-start(bf16[27,128,128]{2,1,0:T(8,128)(2,1)S(1)} %collective-permute-done.3.far), channel_id=1, source_target_pairs={{0,128},{1,129},{2,130},{3,131},{4,132},{5,133},{6,134},{7,135},{8... | collective-permute-start | bytes 2654216 | tf_op jit(solution)/shard_map/ppermute | solution.py:70
  37.7 2.1 %collective-permute-done.4.far_other = bf16[27,128,128]{2,1,0:T(8,128)(2,1)S(1)} collective-permute-done((bf16[27,128,128]{2,1,0:T(8,128)(2,1)S(1)}, bf16[27,128,128]{2,1,0:T(8,128)(2,1)S(1)}, u32[]{:S(2)}, u32[]{:S(2)}) %collective-permute-start.4) | collective-permute-done | bytes 884768 | tf_op jit(solution)/shard_map/ppermute | solution.py:70
  39.8 0.0 copy-start.7
  39.8 1.0 copy-done.7
  40.8 9.3 %shard_map.104 = (bf16[8,128,256]{2,1,0:T(8,128)(2,1)}, bf16[8,128,256]{2,1,0:T(8,128)(2,1)S(1)}, bf16[16,27,16,128]{3,2,1,0:T(8,128)(2,1)S(1)}, bf16[16,27,16,128]{3,2,1,0:T(8,128)(2,1)S(1)}) custom-call(s32[1,4,27]{2,1,0:T(4,128)S(1)} %bitcast.17, s32[1,4,27]{2,1,0:T(4,128)S(1)} %bitcast.19, s32[27,4,128]{2,1,0:T(4,128)S(1)} %bitcast.15, ...), custom_call_target="tpu_custom_call" | custom-call | flops 7000000000 | bytes 12000000 | tf_op jit(solution)/shard_map/pallas_call | solution.py:27
  50.1 0.5 collective-permute-start.5
  50.5 6.2 %shard_map.105 = (f32[8,128,256]{2,1,0:T(8,128)S(1)}, bf16[6,128,256]{2,1,0:T(8,128)(2,1)S(1)}, bf16[5,128,256]{2,1,0:T(8,128)(2,1)S(1)}, bf16[5,128,256]{2,1,0:T(8,128)(2,1)S(1)}) custom-call(s32[1,4,27]{2,1,0:T(4,128)S(1)} %bitcast.18, s32[1,4,27]{2,1,0:T(4,128)S(1)} %bitcast.20, s32[27,4,128]{2,1,0:T(4,128)S(1)} %bitcast.16, ...), custom_call_target="tpu_custom_call" | custom-call | flops 5000000000 | bytes 10000000 | tf_op jit(solution)/shard_map/pallas_call | solution.py:27
  56.7 0.0 copy-start.8
  56.8 0.5 add_convert_fusion
  57.2 0.2 copy-done.8
  57.5 27.7 %all_to_all.15 = bf16[16,27,16,128]{3,2,1,0:T(8,128)(2,1)} all-to-all(bf16[16,27,16,128]{3,2,1,0:T(8,128)(2,1)S(1)} %add_convert_fusion), channel_id=1, replica_groups={{0,2,1,3,4,6,5,7,8,10,9,11,12,14,13,15},{128,130,129,131,132,134,133,13..., dimensions={0} | all-to-all | bytes 3538944 | tf_op jit(solution)/shard_map/all_to_all | solution.py:283
  85.2 1.8 %reduce.1 = bf16[27,16,128]{2,1,0:T(8,128)(2,1)S(1)} reduce(bf16[16,27,16,128]{3,2,1,0:T(8,128)(2,1)} %all_to_all.15, bf16[]{:T(256)} %constant.21.clone.1), dimensions={0}, to_apply=%region_0.0.clone | reduce | flops 829440 | bytes 1880066 | tf_op jit(solution)/shard_map/reduce_sum | solution.py:347
  87.0 0.7 concatenate.3
  87.7 8.1 %all-to-all-start.1 = ((bf16[8,4,16,128]{3,2,1,0:T(8,128)(2,1)}), bf16[8,4,16,128]{3,2,1,0:T(8,128)(2,1)S(1)}, u32[]{:S(2)}, u32[]{:S(2)}) async-start(bf16[8,4,16,128]{3,2,1,0:T(8,128)(2,1)} %bitcast.8), calls=%async_computation.1 | async-start | bytes 262144 | tf_op jit(solution)/shard_map/all_to_all | solution.py:283
  95.7 3.6 %collective-permute-start.6 = (bf16[5,128,256]{2,1,0:T(8,128)(2,1)S(1)}, bf16[5,128,256]{2,1,0:T(8,128)(2,1)S(1)}, u32[]{:S(2)}, u32[]{:S(2)}) collective-permute-start(bf16[5,128,256]{2,1,0:T(8,128)(2,1)S(1)} %copy-done.9), channel_id=1, source_target_pairs={{0,2},{1,3},{2,4},{3,5},{4,6},{5,7},{6,8},{7,9},{8,10},{9,11},{10,... | collective-permute-start | bytes 983048 | tf_op jit(solution)/shard_map/ppermute | solution.py:81
  99.3 4.4 %all-to-all-done.1 = bf16[8,4,16,128]{3,2,1,0:T(8,128)(2,1)S(1)} async-done(((bf16[8,4,16,128]{3,2,1,0:T(8,128)(2,1)}), bf16[8,4,16,128]{3,2,1,0:T(8,128)(2,1)S(1)}, u32[]{:S(2)}, u32[]{:S(2)}) %all-to-all-start.1) | async-done | bytes 131104 | tf_op jit(solution)/shard_map/all_to_all | solution.py:283
  103.8 0.8 broadcast_in_dim.4
  104.5 3.5 %all-to-all-start.2 = ((bf16[16,4,16,128]{3,2,1,0:T(8,128)(2,1)}), bf16[16,4,16,128]{3,2,1,0:T(8,128)(2,1)S(1)}, u32[]{:S(2)}, u32[]{:S(2)}) async-start(bf16[16,4,16,128]{3,2,1,0:T(8,128)(2,1)} %broadcast_in_dim.4), calls=%async_computation.2 | async-start | bytes 524288 | tf_op jit(solution)/shard_map/all_to_all | solution.py:283
  108.1 1.3 collective-permute-start.7
  109.4 7.9 %all-to-all-done.2 = bf16[16,4,16,128]{3,2,1,0:T(8,128)(2,1)S(1)} async-done(((bf16[16,4,16,128]{3,2,1,0:T(8,128)(2,1)}), bf16[16,4,16,128]{3,2,1,0:T(8,128)(2,1)S(1)}, u32[]{:S(2)}, u32[]{:S(2)}) %all-to-all-start.2) | async-done | bytes 262176 | tf_op jit(solution)/shard_map/all_to_all | solution.py:283
  117.3 2.3 %collective-permute-start.11 = (bf16[2,27,16,128]{3,2,1,0:T(8,128)(2,1)S(1)}, bf16[2,27,16,128]{3,2,1,0:T(8,128)(2,1)S(1)}, u32[]{:S(2)}, u32[]{:S(2)}) collective-permute-start(bf16[2,27,16,128]{3,2,1,0:T(8,128)(2,1)S(1)} %slice.24.refs_0_), channel_id=1, source_target_pairs={{0,12},{1,13},{2,14},{3,15},{4,0},{5,1},{6,2},{7,3},{8,4},{9,5},{1... | collective-permute-start | bytes 663560 | tf_op jit(solution)/shard_map/ppermute | solution.py:70
  119.6 0.3 collective-permute-start.10
  120.0 0.3 collective-permute-start.9
  120.3 1.1 collective-permute-done.7.from_high
  121.4 3.9 %collective-permute-start.8 = (bf16[6,128,256]{2,1,0:T(8,128)(2,1)S(1)}, bf16[6,128,256]{2,1,0:T(8,128)(2,1)S(1)}, u32[]{:S(2)}, u32[]{:S(2)}) collective-permute-start(bf16[6,128,256]{2,1,0:T(8,128)(2,1)S(1)} %slice_dynamic-update-slice_fusion), channel_id=1, source_target_pairs={{0,128},{1,129},{2,130},{3,131},{4,132},{5,133},{6,134},{7,135},{8... | collective-permute-start | bytes 1179656 | tf_op jit(solution)/shard_map/ppermute | solution.py:81
  125.3 0.1 collective-permute-start.12
  125.4 0.6 collective-permute-done.10.refs_2_
  126.0 2.3 %collective-permute-done.9.refs_1_ = bf16[2,27,16,128]{3,2,1,0:T(8,128)(2,1)S(1)} collective-permute-done((bf16[2,27,16,128]{3,2,1,0:T(8,128)(2,1)S(1)}, bf16[2,27,16,128]{3,2,1,0:T(8,128)(2,1)S(1)}, u32[]{:S(2)}, u32[]{:S(2)}) %collective-permute-start.9) | collective-permute-done | bytes 221216 | tf_op jit(solution)/shard_map/ppermute | solution.py:70
  128.3 5.8 %collective-permute-start.13 = (bf16[2,27,16,128]{3,2,1,0:T(8,128)(2,1)S(1)}, bf16[2,27,16,128]{3,2,1,0:T(8,128)(2,1)S(1)}, u32[]{:S(2)}, u32[]{:S(2)}) collective-permute-start(bf16[2,27,16,128]{3,2,1,0:T(8,128)(2,1)S(1)} %collective-permute-done.9.refs_1_), channel_id=1, source_target_pairs={{0,128},{1,129},{2,130},{3,131},{4,132},{5,133},{6,134},{7,135},{8... | collective-permute-start | bytes 663560 | tf_op jit(solution)/shard_map/ppermute | solution.py:70
  134.1 0.5 collective-permute-start.15
  134.6 1.7 %shard_map.106 = bf16[8,128,256]{2,1,0:T(8,128)(2,1)} custom-call(s32[1,4,4]{2,1,0:T(4,128)S(1)} %copy-done.4, s32[1,1,4]{2,1,0:T(1,128)S(1)} %bitcast.13, f32[8,128,256]{2,1,0:T(8,128)S(1)} %get-tuple-element.30.local, bf16[6,128,256]{2,1,0:T(8,128)(2,1)S(1)} %collective-permute-done.8.from_x, bf16[5,128,256]{2,1,0:T(8,128)(2,1)S(1)} %collective-permute-done.6.from_low, ...), custom_call_target="tpu_custom_call" | custom-call | tf_op jit(solution)/shard_map/pallas_call | solution.py:27
  136.3 3.1 %shard_map.107 = f32[27,256,128]{2,1,0:T(8,128)} custom-call(bf16[2,27,16,128]{3,2,1,0:T(8,128)(2,1)S(1)} %slice.24.refs_0_, bf16[2,27,16,128]{3,2,1,0:T(8,128)(2,1)S(1)} %collective-permute-done.9.refs_1_, bf16[2,27,16,128]{3,2,1,0:T(8,128)(2,1)S(1)} %collective-permute-done.10.refs_2_, bf16[2,27,16,128]{3,2,1,0:T(8,128)(2,1)S(1)} %collective-permute-done.11.refs_3_, ...), custom_call_target="tpu_custom_call" | custom-call | tf_op jit(solution)/shard_map/pallas_call | solution.py:368
  (34 shorter events, 0.1 us)
Async XLA Ops:
  0.6 39.1 %copy-start.13 = (s32[1,27,4]{1,2,0:T(4,128)S(1)}, s32[1,27,4]{1,2,0:T(4,128)}, u32[]{:S(2)}) copy-start(s32[1,27,4]{1,2,0:T(4,128)} %param.13) | copy-start | bytes 1300
  0.6 1.0 copy-start
  1.7 0.7 copy-start.3
  2.4 0.7 copy-start.5
  3.0 36.7 %copy-start.1 = (bf16[1024,256]{1,0:T(8,128)(2,1)S(1)}, bf16[1024,256]{1,0:T(8,128)(2,1)}, u32[]{:S(2)}) copy-start(bf16[1024,256]{1,0:T(8,128)(2,1)} %param.8) | copy-start | bytes 1572868
  3.0 36.7 %copy-start.2 = (bf16[27,256,128]{2,1,0:T(8,128)(2,1)S(1)}, bf16[27,256,128]{2,1,0:T(8,128)(2,1)}, u32[]{:S(2)}) copy-start(bf16[27,256,128]{2,1,0:T(8,128)(2,1)} %own.3) | copy-start | bytes 5308420
  3.0 36.7 %copy-start.11 = (s32[1,27,4,128]{3,2,1,0:T(4,128)S(1)}, s32[1,27,4,128]{3,2,1,0:T(4,128)}, u32[]{:S(2)}) copy-start(s32[1,27,4,128]{3,2,1,0:T(4,128)} %param.15) | copy-start | bytes 165892
  3.0 36.7 %copy-start.14 = (s32[1,27,4]{1,2,0:T(4,128)S(1)}, s32[1,27,4]{1,2,0:T(4,128)}, u32[]{:S(2)}) copy-start(s32[1,27,4]{1,2,0:T(4,128)} %param.14) | copy-start | bytes 1300
  3.7 0.7 copy-start.10
  4.4 4.6 %collective-permute-start = (bf16[6,128,256]{2,1,0:T(8,128)(2,1)S(1)}, bf16[6,128,256]{2,1,0:T(8,128)(2,1)S(1)}, u32[]{:S(2)}, u32[]{:S(2)}) collective-permute-start(bf16[6,128,256]{2,1,0:T(8,128)(2,1)S(1)} %get-tuple-element.23), channel_id=1, source_target_pairs={{0,128},{1,129},{2,130},{3,131},{4,132},{5,133},{6,134},{7,135},{8... | collective-permute-start | bytes 1179656 | tf_op jit(solution)/shard_map/ppermute | solution.py:81
  9.0 22.2 %collective-permute-start.3 = (bf16[27,128,128]{2,1,0:T(8,128)(2,1)S(1)}, bf16[27,128,128]{2,1,0:T(8,128)(2,1)S(1)}, u32[]{:S(2)}, u32[]{:S(2)}) collective-permute-start(bf16[27,128,128]{2,1,0:T(8,128)(2,1)S(1)} %constant_dynamic-slice_fusion), channel_id=1, source_target_pairs={{0,1},{1,2},{2,3},{3,0},{4,5},{5,6},{6,7},{7,4},{8,9},{9,10},{10,1... | collective-permute-start | bytes 2654216 | tf_op jit(solution)/shard_map/ppermute | solution.py:301
  10.4 12.9 %collective-permute-start.2 = (bf16[5,128,256]{2,1,0:T(8,128)(2,1)S(1)}, bf16[5,128,256]{2,1,0:T(8,128)(2,1)S(1)}, u32[]{:S(2)}, u32[]{:S(2)}) collective-permute-start(bf16[5,128,256]{2,1,0:T(8,128)(2,1)S(1)} %get-tuple-element.43), channel_id=1, source_target_pairs={{2,0},{3,1},{4,2},{5,3},{6,4},{7,5},{8,6},{9,7},{10,8},{11,9},{12,... | collective-permute-start | bytes 983048 | tf_op jit(solution)/shard_map/ppermute | solution.py:81
  11.7 19.3 %collective-permute-start.1 = (bf16[5,128,256]{2,1,0:T(8,128)(2,1)}, bf16[5,128,256]{2,1,0:T(8,128)(2,1)S(1)}, u32[]{:S(2)}, u32[]{:S(2)}) collective-permute-start(bf16[5,128,256]{2,1,0:T(8,128)(2,1)} %get-tuple-element.44), channel_id=1, source_target_pairs={{0,2},{1,3},{2,4},{3,5},{4,6},{5,7},{6,8},{7,9},{8,10},{9,11},{10,... | collective-permute-start | bytes 983048 | tf_op jit(solution)/shard_map/ppermute | solution.py:81
  31.3 8.5 %collective-permute-start.4 = (bf16[27,128,128]{2,1,0:T(8,128)(2,1)S(1)}, bf16[27,128,128]{2,1,0:T(8,128)(2,1)S(1)}, u32[]{:S(2)}, u32[]{:S(2)}) collective-permute-start(bf16[27,128,128]{2,1,0:T(8,128)(2,1)S(1)} %collective-permute-done.3.far), channel_id=1, source_target_pairs={{0,128},{1,129},{2,130},{3,131},{4,132},{5,133},{6,134},{7,135},{8... | collective-permute-start | bytes 2654216 | tf_op jit(solution)/shard_map/ppermute | solution.py:70
  39.8 1.0 copy-start.7
  40.8 9.7 %copy-start.12 = (s32[1,27,4,128]{3,2,1,0:T(4,128)S(1)}, s32[1,27,4,128]{3,2,1,0:T(4,128)}, u32[]{:S(2)}) copy-start(s32[1,27,4,128]{3,2,1,0:T(4,128)} %param.15) | copy-start | bytes 165892
  50.1 6.7 %collective-permute-start.5 = (bf16[16,27,16,128]{3,2,1,0:T(8,128)(2,1)S(1)}, bf16[16,27,16,128]{3,2,1,0:T(8,128)(2,1)S(1)}, u32[]{:S(2)}, u32[]{:S(2)}) collective-permute-start(bf16[16,27,16,128]{3,2,1,0:T(8,128)(2,1)S(1)} %get-tuple-element.36), channel_id=1, source_target_pairs={{0,128},{1,129},{2,130},{3,131},{4,132},{5,133},{6,134},{7,135},{8... | collective-permute-start | bytes 5308424 | tf_op jit(solution)/shard_map/ppermute | solution.py:70
  56.7 0.7 copy-start.8
  85.2 10.5 %copy-start.9 = (bf16[5,128,256]{2,1,0:T(8,128)(2,1)S(1)}, bf16[5,128,256]{2,1,0:T(8,128)(2,1)}, u32[]{:S(2)}) copy-start(bf16[5,128,256]{2,1,0:T(8,128)(2,1)} %copy-done.8) | copy-start | bytes 983044
  85.2 49.4 %copy-start.4 = (s32[1,4,4]{2,1,0:T(4,128)S(1)}, s32[1,4,4]{2,1,0:T(4,128)}, u32[]{:S(2)}) copy-start(s32[1,4,4]{2,1,0:T(4,128)} %face.3) | copy-start | bytes 196
  85.2 49.4 %copy-start.6 = (s32[1,4,1]{1,2,0:T(1,128)S(1)}, s32[1,4,1]{1,2,0:T(1,128)}, u32[]{:S(2)}) copy-start(s32[1,4,1]{1,2,0:T(1,128)} %param.12) | copy-start | bytes 52
  87.7 16.1 %all-to-all-start.1 = ((bf16[8,4,16,128]{3,2,1,0:T(8,128)(2,1)}), bf16[8,4,16,128]{3,2,1,0:T(8,128)(2,1)S(1)}, u32[]{:S(2)}, u32[]{:S(2)}) async-start(bf16[8,4,16,128]{3,2,1,0:T(8,128)(2,1)} %bitcast.8), calls=%async_computation.1 | async-start | bytes 262144 | tf_op jit(solution)/shard_map/all_to_all | solution.py:283
  95.7 13.7 %collective-permute-start.6 = (bf16[5,128,256]{2,1,0:T(8,128)(2,1)S(1)}, bf16[5,128,256]{2,1,0:T(8,128)(2,1)S(1)}, u32[]{:S(2)}, u32[]{:S(2)}) collective-permute-start(bf16[5,128,256]{2,1,0:T(8,128)(2,1)S(1)} %copy-done.9), channel_id=1, source_target_pairs={{0,2},{1,3},{2,4},{3,5},{4,6},{5,7},{6,8},{7,9},{8,10},{9,11},{10,... | collective-permute-start | bytes 983048 | tf_op jit(solution)/shard_map/ppermute | solution.py:81
  104.5 12.8 %all-to-all-start.2 = ((bf16[16,4,16,128]{3,2,1,0:T(8,128)(2,1)}), bf16[16,4,16,128]{3,2,1,0:T(8,128)(2,1)S(1)}, u32[]{:S(2)}, u32[]{:S(2)}) async-start(bf16[16,4,16,128]{3,2,1,0:T(8,128)(2,1)} %broadcast_in_dim.4), calls=%async_computation.2 | async-start | bytes 524288 | tf_op jit(solution)/shard_map/all_to_all | solution.py:283
  108.1 13.3 %collective-permute-start.7 = (bf16[5,128,256]{2,1,0:T(8,128)(2,1)S(1)}, bf16[5,128,256]{2,1,0:T(8,128)(2,1)S(1)}, u32[]{:S(2)}, u32[]{:S(2)}) collective-permute-start(bf16[5,128,256]{2,1,0:T(8,128)(2,1)S(1)} %get-tuple-element.38), channel_id=1, source_target_pairs={{2,0},{3,1},{4,2},{5,3},{6,4},{7,5},{8,6},{9,7},{10,8},{11,9},{12,... | collective-permute-start | bytes 983048 | tf_op jit(solution)/shard_map/ppermute | solution.py:81
  117.3 8.1 %collective-permute-start.11 = (bf16[2,27,16,128]{3,2,1,0:T(8,128)(2,1)S(1)}, bf16[2,27,16,128]{3,2,1,0:T(8,128)(2,1)S(1)}, u32[]{:S(2)}, u32[]{:S(2)}) collective-permute-start(bf16[2,27,16,128]{3,2,1,0:T(8,128)(2,1)S(1)} %slice.24.refs_0_), channel_id=1, source_target_pairs={{0,12},{1,13},{2,14},{3,15},{4,0},{5,1},{6,2},{7,3},{8,4},{9,5},{1... | collective-permute-start | bytes 663560 | tf_op jit(solution)/shard_map/ppermute | solution.py:70
  119.6 6.4 %collective-permute-start.10 = (bf16[2,27,16,128]{3,2,1,0:T(8,128)(2,1)S(1)}, bf16[2,27,16,128]{3,2,1,0:T(8,128)(2,1)S(1)}, u32[]{:S(2)}, u32[]{:S(2)}) collective-permute-start(bf16[2,27,16,128]{3,2,1,0:T(8,128)(2,1)S(1)} %slice.24.refs_0_), channel_id=1, source_target_pairs={{0,8},{1,9},{2,10},{3,11},{4,12},{5,13},{6,14},{7,15},{8,0},{9,1},... | collective-permute-start | bytes 663560 | tf_op jit(solution)/shard_map/ppermute | solution.py:70
  120.0 8.3 %collective-permute-start.9 = (bf16[2,27,16,128]{3,2,1,0:T(8,128)(2,1)S(1)}, bf16[2,27,16,128]{3,2,1,0:T(8,128)(2,1)S(1)}, u32[]{:S(2)}, u32[]{:S(2)}) collective-permute-start(bf16[2,27,16,128]{3,2,1,0:T(8,128)(2,1)S(1)} %slice.24.refs_0_), channel_id=1, source_target_pairs={{0,4},{1,5},{2,6},{3,7},{4,8},{5,9},{6,10},{7,11},{8,12},{9,13},{1... | collective-permute-start | bytes 663560 | tf_op jit(solution)/shard_map/ppermute | solution.py:70
  121.4 13.2 %collective-permute-start.8 = (bf16[6,128,256]{2,1,0:T(8,128)(2,1)S(1)}, bf16[6,128,256]{2,1,0:T(8,128)(2,1)S(1)}, u32[]{:S(2)}, u32[]{:S(2)}) collective-permute-start(bf16[6,128,256]{2,1,0:T(8,128)(2,1)S(1)} %slice_dynamic-update-slice_fusion), channel_id=1, source_target_pairs={{0,128},{1,129},{2,130},{3,131},{4,132},{5,133},{6,134},{7,135},{8... | collective-permute-start | bytes 1179656 | tf_op jit(solution)/shard_map/ppermute | solution.py:81
  125.3 10.9 %collective-permute-start.12 = (bf16[2,27,16,128]{3,2,1,0:T(8,128)(2,1)S(1)}, bf16[2,27,16,128]{3,2,1,0:T(8,128)(2,1)S(1)}, u32[]{:S(2)}, u32[]{:S(2)}) collective-permute-start(bf16[2,27,16,128]{3,2,1,0:T(8,128)(2,1)S(1)} %slice.24.refs_0_), channel_id=1, source_target_pairs={{0,128},{1,129},{2,130},{3,131},{4,132},{5,133},{6,134},{7,135},{8... | collective-permute-start | bytes 663560 | tf_op jit(solution)/shard_map/ppermute | solution.py:70
  128.3 8.0 %collective-permute-start.13 = (bf16[2,27,16,128]{3,2,1,0:T(8,128)(2,1)S(1)}, bf16[2,27,16,128]{3,2,1,0:T(8,128)(2,1)S(1)}, u32[]{:S(2)}, u32[]{:S(2)}) collective-permute-start(bf16[2,27,16,128]{3,2,1,0:T(8,128)(2,1)S(1)} %collective-permute-done.9.refs_1_), channel_id=1, source_target_pairs={{0,128},{1,129},{2,130},{3,131},{4,132},{5,133},{6,134},{7,135},{8... | collective-permute-start | bytes 663560 | tf_op jit(solution)/shard_map/ppermute | solution.py:70
  134.1 2.2 %collective-permute-start.14 = (bf16[2,27,16,128]{3,2,1,0:T(8,128)(2,1)S(1)}, bf16[2,27,16,128]{3,2,1,0:T(8,128)(2,1)S(1)}, u32[]{:S(2)}, u32[]{:S(2)}) collective-permute-start(bf16[2,27,16,128]{3,2,1,0:T(8,128)(2,1)S(1)} %collective-permute-done.10.refs_2_), channel_id=1, source_target_pairs={{0,128},{1,129},{2,130},{3,131},{4,132},{5,133},{6,134},{7,135},{8... | collective-permute-start | bytes 663560 | tf_op jit(solution)/shard_map/ppermute | solution.py:70
  134.1 2.2 %collective-permute-start.15 = (bf16[2,27,16,128]{3,2,1,0:T(8,128)(2,1)S(1)}, bf16[2,27,16,128]{3,2,1,0:T(8,128)(2,1)S(1)}, u32[]{:S(2)}, u32[]{:S(2)}) collective-permute-start(bf16[2,27,16,128]{3,2,1,0:T(8,128)(2,1)S(1)} %collective-permute-done.11.refs_3_), channel_id=1, source_target_pairs={{0,128},{1,129},{2,130},{3,131},{4,132},{5,133},{6,134},{7,135},{8... | collective-permute-start | bytes 663560 | tf_op jit(solution)/shard_map/ppermute | solution.py:70

commit v4 on v3

--- a/solution.py
+++ b/solution.py
@@ -22,7 +22,12 @@
 
 
 def call(kernel, ins, outs, scratch=(), cost=None):
-    place = {"s": SM, "v": VM, "a": pl.BlockSpec(memory_space=pl.ANY)}
+    place = {
+        "s": SM,
+        "v": VM,
+        "a": pl.BlockSpec(memory_space=pl.ANY),
+        "h": pl.BlockSpec(memory_space=pltpu.HBM),
+    }
     outs = [out if isinstance(out, tuple) else ("v", out) for out in outs]
     return pl.pallas_call(
         kernel,
@@ -70,27 +75,29 @@
     return lax.ppermute(value, ALL, torus_perm(move))
 
 
-def grid_shift(value, step_x, step_y):
+def swap_y(value, which):
     pairs = []
-    for i in range(2):
-        for j in range(64):
-            if 0 <= j + step_y < 64:
-                for r in range(2):
-                    to = ((i + step_x) % 2 * 64 + j + step_y) * 2 + r
-                    pairs.append(((i * 64 + j) * 2 + r, to))
+    for j in range(64):
+        to = (j ^ 1) if which == 0 else (j + 1 if j % 2 else j - 1)
+        if 0 <= to < 64:
+            pairs += [((i * 64 + j) * 2 + r, (i * 64 + to) * 2 + r) for i in (0, 1) for r in (0, 1)]
     return lax.ppermute(value, ALL, pairs)
 
 
-def pick_kernel(face, corner, feats, face_x, low_y, high_y):
-    i = lax.axis_index("gx")
+def ends():
+    return lax.axis_index("gx"), 1 - lax.axis_index("gy") % 2
+
+
+def pick_kernel(face, corner, feats, face_x, first, second):
+    i, even = ends()
     for n in range(4):
         face_x[n] = feats[face[0, 1 - i, n]]
-        low_y[n] = feats[face[0, 2, n]]
-        high_y[n] = feats[face[0, 3, n]]
-    for n in range(2):
-        face_x[4 + n] = feats[corner[0, 0, 2 * (1 - i) + n]]
-    low_y[4] = face_x[4]
-    high_y[4] = face_x[5]
+        first[n] = feats[face[0, 2 + even, n]]
+        second[n] = feats[face[0, 3 - even, n]]
+    face_x[4] = feats[corner[0, 0, 2 * (1 - i) + even]]
+    face_x[5] = feats[corner[0, 0, 2 * (1 - i) + 1 - even]]
+    first[4] = face_x[4]
+    second[4] = face_x[5]
 
 
 def weight_copies(core, side, own, far, far_other, full, sems):
@@ -114,32 +121,26 @@
                 getattr(copy, act)()
 
 
-def forward_kernel(
-    outs, ins, maps, feats, from_x, from_low, from_high, own, far, far_other, cotan,
-    act, grad, keep, send,
-    ext, full, rows, acc, flipped, sems,
-):
-    core, rep = places()[:2]
-    weights = (own, far, far_other, full, sems)
-    on_weights("start", core, rep, *weights)
+def gather_kernel(ins, maps, feats, from_x, first, second, rows, ext, sems):
+    core, even = ends()
     ext[8:16] = jnp.zeros((8, ROWS, C), BF)
     ext[24:29] = jnp.zeros((5, ROWS, C), BF)
+    corners = 24 + 2 * (1 - core)
     copies = [
-        pltpu.make_async_copy(feats, ext.at[0:8], sems.at[3]),
-        pltpu.make_async_copy(from_x.at[0:4], ext.at[pl.ds(8 + 4 * (1 - core), 4)], sems.at[4]),
-        pltpu.make_async_copy(from_low.at[0:4], ext.at[16:20], sems.at[5]),
-        pltpu.make_async_copy(from_high.at[0:4], ext.at[20:24], sems.at[6]),
-        pltpu.make_async_copy(from_low.at[4], ext.at[24 + 2 * (1 - core)], sems.at[7]),
-        pltpu.make_async_copy(from_high.at[4], ext.at[25 + 2 * (1 - core)], sems.at[8]),
+        pltpu.make_async_copy(feats, ext.at[0:8], sems.at[0]),
+        pltpu.make_async_copy(from_x.at[0:4], ext.at[pl.ds(8 + 4 * (1 - core), 4)], sems.at[1]),
+        pltpu.make_async_copy(first.at[0:4], ext.at[pl.ds(16 + 4 * even, 4)], sems.at[2]),
+        pltpu.make_async_copy(second.at[0:4], ext.at[pl.ds(20 - 4 * even, 4)], sems.at[3]),
+        pltpu.make_async_copy(first.at[4], ext.at[corners + even], sems.at[4]),
+        pltpu.make_async_copy(second.at[4], ext.at[corners + 1 - even], sems.at[5]),
     ]
     for copy in copies:
         copy.start()
-    acc[...] = jnp.zeros_like(acc)
     lanes = lax.broadcasted_iota(jnp.int32, (ROWS, ROWS), 0)
     for copy in copies:
         copy.wait()
 
-    def gather_step(k, carry):
+    def step(k, carry):
         map_k = maps[k]
         for p in range(PAIRS):
             hot = (lanes == map_k[p : p + 1, :]).astype(F32).astype(BF)
@@ -149,7 +150,20 @@
             rows[k, p * ROWS : (p + 1) * ROWS, :] = picked.astype(BF)
         return carry
 
-    lax.fori_loop(0, K, gather_step, 0, unroll=27)
+    lax.fori_loop(0, K, step, 0, unroll=27)
+
+
+def forward_kernel(
+    outs, rows, own, far, far_other, cotan_in,
+    act, grad, keep, send,
+    full, acc, flipped, cotan, sems,
+):
+    core, rep = places()[:2]
+    weights = (own, far, far_other, full, sems)
+    on_weights("start", core, rep, *weights)
+    cotan_copy = pltpu.make_async_copy(cotan_in, cotan, sems.at[3])
+    cotan_copy.start()
+    acc[...] = jnp.zeros_like(acc)
     on_weights("wait", core, rep, *weights)
 
     def product_step(k, carry):
@@ -159,6 +173,8 @@
         return carry
 
     lax.fori_loop(0, K, product_step, 0, unroll=27)
+
+    cotan_copy.wait()
 
     def grad_step(b, carry):
         value = acc[b]
@@ -191,7 +207,7 @@
 
 def backward_kernel(
     outs, ins, maps, grad, own, far, far_other,
-    local, face_x, to_low, to_high,
+    local, face_x, first, second,
     full, rows, acc, sems,
 ):
     core, rep = places()[:2]
@@ -223,22 +239,42 @@
     local[...] = acc[0:8]
     face_x[0:4] = acc[pl.ds(8 + 4 * (1 - core), 4)].astype(BF)
     face_x[4:6] = jnp.zeros((2, ROWS, C), BF)
-    to_low[0:4] = acc[16:20].astype(BF)
-    to_low[4] = acc[24 + 2 * (1 - core)].astype(BF)
-    to_high[0:4] = acc[20:24].astype(BF)
-    to_high[4] = acc[25 + 2 * (1 - core)].astype(BF)
-
-
-def input_kernel(face, corner, local, from_x, from_low, from_high, out, acc):
-    i = lax.axis_index("gx")
+    even = ends()[1]
+    first[0:4] = acc[pl.ds(16 + 4 * even, 4)].astype(BF)
+    first[4] = acc[24 + 2 * (1 - core) + even].astype(BF)
+    second[0:4] = acc[pl.ds(20 - 4 * even, 4)].astype(BF)
+    second[4] = acc[25 + 2 * (1 - core) - even].astype(BF)
+
+
+def input_kernel(face, corner, local, from_x, first, second, out, acc):
+    i, even = ends()
     acc[...] = local[...]
     for n in range(4):
         acc[face[0, 1 - i, n]] += from_x[n].astype(F32)
-        acc[face[0, 2, n]] += from_low[n].astype(F32)
-        acc[face[0, 3, n]] += from_high[n].astype(F32)
-    for n in range(2):
-        acc[corner[0, 0, 2 * (1 - i) + n]] += from_x[4 + n].astype(F32)
+        acc[face[0, 2 + even, n]] += first[n].astype(F32)
+        acc[face[0, 3 - even, n]] += second[n].astype(F32)
+    acc[corner[0, 0, 2 * (1 - i) + even]] += from_x[4].astype(F32)
+    acc[corner[0, 0, 2 * (1 - i) + 1 - even]] += from_x[5].astype(F32)
     out[...] = acc[...].astype(BF)
+
+
+def plane_kernel(spread, out):
+    for k in range(K):
+        total = spread[0, k].astype(F32)
+        for n in range(1, 16):
+            total = total + spread[n, k].astype(F32)
+        out[k // 4, k % 4] = total.astype(BF)
+    for k in range(K, KPAD):
+        out[k // 4, k % 4] = jnp.zeros((16, 128), BF)
+
+
+def depth_kernel(spread, out):
+    for k in range(4):
+        total = spread[0, k].astype(F32)
+        for n in range(1, 8):
+            total = total + spread[n, k].astype(F32)
+        for n in range(16):
+            out[n, k] = total.astype(BF)
 
 
 def final_kernel(scale, *refs):
@@ -291,24 +327,30 @@
     pairs = [("s", v.swapaxes(1, 2)) for v in (pair_out, pair_in)] + [("v", row_map[0])]
     five, six = shape_of(5, ROWS, C), shape_of(6, ROWS, C)
 
-    face_x, low_y, high_y = call(pick_kernel, lists + [("v", blocks)], [six, five, five])
-    from_x = grid_shift(face_x, 1, 0)
-    low_y = lax.dynamic_update_slice(low_y, from_x[4:5], (4, 0, 0))
-    high_y = lax.dynamic_update_slice(high_y, from_x[5:6], (4, 0, 0))
-    from_high = grid_shift(low_y, 0, -1)
-    from_low = grid_shift(high_y, 0, 1)
+    face_x, first, second = call(pick_kernel, lists + [("v", blocks)], [six, five, five])
+    from_x = shift(face_x, core=1)
+    first = swap_y(lax.dynamic_update_slice(first, from_x[4:5], (4, 0, 0)), 0)
+    second = swap_y(lax.dynamic_update_slice(second, from_x[5:6], (4, 0, 0)), 1)
     part = lax.dynamic_slice_in_dim(weight, lax.axis_index("gx") * 128, 128, 1)
     far = lax.ppermute(
         tie(part, from_x), ALL, torus_perm(lambda c, x, y, z: (c, x + (1 if c == 0 else -1), y, z))
     )
-    far = tie(far, from_high, from_low)
+    far = tie(far, first, second)
     far_other = shift(far, core=1)
 
+    rows = call(
+        gather_kernel,
+        pairs[1:] + [("a", v) for v in (blocks, from_x, first, second)],
+        [shape_of(K, PAIRS * ROWS, C)],
+        [pltpu.VMEM((EXT, ROWS, C), BF), pltpu.SemaphoreType.DMA((6,))],
+        pl.CostEstimate(flops=2_000_000_000, bytes_accessed=9_000_000, transcendentals=0),
+    )[0]
     act, grad, keep, send = call(
         forward_kernel,
-        pairs
-        + [("a", v) for v in (blocks, from_x, from_low, from_high, weight, far, far_other)]
-        + [("v", cotan.reshape(NB, ROWS, C))],
+        pairs[:1]
+        + [("v", rows)]
+        + [("a", v) for v in (weight, far, far_other)]
+        + [("h", cotan.reshape(NB, ROWS, C))],
         [
             shape_of(NB, ROWS, C),
             shape_of(NB, ROWS, C),
@@ -316,17 +358,16 @@
             shape_of(16, K, 16, 128),
         ],
         [
-            pltpu.VMEM((EXT, ROWS, C), BF),
             pltpu.VMEM((K, C, C), BF),
-            pltpu.VMEM((K, PAIRS * ROWS, C), BF),
             pltpu.VMEM((NB, ROWS, C), F32),
             pltpu.VMEM((NB, C, ROWS), BF),
-            pltpu.SemaphoreType.DMA((9,)),
+            pltpu.VMEM((NB, ROWS, C), BF),
+            pltpu.SemaphoreType.DMA((4,)),
         ],
-        pl.CostEstimate(flops=7_000_000_000, bytes_accessed=12_000_000, transcendentals=0),
+        pl.CostEstimate(flops=5_000_000_000, bytes_accessed=12_000_000, transcendentals=0),
     )
     got = shift(send, core=1)
-    local, back_x, to_low, to_high = call(
+    local, back_x, to_first, to_second = call(
         backward_kernel,
         pairs
         + [("v", grad)]
@@ -340,25 +381,24 @@
         ],
         pl.CostEstimate(flops=5_000_000_000, bytes_accessed=10_000_000, transcendentals=0),
     )
-    paired = (tie(keep, to_low).astype(F32) + got.astype(F32)).astype(BF)
+    paired = (tie(keep, to_first).astype(F32) + got.astype(F32)).astype(BF)
     spread = exchange(paired, lambda c, x, y, z: (c, z))
-    return_high = grid_shift(tie(to_low, spread), 0, -1)
-    return_low = grid_shift(tie(to_high, spread), 0, 1)
-    sum_xy = jnp.sum(spread.astype(F32), 0)
-    padded = jnp.concatenate([sum_xy, jnp.zeros((KPAD - K, 16, 128), F32)], 0)
-    spread = exchange(padded.astype(BF).reshape(8, 4, 16, 128), lambda c, x, y, z: (c, x, y))
-    sum_z = jnp.sum(spread.astype(F32), 0).astype(BF)
-    all_x = exchange(jnp.broadcast_to(sum_z, (16, 4, 16, 128)), lambda c, x, y, z: (c, x % 2, y))
+    first = swap_y(tie(to_first, spread), 0)
+    second = swap_y(tie(to_second, spread), 1)
+    plane = call(plane_kernel, [("v", spread)], [shape_of(8, 4, 16, 128)])[0]
+    spread = exchange(plane, lambda c, x, y, z: (c, x, y))
+    depth = call(depth_kernel, [("v", spread)], [shape_of(16, 4, 16, 128)])[0]
+    all_x = exchange(depth, lambda c, x, y, z: (c, x % 2, y))
     all_x = all_x.reshape(2, KPAD, 16, 128)[:, :K]
-    back_x = lax.dynamic_update_slice(back_x, return_low[4:5], (4, 0, 0))
-    back_x = lax.dynamic_update_slice(back_x, return_high[4:5], (5, 0, 0))
-    return_x = grid_shift(back_x, 1, 0)
+    back_x = lax.dynamic_update_slice(back_x, first[4:5], (4, 0, 0))
+    back_x = lax.dynamic_update_slice(back_x, second[4:5], (5, 0, 0))
+    return_x = shift(back_x, core=1)
     mine = [all_x] + [shift(all_x, y=s) for s in range(1, 4)]
-    other = [shift(tie(piece, return_low, return_high), core=1) for piece in mine]
+    other = [shift(tie(piece, first, second), core=1) for piece in mine]
 
     input_grad = call(
         input_kernel,
-        lists + [("v", v) for v in (local, return_x, return_low, return_high)],
+        lists + [("v", v) for v in (local, return_x, first, second)],
         [shape_of(NB, ROWS, C)],
         [pltpu.VMEM((NB, ROWS, C), F32)],
     )[0]

time: 140 us -> 136 us (0.971)
  local copies, waits for them, and re-layouts: 7.75 us -> 3.7 us
  Pallas kernels: 20.9 us -> 23.4 us
  starting transfers between devices: 47.4 us -> 45.3 us
  other arithmetic: 2.26 us -> 0.46 us
    ppermute x6 -> x4, starting transfers between devices: 18.8 us -> 8.29 us  [swap_y(): return lax.ppermute(value, ALL, pairs)]
    ppermute x9 -> x11, starting transfers between devices: 16.3 us -> 24.5 us  [shift(): return lax.ppermute(value, ALL, torus_perm(move))]
    pallas_call x4 -> x7, Pallas kernels: 17.8 us -> 20.3 us  [call(): pl.pallas_call(kernel, out_shape=[out for _, out in outs], in_specs=[plac...]
    all_to_all x2, waiting for transfers between devices: 12.4 us -> 14.8 us  [exchange(): lax.all_to_all(value, ALL, split_axis=0, concat_axis=0, axis_index_groups...]
    ppermute x9 -> x11, waiting for transfers between devices: 4.92 us -> 2.62 us  [shift(): return lax.ppermute(value, ALL, torus_perm(move))]
    unnamed x30 -> x22, local copies, waits for them, and re-layouts: 4.41 us -> 2.41 us
    reduce_sum x2 -> x0, other arithmetic: 1.8 us -> none  [the longest x1 1.78 us: body(): sum_xy = jnp.sum(spread.astype(F32), 0)]
    ppermute x6 -> x4, waiting for transfers between devices: 15 us -> 15.1 us  [swap_y(): return lax.ppermute(value, ALL, pairs)]
  transfers between devices with their start and end apart: 18 -> 18, of which waited for: 10 -> 7; matrix products, arithmetic and copies ran while one was open for 2% -> 1% of each run, Pallas kernels for 6% -> 9%
where the time goes in v4:
time: 136 us; the launch traced here: 134 us
  starting transfers between devices  45.3 us (33%)
  waiting for transfers between devices  33.4 us (25%)
  blocking collectives  27 us (20%)
  Pallas kernels  23.4 us (17%)
  local copies, waits for them, and re-layouts  3.7 us (3%)
    all_to_all x1, blocking collectives, exchange(): lax.all_to_all(value, ALL, split_axis=0, concat_axis=0, axis_index_groups...  27 us
    ppermute x11, starting transfers between devices, shift(): return lax.ppermute(value, ALL, torus_perm(move))  24.5 us
    pallas_call x7, Pallas kernels, call(): pl.pallas_call(kernel, out_shape=[out for _, out in outs], in_specs=[plac...  20.3 us
    ppermute x4, waiting for transfers between devices, swap_y(): return lax.ppermute(value, ALL, pairs)  15.1 us
    all_to_all x2, waiting for transfers between devices, exchange(): lax.all_to_all(value, ALL, split_axis=0, concat_axis=0, axis_index_groups...  14.8 us
    all_to_all x2, starting transfers between devices, exchange(): lax.all_to_all(value, ALL, split_axis=0, concat_axis=0, axis_index_groups...  11.7 us
    ppermute x4, starting transfers between devices, swap_y(): return lax.ppermute(value, ALL, pairs)  8.29 us
    pallas_call x1, Pallas kernels, body(): pl.pallas_call(functools.partial(final_kernel, scale), grid=(3,), out_sha...  3.12 us
  transfers between devices with their start and end apart: 18, of which 7 were waited for; matrix products, arithmetic and copies ran while one was open for 1% of the time, Pallas kernels for 9%

profile of v4, /device:TPU:1, one launch (start us, length us, event | category | flops | bytes accessed | tf_op | source)
XLA Modules:
  0.0 134.2 jit_solution(10934765898430033260)
XLA Ops:
  0.7 1.0 copy-done
  1.7 0.7 copy-done.4
  2.4 0.7 copy-done.7
  3.0 0.7 shard_map.103
  3.7 3.3 %collective-permute-start = (bf16[6,128,256]{2,1,0:T(8,128)(2,1)S(1)}, bf16[6,128,256]{2,1,0:T(8,128)(2,1)S(1)}, u32[]{:S(2)}, u32[]{:S(2)}) collective-permute-start(bf16[6,128,256]{2,1,0:T(8,128)(2,1)S(1)} %get-tuple-element.23), channel_id=1, source_target_pairs={{0,128},{1,129},{2,130},{3,131},{4,132},{5,133},{6,134},{7,135},{8... | collective-permute-start | bytes 1179656 | tf_op jit(solution)/shard_map/ppermute | solution.py:75
  7.0 1.3 constant_dynamic-slice_fusion
  8.3 0.1 collective-permute-done.from_x
  8.4 0.7 collective-permute-start.3
  9.1 0.7 collective-permute-start.2
  9.8 5.3 %collective-permute-start.1 = (bf16[5,128,256]{2,1,0:T(8,128)(2,1)S(1)}, bf16[5,128,256]{2,1,0:T(8,128)(2,1)S(1)}, u32[]{:S(2)}, u32[]{:S(2)}) collective-permute-start(bf16[5,128,256]{2,1,0:T(8,128)(2,1)S(1)} %get-tuple-element.44), channel_id=1, source_target_pairs={{0,2},{1,3},{128,130},{129,131},{2,0},{3,1},{130,128},{131,129},{4... | collective-permute-start | bytes 983048 | tf_op jit(solution)/shard_map/ppermute | solution.py:84
  15.1 0.0 collective-permute-done.2.second
  15.1 15.0 %collective-permute-done.1.first = bf16[5,128,256]{2,1,0:T(8,128)(2,1)S(1)} collective-permute-done((bf16[5,128,256]{2,1,0:T(8,128)(2,1)S(1)}, bf16[5,128,256]{2,1,0:T(8,128)(2,1)S(1)}, u32[]{:S(2)}, u32[]{:S(2)}) %collective-permute-start.1) | collective-permute-done | bytes 327712 | tf_op jit(solution)/shard_map/ppermute | solution.py:84
  30.2 0.9 collective-permute-done.3.far
  31.1 5.9 %collective-permute-start.4 = (bf16[27,128,128]{2,1,0:T(8,128)(2,1)S(1)}, bf16[27,128,128]{2,1,0:T(8,128)(2,1)S(1)}, u32[]{:S(2)}, u32[]{:S(2)}) collective-permute-start(bf16[27,128,128]{2,1,0:T(8,128)(2,1)S(1)} %collective-permute-done.3.far), channel_id=1, source_target_pairs={{0,128},{1,129},{2,130},{3,131},{4,132},{5,133},{6,134},{7,135},{8... | collective-permute-start | bytes 2654216 | tf_op jit(solution)/shard_map/ppermute | solution.py:75
  37.1 0.0 copy-start.9
  37.1 0.0 copy-start.10
  37.1 3.0 %shard_map.104.rows = bf16[27,512,256]{2,1,0:T(8,128)(2,1)S(1)} custom-call(s32[1,4,27]{2,1,0:T(4,128)S(1)} %bitcast.13, s32[27,4,128]{2,1,0:T(4,128)S(1)} %bitcast.11, bf16[8,128,256]{2,1,0:T(8,128)(2,1)S(1)} %bitcast.10, bf16[6,128,256]{2,1,0:T(8,128)(2,1)S(1)} %collective-permute-done.from_x, bf16[5,128,256]{2,1,0:T(8,128)(2,1)S(1)} %collective-permute-done.1.first, ...), custom_call_target="tpu_custom_call" | custom-call | flops 2000000000 | bytes 9000000 | tf_op jit(solution)/shard_map/pallas_call | solution.py:32
  40.1 0.0 collective-permute-done.4.far_other
  40.1 7.2 %shard_map.105 = (bf16[8,128,256]{2,1,0:T(8,128)(2,1)}, bf16[8,128,256]{2,1,0:T(8,128)(2,1)S(1)}, bf16[16,27,16,128]{3,2,1,0:T(8,128)(2,1)S(1)}, bf16[16,27,16,128]{3,2,1,0:T(8,128)(2,1)S(1)}) custom-call(s32[1,4,27]{2,1,0:T(4,128)S(1)} %bitcast.18, bf16[27,512,256]{2,1,0:T(8,128)(2,1)S(1)} %shard_map.104.rows, bf16[27,256,128]{2,1,0:T(8,128)(2,1)S(1)} %copy-done.2, ...), custom_call_target="tpu_custom_call" | custom-call | flops 5000000000 | bytes 12000000 | tf_op jit(solution)/shard_map/pallas_call | solution.py:32
  47.3 0.1 collective-permute-start.5
  47.4 6.2 %shard_map.106 = (f32[8,128,256]{2,1,0:T(8,128)S(1)}, bf16[6,128,256]{2,1,0:T(8,128)(2,1)S(1)}, bf16[5,128,256]{2,1,0:T(8,128)(2,1)S(1)}, bf16[5,128,256]{2,1,0:T(8,128)(2,1)S(1)}) custom-call(s32[1,4,27]{2,1,0:T(4,128)S(1)} %bitcast.19, s32[1,4,27]{2,1,0:T(4,128)S(1)} %bitcast.14, s32[27,4,128]{2,1,0:T(4,128)S(1)} %bitcast.12, ...), custom_call_target="tpu_custom_call" | custom-call | flops 5000000000 | bytes 10000000 | tf_op jit(solution)/shard_map/pallas_call | solution.py:32
  53.6 0.0 collective-permute-done.5
  53.6 0.5 add_convert_fusion
  54.1 27.0 %all_to_all.15.spread = bf16[16,27,16,128]{3,2,1,0:T(8,128)(2,1)S(1)} all-to-all(bf16[16,27,16,128]{3,2,1,0:T(8,128)(2,1)S(1)} %add_convert_fusion), channel_id=1, replica_groups={{0,2,1,3,4,6,5,7,8,10,9,11,12,14,13,15},{128,130,129,131,132,134,133,13..., dimensions={0} | all-to-all | bytes 3538944 | tf_op jit(solution)/shard_map/all_to_all | solution.py:319
  81.1 0.9 shard_map.108
  82.0 8.2 %all-to-all-start.1 = ((bf16[8,4,16,128]{3,2,1,0:T(8,128)(2,1)}), bf16[8,4,16,128]{3,2,1,0:T(8,128)(2,1)S(1)}, u32[]{:S(2)}, u32[]{:S(2)}) async-start(bf16[8,4,16,128]{3,2,1,0:T(8,128)(2,1)} %shard_map.108), calls=%async_computation.1 | async-start | bytes 262144 | tf_op jit(solution)/shard_map/all_to_all | solution.py:319
  90.2 1.6 %collective-permute-start.6 = (bf16[5,128,256]{2,1,0:T(8,128)(2,1)S(1)}, bf16[5,128,256]{2,1,0:T(8,128)(2,1)S(1)}, u32[]{:S(2)}, u32[]{:S(2)}) collective-permute-start(bf16[5,128,256]{2,1,0:T(8,128)(2,1)S(1)} %get-tuple-element.36), channel_id=1, source_target_pairs={{0,2},{1,3},{128,130},{129,131},{2,0},{3,1},{130,128},{131,129},{4... | collective-permute-start | bytes 983048 | tf_op jit(solution)/shard_map/ppermute | solution.py:84
  91.8 6.3 %all-to-all-done.1.spread = bf16[8,4,16,128]{3,2,1,0:T(8,128)(2,1)S(1)} async-done(((bf16[8,4,16,128]{3,2,1,0:T(8,128)(2,1)}), bf16[8,4,16,128]{3,2,1,0:T(8,128)(2,1)S(1)}, u32[]{:S(2)}, u32[]{:S(2)}) %all-to-all-start.1) | async-done | bytes 131104 | tf_op jit(solution)/shard_map/all_to_all | solution.py:319
  98.1 0.7 shard_map.109
  98.9 3.5 %all-to-all-start.2 = ((bf16[16,4,16,128]{3,2,1,0:T(8,128)(2,1)}), bf16[16,4,16,128]{3,2,1,0:T(8,128)(2,1)S(1)}, u32[]{:S(2)}, u32[]{:S(2)}) async-start(bf16[16,4,16,128]{3,2,1,0:T(8,128)(2,1)} %shard_map.109), calls=%async_computation.2 | async-start | bytes 524288 | tf_op jit(solution)/shard_map/all_to_all | solution.py:319
  102.4 0.7 collective-permute-start.7
  103.1 0.0 collective-permute-done.6.first
  103.1 8.5 %all-to-all-done.2 = bf16[16,4,16,128]{3,2,1,0:T(8,128)(2,1)S(1)} async-done(((bf16[16,4,16,128]{3,2,1,0:T(8,128)(2,1)}), bf16[16,4,16,128]{3,2,1,0:T(8,128)(2,1)S(1)}, u32[]{:S(2)}, u32[]{:S(2)}) %all-to-all-start.2) | async-done | bytes 262176 | tf_op jit(solution)/shard_map/all_to_all | solution.py:319
  111.7 1.0 collective-permute-start.11
  112.6 1.2 collective-permute-start.10
  113.8 0.3 collective-permute-start.9
  114.1 6.1 %collective-permute-start.8 = (bf16[6,128,256]{2,1,0:T(8,128)(2,1)S(1)}, bf16[6,128,256]{2,1,0:T(8,128)(2,1)S(1)}, u32[]{:S(2)}, u32[]{:S(2)}) collective-permute-start(bf16[6,128,256]{2,1,0:T(8,128)(2,1)S(1)} %slice_dynamic-update-slice_fusion), channel_id=1, source_target_pairs={{0,128},{1,129},{2,130},{3,131},{4,132},{5,133},{6,134},{7,135},{8... | collective-permute-start | bytes 1179656 | tf_op jit(solution)/shard_map/ppermute | solution.py:75
  120.2 0.1 collective-permute-start.12
  120.3 0.0 collective-permute-done.11.refs_3_
  120.3 1.1 collective-permute-done.10.refs_2_
  121.5 1.4 %collective-permute-done.9.refs_1_ = bf16[2,27,16,128]{3,2,1,0:T(8,128)(2,1)S(1)} collective-permute-done((bf16[2,27,16,128]{3,2,1,0:T(8,128)(2,1)S(1)}, bf16[2,27,16,128]{3,2,1,0:T(8,128)(2,1)S(1)}, u32[]{:S(2)}, u32[]{:S(2)}) %collective-permute-start.9) | collective-permute-done | bytes 221216 | tf_op jit(solution)/shard_map/ppermute | solution.py:75
  122.8 6.0 %collective-permute-start.13 = (bf16[2,27,16,128]{3,2,1,0:T(8,128)(2,1)S(1)}, bf16[2,27,16,128]{3,2,1,0:T(8,128)(2,1)S(1)}, u32[]{:S(2)}, u32[]{:S(2)}) collective-permute-start(bf16[2,27,16,128]{3,2,1,0:T(8,128)(2,1)S(1)} %collective-permute-done.9.refs_1_), channel_id=1, source_target_pairs={{0,128},{1,129},{2,130},{3,131},{4,132},{5,133},{6,134},{7,135},{8... | collective-permute-start | bytes 663560 | tf_op jit(solution)/shard_map/ppermute | solution.py:75
  128.8 0.0 collective-permute-start.14
  128.8 0.5 collective-permute-start.15
  129.4 1.7 %shard_map.107 = bf16[8,128,256]{2,1,0:T(8,128)(2,1)} custom-call(s32[1,4,4]{2,1,0:T(4,128)S(1)} %copy-done.5, s32[1,1,4]{2,1,0:T(1,128)S(1)} %bitcast.16, f32[8,128,256]{2,1,0:T(8,128)S(1)} %get-tuple-element.30.local, bf16[6,128,256]{2,1,0:T(8,128)(2,1)S(1)} %collective-permute-done.8.from_x, bf16[5,128,256]{2,1,0:T(8,128)(2,1)S(1)} %collective-permute-done.6.first, ...), custom_call_target="tpu_custom_call" | custom-call | tf_op jit(solution)/shard_map/pallas_call | solution.py:32
  131.0 0.0 collective-permute-done.12.refs_4_
  131.0 0.0 collective-permute-done.13.refs_5_
  131.0 3.1 %shard_map.110 = f32[27,256,128]{2,1,0:T(8,128)} custom-call(bf16[2,27,16,128]{3,2,1,0:T(8,128)(2,1)S(1)} %slice.24.refs_0_, bf16[2,27,16,128]{3,2,1,0:T(8,128)(2,1)S(1)} %collective-permute-done.9.refs_1_, bf16[2,27,16,128]{3,2,1,0:T(8,128)(2,1)S(1)} %collective-permute-done.10.refs_2_, bf16[2,27,16,128]{3,2,1,0:T(8,128)(2,1)S(1)} %collective-permute-done.11.refs_3_, ...), custom_call_target="tpu_custom_call" | custom-call | tf_op jit(solution)/shard_map/pallas_call | solution.py:408
  (25 shorter events, 0.1 us)
Async XLA Ops:
  0.6 36.4 %copy-start.6 = (s32[1,27,4]{1,2,0:T(4,128)S(1)}, s32[1,27,4]{1,2,0:T(4,128)}, u32[]{:S(2)}) copy-start(s32[1,27,4]{1,2,0:T(4,128)} %param.14) | copy-start | bytes 1300
  0.6 1.0 copy-start
  1.7 0.7 copy-start.4
  2.4 0.7 copy-start.7
  3.0 34.0 %copy-start.1 = (bf16[1024,256]{1,0:T(8,128)(2,1)S(1)}, bf16[1024,256]{1,0:T(8,128)(2,1)}, u32[]{:S(2)}) copy-start(bf16[1024,256]{1,0:T(8,128)(2,1)} %param.8) | copy-start | bytes 1572868
  3.0 34.0 %copy-start.3 = (s32[1,27,4,128]{3,2,1,0:T(4,128)S(1)}, s32[1,27,4,128]{3,2,1,0:T(4,128)}, u32[]{:S(2)}) copy-start(s32[1,27,4,128]{3,2,1,0:T(4,128)} %param.15) | copy-start | bytes 165892
  3.7 4.7 %collective-permute-start = (bf16[6,128,256]{2,1,0:T(8,128)(2,1)S(1)}, bf16[6,128,256]{2,1,0:T(8,128)(2,1)S(1)}, u32[]{:S(2)}, u32[]{:S(2)}) collective-permute-start(bf16[6,128,256]{2,1,0:T(8,128)(2,1)S(1)} %get-tuple-element.23), channel_id=1, source_target_pairs={{0,128},{1,129},{2,130},{3,131},{4,132},{5,133},{6,134},{7,135},{8... | collective-permute-start | bytes 1179656 | tf_op jit(solution)/shard_map/ppermute | solution.py:75
  8.4 22.7 %collective-permute-start.3 = (bf16[27,128,128]{2,1,0:T(8,128)(2,1)S(1)}, bf16[27,128,128]{2,1,0:T(8,128)(2,1)S(1)}, u32[]{:S(2)}, u32[]{:S(2)}) collective-permute-start(bf16[27,128,128]{2,1,0:T(8,128)(2,1)S(1)} %constant_dynamic-slice_fusion), channel_id=1, source_target_pairs={{0,1},{1,2},{2,3},{3,0},{4,5},{5,6},{6,7},{7,4},{8,9},{9,10},{10,1... | collective-permute-start | bytes 2654216 | tf_op jit(solution)/shard_map/ppermute | solution.py:335
  9.1 6.0 %collective-permute-start.2 = (bf16[5,128,256]{2,1,0:T(8,128)(2,1)S(1)}, bf16[5,128,256]{2,1,0:T(8,128)(2,1)S(1)}, u32[]{:S(2)}, u32[]{:S(2)}) collective-permute-start(bf16[5,128,256]{2,1,0:T(8,128)(2,1)S(1)} %get-tuple-element.43), channel_id=1, source_target_pairs={{2,4},{3,5},{130,132},{131,133},{4,2},{5,3},{132,130},{133,131},{6... | collective-permute-start | bytes 983048 | tf_op jit(solution)/shard_map/ppermute | solution.py:84
  9.8 20.3 %collective-permute-start.1 = (bf16[5,128,256]{2,1,0:T(8,128)(2,1)S(1)}, bf16[5,128,256]{2,1,0:T(8,128)(2,1)S(1)}, u32[]{:S(2)}, u32[]{:S(2)}) collective-permute-start(bf16[5,128,256]{2,1,0:T(8,128)(2,1)S(1)} %get-tuple-element.44), channel_id=1, source_target_pairs={{0,2},{1,3},{128,130},{129,131},{2,0},{3,1},{130,128},{131,129},{4... | collective-permute-start | bytes 983048 | tf_op jit(solution)/shard_map/ppermute | solution.py:84
  31.1 9.0 %collective-permute-start.4 = (bf16[27,128,128]{2,1,0:T(8,128)(2,1)S(1)}, bf16[27,128,128]{2,1,0:T(8,128)(2,1)S(1)}, u32[]{:S(2)}, u32[]{:S(2)}) collective-permute-start(bf16[27,128,128]{2,1,0:T(8,128)(2,1)S(1)} %collective-permute-done.3.far), channel_id=1, source_target_pairs={{0,128},{1,129},{2,130},{3,131},{4,132},{5,133},{6,134},{7,135},{8... | collective-permute-start | bytes 2654216 | tf_op jit(solution)/shard_map/ppermute | solution.py:75
  37.0 3.0 %copy-start.2 = (bf16[27,256,128]{2,1,0:T(8,128)(2,1)S(1)}, bf16[27,256,128]{2,1,0:T(8,128)(2,1)}, u32[]{:S(2)}) copy-start(bf16[27,256,128]{2,1,0:T(8,128)(2,1)} %own.3) | copy-start | bytes 5308420
  37.1 3.0 %copy-start.9 = (bf16[1024,256]{1,0:T(8,128)(2,1)S(1)}, bf16[1024,256]{1,0:T(8,128)(2,1)}, u32[]{:S(2)}) copy-start(bf16[1024,256]{1,0:T(8,128)(2,1)} %param.10) | copy-start | bytes 1572868
  37.1 3.0 %copy-start.10 = (s32[1,27,4]{1,2,0:T(4,128)S(1)}, s32[1,27,4]{1,2,0:T(4,128)}, u32[]{:S(2)}) copy-start(s32[1,27,4]{1,2,0:T(4,128)} %param.13) | copy-start | bytes 1300
  47.3 6.3 %collective-permute-start.5 = (bf16[16,27,16,128]{3,2,1,0:T(8,128)(2,1)S(1)}, bf16[16,27,16,128]{3,2,1,0:T(8,128)(2,1)S(1)}, u32[]{:S(2)}, u32[]{:S(2)}) collective-permute-start(bf16[16,27,16,128]{3,2,1,0:T(8,128)(2,1)S(1)} %get-tuple-element.35), channel_id=1, source_target_pairs={{0,128},{1,129},{2,130},{3,131},{4,132},{5,133},{6,134},{7,135},{8... | collective-permute-start | bytes 5308424 | tf_op jit(solution)/shard_map/ppermute | solution.py:75
  81.1 48.2 %copy-start.5 = (s32[1,4,4]{2,1,0:T(4,128)S(1)}, s32[1,4,4]{2,1,0:T(4,128)}, u32[]{:S(2)}) copy-start(s32[1,4,4]{2,1,0:T(4,128)} %face.3) | copy-start | bytes 196
  81.1 48.2 %copy-start.8 = (s32[1,4,1]{1,2,0:T(1,128)S(1)}, s32[1,4,1]{1,2,0:T(1,128)}, u32[]{:S(2)}) copy-start(s32[1,4,1]{1,2,0:T(1,128)} %param.12) | copy-start | bytes 52
  82.0 16.1 %all-to-all-start.1 = ((bf16[8,4,16,128]{3,2,1,0:T(8,128)(2,1)}), bf16[8,4,16,128]{3,2,1,0:T(8,128)(2,1)S(1)}, u32[]{:S(2)}, u32[]{:S(2)}) async-start(bf16[8,4,16,128]{3,2,1,0:T(8,128)(2,1)} %shard_map.108), calls=%async_computation.1 | async-start | bytes 262144 | tf_op jit(solution)/shard_map/all_to_all | solution.py:319
  90.2 12.9 %collective-permute-start.6 = (bf16[5,128,256]{2,1,0:T(8,128)(2,1)S(1)}, bf16[5,128,256]{2,1,0:T(8,128)(2,1)S(1)}, u32[]{:S(2)}, u32[]{:S(2)}) collective-permute-start(bf16[5,128,256]{2,1,0:T(8,128)(2,1)S(1)} %get-tuple-element.36), channel_id=1, source_target_pairs={{0,2},{1,3},{128,130},{129,131},{2,0},{3,1},{130,128},{131,129},{4... | collective-permute-start | bytes 983048 | tf_op jit(solution)/shard_map/ppermute | solution.py:84
  98.9 12.8 %all-to-all-start.2 = ((bf16[16,4,16,128]{3,2,1,0:T(8,128)(2,1)}), bf16[16,4,16,128]{3,2,1,0:T(8,128)(2,1)S(1)}, u32[]{:S(2)}, u32[]{:S(2)}) async-start(bf16[16,4,16,128]{3,2,1,0:T(8,128)(2,1)} %shard_map.109), calls=%async_computation.2 | async-start | bytes 524288 | tf_op jit(solution)/shard_map/all_to_all | solution.py:319
  102.4 11.7 %collective-permute-start.7 = (bf16[5,128,256]{2,1,0:T(8,128)(2,1)S(1)}, bf16[5,128,256]{2,1,0:T(8,128)(2,1)S(1)}, u32[]{:S(2)}, u32[]{:S(2)}) collective-permute-start(bf16[5,128,256]{2,1,0:T(8,128)(2,1)S(1)} %get-tuple-element.38), channel_id=1, source_target_pairs={{2,4},{3,5},{130,132},{131,133},{4,2},{5,3},{132,130},{133,131},{6... | collective-permute-start | bytes 983048 | tf_op jit(solution)/shard_map/ppermute | solution.py:84
  111.7 8.7 %collective-permute-start.11 = (bf16[2,27,16,128]{3,2,1,0:T(8,128)(2,1)S(1)}, bf16[2,27,16,128]{3,2,1,0:T(8,128)(2,1)S(1)}, u32[]{:S(2)}, u32[]{:S(2)}) collective-permute-start(bf16[2,27,16,128]{3,2,1,0:T(8,128)(2,1)S(1)} %slice.24.refs_0_), channel_id=1, source_target_pairs={{0,12},{1,13},{2,14},{3,15},{4,0},{5,1},{6,2},{7,3},{8,4},{9,5},{1... | collective-permute-start | bytes 663560 | tf_op jit(solution)/shard_map/ppermute | solution.py:75
  112.6 8.8 %collective-permute-start.10 = (bf16[2,27,16,128]{3,2,1,0:T(8,128)(2,1)S(1)}, bf16[2,27,16,128]{3,2,1,0:T(8,128)(2,1)S(1)}, u32[]{:S(2)}, u32[]{:S(2)}) collective-permute-start(bf16[2,27,16,128]{3,2,1,0:T(8,128)(2,1)S(1)} %slice.24.refs_0_), channel_id=1, source_target_pairs={{0,8},{1,9},{2,10},{3,11},{4,12},{5,13},{6,14},{7,15},{8,0},{9,1},... | collective-permute-start | bytes 663560 | tf_op jit(solution)/shard_map/ppermute | solution.py:75
  113.8 9.0 %collective-permute-start.9 = (bf16[2,27,16,128]{3,2,1,0:T(8,128)(2,1)S(1)}, bf16[2,27,16,128]{3,2,1,0:T(8,128)(2,1)S(1)}, u32[]{:S(2)}, u32[]{:S(2)}) collective-permute-start(bf16[2,27,16,128]{3,2,1,0:T(8,128)(2,1)S(1)} %slice.24.refs_0_), channel_id=1, source_target_pairs={{0,4},{1,5},{2,6},{3,7},{4,8},{5,9},{6,10},{7,11},{8,12},{9,13},{1... | collective-permute-start | bytes 663560 | tf_op jit(solution)/shard_map/ppermute | solution.py:75
  114.1 15.2 %collective-permute-start.8 = (bf16[6,128,256]{2,1,0:T(8,128)(2,1)S(1)}, bf16[6,128,256]{2,1,0:T(8,128)(2,1)S(1)}, u32[]{:S(2)}, u32[]{:S(2)}) collective-permute-start(bf16[6,128,256]{2,1,0:T(8,128)(2,1)S(1)} %slice_dynamic-update-slice_fusion), channel_id=1, source_target_pairs={{0,128},{1,129},{2,130},{3,131},{4,132},{5,133},{6,134},{7,135},{8... | collective-permute-start | bytes 1179656 | tf_op jit(solution)/shard_map/ppermute | solution.py:75
  120.2 10.8 %collective-permute-start.12 = (bf16[2,27,16,128]{3,2,1,0:T(8,128)(2,1)S(1)}, bf16[2,27,16,128]{3,2,1,0:T(8,128)(2,1)S(1)}, u32[]{:S(2)}, u32[]{:S(2)}) collective-permute-start(bf16[2,27,16,128]{3,2,1,0:T(8,128)(2,1)S(1)} %slice.24.refs_0_), channel_id=1, source_target_pairs={{0,128},{1,129},{2,130},{3,131},{4,132},{5,133},{6,134},{7,135},{8... | collective-permute-start | bytes 663560 | tf_op jit(solution)/shard_map/ppermute | solution.py:75
  122.8 8.2 %collective-permute-start.13 = (bf16[2,27,16,128]{3,2,1,0:T(8,128)(2,1)S(1)}, bf16[2,27,16,128]{3,2,1,0:T(8,128)(2,1)S(1)}, u32[]{:S(2)}, u32[]{:S(2)}) collective-permute-start(bf16[2,27,16,128]{3,2,1,0:T(8,128)(2,1)S(1)} %collective-permute-done.9.refs_1_), channel_id=1, source_target_pairs={{0,128},{1,129},{2,130},{3,131},{4,132},{5,133},{6,134},{7,135},{8... | collective-permute-start | bytes 663560 | tf_op jit(solution)/shard_map/ppermute | solution.py:75
  128.8 2.2 %collective-permute-start.14 = (bf16[2,27,16,128]{3,2,1,0:T(8,128)(2,1)S(1)}, bf16[2,27,16,128]{3,2,1,0:T(8,128)(2,1)S(1)}, u32[]{:S(2)}, u32[]{:S(2)}) collective-permute-start(bf16[2,27,16,128]{3,2,1,0:T(8,128)(2,1)S(1)} %collective-permute-done.10.refs_2_), channel_id=1, source_target_pairs={{0,128},{1,129},{2,130},{3,131},{4,132},{5,133},{6,134},{7,135},{8... | collective-permute-start | bytes 663560 | tf_op jit(solution)/shard_map/ppermute | solution.py:75
  128.8 2.2 %collective-permute-start.15 = (bf16[2,27,16,128]{3,2,1,0:T(8,128)(2,1)S(1)}, bf16[2,27,16,128]{3,2,1,0:T(8,128)(2,1)S(1)}, u32[]{:S(2)}, u32[]{:S(2)}) collective-permute-start(bf16[2,27,16,128]{3,2,1,0:T(8,128)(2,1)S(1)} %collective-permute-done.11.refs_3_), channel_id=1, source_target_pairs={{0,128},{1,129},{2,130},{3,131},{4,132},{5,133},{6,134},{7,135},{8... | collective-permute-start | bytes 663560 | tf_op jit(solution)/shard_map/ppermute | solution.py:75

commit v5 on v4

--- a/solution.py
+++ b/solution.py
@@ -100,25 +100,14 @@
     second[4] = face_x[5]
 
 
-def weight_copies(core, side, own, far, far_other, full, sems):
-    near_rows = pl.ds(pl.multiple_of(core * 128, 128), 128)
-    other_rows = pl.ds(pl.multiple_of((1 - core) * 128, 128), 128)
-    mine = slice(side * 128, side * 128 + 128)
-    theirs = slice(128 - side * 128, 256 - side * 128)
-    return (
-        pltpu.make_async_copy(own, full.at[:, :, mine], sems.at[0]),
-        pltpu.make_async_copy(far, full.at[:, near_rows, theirs], sems.at[1]),
-        pltpu.make_async_copy(far_other, full.at[:, other_rows, theirs], sems.at[2]),
-    )
-
-
-def on_weights(act, core, rep, *refs):
-    for side in range(2):
-
-        @pl.when(rep == side)
-        def _():
-            for copy in weight_copies(core, side, *refs):
-                getattr(copy, act)()
+def weight_of(k, core, rep, y_at, own, near, other):
+    ours = [near[(y_at - y) & 3, k] for y in range(4)]
+    theirs = [other[(y_at - y) & 3, k] for y in range(4)]
+    ours, theirs = jnp.concatenate(ours, 0), jnp.concatenate(theirs, 0)
+    first, second = jnp.where(core == 0, ours, theirs), jnp.where(core == 0, theirs, ours)
+    mine, far = own[k], jnp.concatenate([first, second], 0)
+    low, high = jnp.where(rep == 0, mine, far), jnp.where(rep == 0, far, mine)
+    return jnp.concatenate([low, high], 1)
 
 
 def gather_kernel(ins, maps, feats, from_x, first, second, rows, ext, sems):
@@ -154,20 +143,18 @@
 
 
 def forward_kernel(
-    outs, rows, own, far, far_other, cotan_in,
+    outs, rows, own, near, other, cotan_in,
     act, grad, keep, send,
-    full, acc, flipped, cotan, sems,
+    acc, flipped, cotan, sem,
 ):
-    core, rep = places()[:2]
-    weights = (own, far, far_other, full, sems)
-    on_weights("start", core, rep, *weights)
-    cotan_copy = pltpu.make_async_copy(cotan_in, cotan, sems.at[3])
+    core, rep, _, y_at, _ = places()
+    cotan_copy = pltpu.make_async_copy(cotan_in, cotan, sem)
     cotan_copy.start()
     acc[...] = jnp.zeros_like(acc)
-    on_weights("wait", core, rep, *weights)
 
     def product_step(k, carry):
-        product = jnp.dot(rows[k], full[k], preferred_element_type=F32)
+        full = weight_of(k, core, rep, y_at, own, near, other)
+        product = jnp.dot(rows[k], full, preferred_element_type=F32)
         for p in range(PAIRS):
             acc[outs[0, p, k]] += product[p * ROWS : (p + 1) * ROWS]
         return carry
@@ -206,13 +193,11 @@
 
 
 def backward_kernel(
-    outs, ins, maps, grad, own, far, far_other,
+    outs, ins, maps, grad, own, near, other,
     local, face_x, first, second,
-    full, rows, acc, sems,
+    rows, acc,
 ):
-    core, rep = places()[:2]
-    weights = (own, far, far_other, full, sems)
-    on_weights("start", core, rep, *weights)
+    core, rep, _, y_at, _ = places()
     acc[...] = jnp.zeros_like(acc)
     lanes = lax.broadcasted_iota(jnp.int32, (ROWS, ROWS), 0)
 
@@ -225,11 +210,11 @@
         return carry
 
     lax.fori_loop(0, K, spread_step, 0, unroll=27)
-    on_weights("wait", core, rep, *weights)
 
     def step(k, carry):
+        full = weight_of(k, core, rep, y_at, own, near, other)
         product = lax.dot_general(
-            rows[k], full[k], (((1,), (1,)), ((), ())), preferred_element_type=F32
+            rows[k], full, (((1,), (1,)), ((), ())), preferred_element_type=F32
         )
         for p in range(PAIRS):
             acc[ins[0, p, k]] += product[p * ROWS : (p + 1) * ROWS]
@@ -289,12 +274,12 @@
             for side in range(2):
                 halves = []
                 for x in range(2):
-                    pieces = [refs[side * 4 + (turn - y) % 4][x, k].astype(F32) for y in range(4)]
+                    pieces = [refs[side * 4 + (turn - y) % 4][x, k] for y in range(4)]
                     halves.append(jnp.concatenate(pieces, 0))
-                sides.append(jnp.concatenate(halves, 1) * scale)
+                sides.append(jnp.concatenate(halves, 1))
             low = jnp.where(core == 0, sides[0], sides[1])
             high = jnp.where(core == 0, sides[1], sides[0])
-            out[n] = jnp.concatenate([low, high], 0).T
+            out[n] = jnp.concatenate([low, high], 0).T.astype(F32) * scale
             return carry
 
         lax.fori_loop(0, 9, step, 0, unroll=3)
@@ -331,12 +316,13 @@
     from_x = shift(face_x, core=1)
     first = swap_y(lax.dynamic_update_slice(first, from_x[4:5], (4, 0, 0)), 0)
     second = swap_y(lax.dynamic_update_slice(second, from_x[5:6], (4, 0, 0)), 1)
-    part = lax.dynamic_slice_in_dim(weight, lax.axis_index("gx") * 128, 128, 1)
+    row = lax.axis_index("gx") * 128 + places()[3] * 32
+    part = lax.dynamic_slice_in_dim(weight, row, 32, 1)
     far = lax.ppermute(
-        tie(part, from_x), ALL, torus_perm(lambda c, x, y, z: (c, x + (1 if c == 0 else -1), y, z))
+        part, ALL, torus_perm(lambda c, x, y, z: (c, x + (1 if c == 0 else -1), y, z))
     )
-    far = tie(far, first, second)
-    far_other = shift(far, core=1)
+    near = jnp.stack([far] + [tie(shift(far, y=s), first, second) for s in range(1, 4)], 0)
+    other = shift(near, core=1)
 
     rows = call(
         gather_kernel,
@@ -349,7 +335,7 @@
         forward_kernel,
         pairs[:1]
         + [("v", rows)]
-        + [("a", v) for v in (weight, far, far_other)]
+        + [("v", v) for v in (weight, near, other)]
         + [("h", cotan.reshape(NB, ROWS, C))],
         [
             shape_of(NB, ROWS, C),
@@ -358,11 +344,10 @@
             shape_of(16, K, 16, 128),
         ],
         [
-            pltpu.VMEM((K, C, C), BF),
             pltpu.VMEM((NB, ROWS, C), F32),
             pltpu.VMEM((NB, C, ROWS), BF),
             pltpu.VMEM((NB, ROWS, C), BF),
-            pltpu.SemaphoreType.DMA((4,)),
+            pltpu.SemaphoreType.DMA,
         ],
         pl.CostEstimate(flops=5_000_000_000, bytes_accessed=12_000_000, transcendentals=0),
     )
@@ -371,13 +356,11 @@
         backward_kernel,
         pairs
         + [("v", grad)]
-        + [("a", v) for v in (weight, far, far_other)],
+        + [("v", v) for v in (weight, near, other)],
         [shape_of(NB, ROWS, C, dtype=F32), six, five, five],
         [
-            pltpu.VMEM((K, C, C), BF),
             pltpu.VMEM((K, PAIRS * ROWS, C), BF),
             pltpu.VMEM((EXT, ROWS, C), F32),
-            pltpu.SemaphoreType.DMA((3,)),
         ],
         pl.CostEstimate(flops=5_000_000_000, bytes_accessed=10_000_000, transcendentals=0),
     )
@@ -394,14 +377,14 @@
     back_x = lax.dynamic_update_slice(back_x, second[4:5], (5, 0, 0))
     return_x = shift(back_x, core=1)
     mine = [all_x] + [shift(all_x, y=s) for s in range(1, 4)]
-    other = [shift(tie(piece, first, second), core=1) for piece in mine]
-
     input_grad = call(
         input_kernel,
         lists + [("v", v) for v in (local, return_x, first, second)],
         [shape_of(NB, ROWS, C)],
         [pltpu.VMEM((NB, ROWS, C), F32)],
     )[0]
+    other = [shift(piece, core=1) for piece in mine[:3]]
+    other.append(shift(tie(mine[3], input_grad), core=1))
     tiles = lax.axis_size("gx") * lax.axis_size("gy") * lax.axis_size("rep")
     scale = float((tiles * PAIRS * ROWS) ** (-0.5))
     pieces = mine + other

time: 136 us -> 133 us (0.978)
  waiting for transfers between devices: 33.4 us -> 27.4 us
  blocking collectives: 27 us -> 30.9 us
  starting transfers between devices: 45.3 us -> 47.1 us
    ppermute x4, waiting for transfers between devices: 15.1 us -> 2.22 us  [swap_y(): return lax.ppermute(value, ALL, pairs)]
    ppermute x11 -> x14, waiting for transfers between devices: 2.62 us -> 12.1 us  [shift(): return lax.ppermute(value, ALL, torus_perm(move))]
    all_to_all x1, blocking collectives: 27 us -> 30.9 us  [exchange(): lax.all_to_all(value, ALL, split_axis=0, concat_axis=0, axis_index_groups...]
    ppermute x11 -> x14, starting transfers between devices: 24.5 us -> 26.3 us  [shift(): return lax.ppermute(value, ALL, torus_perm(move))]
    all_to_all x2, waiting for transfers between devices: 14.8 us -> 13.1 us  [exchange(): lax.all_to_all(value, ALL, split_axis=0, concat_axis=0, axis_index_groups...]
  transfers between devices with their start and end apart: 18 -> 21, of which waited for: 7 -> 8; matrix products, arithmetic and copies ran while one was open for 1% -> 1% of each run, Pallas kernels for 9% -> 9%
where the time goes in v5:
time: 133 us; the launch traced here: 132 us
  starting transfers between devices  47.1 us (35%)
  blocking collectives  30.9 us (23%)
  waiting for transfers between devices  27.4 us (21%)
  Pallas kernels  22.1 us (17%)
  local copies, waits for them, and re-layouts  3.4 us (3%)
    all_to_all x1, blocking collectives, exchange(): lax.all_to_all(value, ALL, split_axis=0, concat_axis=0, axis_index_groups...  30.9 us
    ppermute x14, starting transfers between devices, shift(): return lax.ppermute(value, ALL, torus_perm(move))  26.3 us
    pallas_call x7, Pallas kernels, call(): pl.pallas_call(kernel, out_shape=[out for _, out in outs], in_specs=[plac...  19.3 us
    all_to_all x2, waiting for transfers between devices, exchange(): lax.all_to_all(value, ALL, split_axis=0, concat_axis=0, axis_index_groups...  13.1 us
    ppermute x14, waiting for transfers between devices, shift(): return lax.ppermute(value, ALL, torus_perm(move))  12.1 us
    all_to_all x2, starting transfers between devices, exchange(): lax.all_to_all(value, ALL, split_axis=0, concat_axis=0, axis_index_groups...  11.7 us
    ppermute x4, starting transfers between devices, swap_y(): return lax.ppermute(value, ALL, pairs)  8.28 us
    pallas_call x1, Pallas kernels, body(): pl.pallas_call(functools.partial(final_kernel, scale), grid=(3,), out_sha...  2.73 us
  transfers between devices with their start and end apart: 21, of which 8 were waited for; matrix products, arithmetic and copies ran while one was open for 1% of the time, Pallas kernels for 9%

profile of v5, /device:TPU:1, one launch (start us, length us, event | category | flops | bytes accessed | tf_op | source)
XLA Modules:
  0.0 132.3 jit_solution(11399448717828825118)
XLA Ops:
  0.7 1.0 copy-done
  1.7 0.7 copy-done.4
  2.4 0.7 copy-done.7
  3.0 0.7 shard_map.103
  3.7 3.3 %collective-permute-start = (bf16[6,128,256]{2,1,0:T(8,128)(2,1)S(1)}, bf16[6,128,256]{2,1,0:T(8,128)(2,1)S(1)}, u32[]{:S(2)}, u32[]{:S(2)}) collective-permute-start(bf16[6,128,256]{2,1,0:T(8,128)(2,1)S(1)} %get-tuple-element.21), channel_id=1, source_target_pairs={{0,128},{1,129},{2,130},{3,131},{4,132},{5,133},{6,134},{7,135},{8... | collective-permute-start | bytes 1179656 | tf_op jit(solution)/shard_map/ppermute | solution.py:75
  7.0 1.0 constant_dynamic-slice_fusion
  8.0 0.8 collective-permute-start.3
  8.8 0.7 collective-permute-start.2
  9.5 5.3 %collective-permute-start.1 = (bf16[5,128,256]{2,1,0:T(8,128)(2,1)S(1)}, bf16[5,128,256]{2,1,0:T(8,128)(2,1)S(1)}, u32[]{:S(2)}, u32[]{:S(2)}) collective-permute-start(bf16[5,128,256]{2,1,0:T(8,128)(2,1)S(1)} %get-tuple-element.40), channel_id=1, source_target_pairs={{0,2},{1,3},{128,130},{129,131},{2,0},{3,1},{130,128},{131,129},{4... | collective-permute-start | bytes 983048 | tf_op jit(solution)/shard_map/ppermute | solution.py:84
  14.8 2.7 %collective-permute-start.6 = (bf16[27,32,128]{2,1,0:T(8,128)(2,1)S(1)}, bf16[27,32,128]{2,1,0:T(8,128)(2,1)S(1)}, u32[]{:S(2)}, u32[]{:S(2)}) collective-permute-start(bf16[27,32,128]{2,1,0:T(8,128)(2,1)S(1)} %collective-permute-done.3), channel_id=1, source_target_pairs={{0,12},{1,13},{2,14},{3,15},{4,0},{5,1},{6,2},{7,3},{8,4},{9,5},{1... | collective-permute-start | bytes 663560 | tf_op jit(solution)/shard_map/ppermute | solution.py:75
  17.5 0.3 collective-permute-start.5
  17.9 0.4 collective-permute-start.4
  18.3 9.0 %collective-permute-done.6 = bf16[27,32,128]{2,1,0:T(8,128)(2,1)S(1)} collective-permute-done((bf16[27,32,128]{2,1,0:T(8,128)(2,1)S(1)}, bf16[27,32,128]{2,1,0:T(8,128)(2,1)S(1)}, u32[]{:S(2)}, u32[]{:S(2)}) %collective-permute-start.6) | collective-permute-done | bytes 221216 | tf_op jit(solution)/shard_map/ppermute | solution.py:75
  27.3 0.0 collective-permute-done.2.second
  27.3 2.2 %collective-permute-done.1.first = bf16[5,128,256]{2,1,0:T(8,128)(2,1)S(1)} collective-permute-done((bf16[5,128,256]{2,1,0:T(8,128)(2,1)S(1)}, bf16[5,128,256]{2,1,0:T(8,128)(2,1)S(1)}, u32[]{:S(2)}, u32[]{:S(2)}) %collective-permute-start.1) | collective-permute-done | bytes 327712 | tf_op jit(solution)/shard_map/ppermute | solution.py:84
  29.5 0.1 collective-permute-done.5
  29.6 1.5 %collective-permute-done.4 = bf16[27,32,128]{2,1,0:T(8,128)(2,1)S(1)} collective-permute-done((bf16[27,32,128]{2,1,0:T(8,128)(2,1)S(1)}, bf16[27,32,128]{2,1,0:T(8,128)(2,1)S(1)}, u32[]{:S(2)}, u32[]{:S(2)}) %collective-permute-start.4) | collective-permute-done | bytes 221216 | tf_op jit(solution)/shard_map/ppermute | solution.py:75
  31.1 0.1 pad_maximum_fusion.near
  31.2 0.7 collective-permute-start.7
  31.9 0.0 copy-start.9
  31.9 0.0 copy-start.10
  31.9 3.0 %shard_map.104.rows = bf16[27,512,256]{2,1,0:T(8,128)(2,1)S(1)} custom-call(s32[1,4,27]{2,1,0:T(4,128)S(1)} %bitcast.17, s32[27,4,128]{2,1,0:T(4,128)S(1)} %bitcast.15, bf16[8,128,256]{2,1,0:T(8,128)(2,1)S(1)} %bitcast.14, bf16[6,128,256]{2,1,0:T(8,128)(2,1)S(1)} %collective-permute-done.from_x, bf16[5,128,256]{2,1,0:T(8,128)(2,1)S(1)} %collective-permute-done.1.first, ...), custom_call_target="tpu_custom_call" | custom-call | flops 2000000000 | bytes 9000000 | tf_op jit(solution)/shard_map/pallas_call | solution.py:32
  34.9 0.0 collective-permute-done.7.other
  35.0 6.7 %shard_map.105 = (bf16[8,128,256]{2,1,0:T(8,128)(2,1)}, bf16[8,128,256]{2,1,0:T(8,128)(2,1)S(1)}, bf16[16,27,16,128]{3,2,1,0:T(8,128)(2,1)S(1)}, bf16[16,27,16,128]{3,2,1,0:T(8,128)(2,1)S(1)}) custom-call(s32[1,4,27]{2,1,0:T(4,128)S(1)} %bitcast.22, bf16[27,512,256]{2,1,0:T(8,128)(2,1)S(1)} %shard_map.104.rows, bf16[27,256,128]{2,1,0:T(8,128)(2,1)S(1)} %copy-done.3, ...), custom_call_target="tpu_custom_call" | custom-call | flops 5000000000 | bytes 12000000 | tf_op jit(solution)/shard_map/pallas_call | solution.py:32
  41.7 0.3 collective-permute-start.8
  42.0 5.7 %shard_map.106 = (f32[8,128,256]{2,1,0:T(8,128)S(1)}, bf16[6,128,256]{2,1,0:T(8,128)(2,1)S(1)}, bf16[5,128,256]{2,1,0:T(8,128)(2,1)S(1)}, bf16[5,128,256]{2,1,0:T(8,128)(2,1)S(1)}) custom-call(s32[1,4,27]{2,1,0:T(4,128)S(1)} %bitcast.23, s32[1,4,27]{2,1,0:T(4,128)S(1)} %bitcast.18, s32[27,4,128]{2,1,0:T(4,128)S(1)} %bitcast.16, ...), custom_call_target="tpu_custom_call" | custom-call | flops 5000000000 | bytes 10000000 | tf_op jit(solution)/shard_map/pallas_call | solution.py:32
  47.7 0.5 add_convert_fusion
  48.2 30.9 %all_to_all.15.spread = bf16[16,27,16,128]{3,2,1,0:T(8,128)(2,1)S(1)} all-to-all(bf16[16,27,16,128]{3,2,1,0:T(8,128)(2,1)S(1)} %add_convert_fusion), channel_id=1, replica_groups={{0,2,1,3,4,6,5,7,8,10,9,11,12,14,13,15},{128,130,129,131,132,134,133,13..., dimensions={0} | all-to-all | bytes 3538944 | tf_op jit(solution)/shard_map/all_to_all | solution.py:304
  79.1 1.6 %collective-permute-start.9 = (bf16[5,128,256]{2,1,0:T(8,128)(2,1)S(1)}, bf16[5,128,256]{2,1,0:T(8,128)(2,1)S(1)}, u32[]{:S(2)}, u32[]{:S(2)}) collective-permute-start(bf16[5,128,256]{2,1,0:T(8,128)(2,1)S(1)} %get-tuple-element.35), channel_id=1, source_target_pairs={{0,2},{1,3},{128,130},{129,131},{2,0},{3,1},{130,128},{131,129},{4... | collective-permute-start | bytes 983048 | tf_op jit(solution)/shard_map/ppermute | solution.py:84
  80.7 0.9 shard_map.108
  81.6 8.2 %all-to-all-start.1 = ((bf16[8,4,16,128]{3,2,1,0:T(8,128)(2,1)}), bf16[8,4,16,128]{3,2,1,0:T(8,128)(2,1)S(1)}, u32[]{:S(2)}, u32[]{:S(2)}) async-start(bf16[8,4,16,128]{3,2,1,0:T(8,128)(2,1)} %shard_map.108), calls=%async_computation.1 | async-start | bytes 262144 | tf_op jit(solution)/shard_map/all_to_all | solution.py:304
  89.7 0.7 collective-permute-start.10
  90.4 7.4 %all-to-all-done.1.spread = bf16[8,4,16,128]{3,2,1,0:T(8,128)(2,1)S(1)} async-done(((bf16[8,4,16,128]{3,2,1,0:T(8,128)(2,1)}), bf16[8,4,16,128]{3,2,1,0:T(8,128)(2,1)S(1)}, u32[]{:S(2)}, u32[]{:S(2)}) %all-to-all-start.1) | async-done | bytes 131104 | tf_op jit(solution)/shard_map/all_to_all | solution.py:304
  97.8 0.7 shard_map.109
  98.5 3.5 %all-to-all-start.2 = ((bf16[16,4,16,128]{3,2,1,0:T(8,128)(2,1)}), bf16[16,4,16,128]{3,2,1,0:T(8,128)(2,1)S(1)}, u32[]{:S(2)}, u32[]{:S(2)}) async-start(bf16[16,4,16,128]{3,2,1,0:T(8,128)(2,1)} %shard_map.109), calls=%async_computation.2 | async-start | bytes 524288 | tf_op jit(solution)/shard_map/all_to_all | solution.py:304
  102.1 0.0 collective-permute-done.9.first
  102.1 3.4 %collective-permute-start.11 = (bf16[6,128,256]{2,1,0:T(8,128)(2,1)S(1)}, bf16[6,128,256]{2,1,0:T(8,128)(2,1)S(1)}, u32[]{:S(2)}, u32[]{:S(2)}) collective-permute-start(bf16[6,128,256]{2,1,0:T(8,128)(2,1)S(1)} %slice_dynamic-update-slice_fusion), channel_id=1, source_target_pairs={{0,128},{1,129},{2,130},{3,131},{4,132},{5,133},{6,134},{7,135},{8... | collective-permute-start | bytes 1179656 | tf_op jit(solution)/shard_map/ppermute | solution.py:75
  105.5 5.8 %all-to-all-done.2 = bf16[16,4,16,128]{3,2,1,0:T(8,128)(2,1)S(1)} async-done(((bf16[16,4,16,128]{3,2,1,0:T(8,128)(2,1)}), bf16[16,4,16,128]{3,2,1,0:T(8,128)(2,1)S(1)}, u32[]{:S(2)}, u32[]{:S(2)}) %all-to-all-start.2) | async-done | bytes 262176 | tf_op jit(solution)/shard_map/all_to_all | solution.py:304
  111.3 2.3 %collective-permute-start.14 = (bf16[2,27,16,128]{3,2,1,0:T(8,128)(2,1)S(1)}, bf16[2,27,16,128]{3,2,1,0:T(8,128)(2,1)S(1)}, u32[]{:S(2)}, u32[]{:S(2)}) collective-permute-start(bf16[2,27,16,128]{3,2,1,0:T(8,128)(2,1)S(1)} %slice.24.refs_0_), channel_id=1, source_target_pairs={{0,12},{1,13},{2,14},{3,15},{4,0},{5,1},{6,2},{7,3},{8,4},{9,5},{1... | collective-permute-start | bytes 663560 | tf_op jit(solution)/shard_map/ppermute | solution.py:75
  113.6 0.7 collective-permute-start.12
  114.3 4.9 %collective-permute-start.15 = (bf16[2,27,16,128]{3,2,1,0:T(8,128)(2,1)S(1)}, bf16[2,27,16,128]{3,2,1,0:T(8,128)(2,1)S(1)}, u32[]{:S(2)}, u32[]{:S(2)}) collective-permute-start(bf16[2,27,16,128]{3,2,1,0:T(8,128)(2,1)S(1)} %slice.24.refs_0_), channel_id=1, source_target_pairs={{0,128},{1,129},{2,130},{3,131},{4,132},{5,133},{6,134},{7,135},{8... | collective-permute-start | bytes 663560 | tf_op jit(solution)/shard_map/ppermute | solution.py:75
  119.2 1.7 %shard_map.107 = bf16[8,128,256]{2,1,0:T(8,128)(2,1)} custom-call(s32[1,4,4]{2,1,0:T(4,128)S(1)} %copy-done.5, s32[1,1,4]{2,1,0:T(1,128)S(1)} %bitcast.20, f32[8,128,256]{2,1,0:T(8,128)S(1)} %get-tuple-element.29.local, bf16[6,128,256]{2,1,0:T(8,128)(2,1)S(1)} %collective-permute-done.11.from_x, bf16[5,128,256]{2,1,0:T(8,128)(2,1)S(1)} %collective-permute-done.9.first, ...), custom_call_target="tpu_custom_call" | custom-call | tf_op jit(solution)/shard_map/pallas_call | solution.py:32
  120.9 4.9 %collective-permute-start.17 = (bf16[2,27,16,128]{3,2,1,0:T(8,128)(2,1)S(1)}, bf16[2,27,16,128]{3,2,1,0:T(8,128)(2,1)S(1)}, u32[]{:S(2)}, u32[]{:S(2)}) collective-permute-start(bf16[2,27,16,128]{3,2,1,0:T(8,128)(2,1)S(1)} %collective-permute-done.13.refs_2_), channel_id=1, source_target_pairs={{0,128},{1,129},{2,130},{3,131},{4,132},{5,133},{6,134},{7,135},{8... | collective-permute-start | bytes 663560 | tf_op jit(solution)/shard_map/ppermute | solution.py:75
  125.8 2.3 %collective-permute-start.16 = (bf16[2,27,16,128]{3,2,1,0:T(8,128)(2,1)S(1)}, bf16[2,27,16,128]{3,2,1,0:T(8,128)(2,1)S(1)}, u32[]{:S(2)}, u32[]{:S(2)}) collective-permute-start(bf16[2,27,16,128]{3,2,1,0:T(8,128)(2,1)S(1)} %collective-permute-done.12.refs_1_), channel_id=1, source_target_pairs={{0,128},{1,129},{2,130},{3,131},{4,132},{5,133},{6,134},{7,135},{8... | collective-permute-start | bytes 663560 | tf_op jit(solution)/shard_map/ppermute | solution.py:75
  128.0 0.0 collective-permute-start.18
  128.1 1.1 collective-permute-done.16.refs_5_
  129.1 0.4 collective-permute-done.18.refs_7_
  129.5 2.7 %shard_map.110 = f32[27,256,128]{2,1,0:T(8,128)} custom-call(bf16[2,27,16,128]{3,2,1,0:T(8,128)(2,1)S(1)} %slice.24.refs_0_, bf16[2,27,16,128]{3,2,1,0:T(8,128)(2,1)S(1)} %collective-permute-done.12.refs_1_, bf16[2,27,16,128]{3,2,1,0:T(8,128)(2,1)S(1)} %collective-permute-done.13.refs_2_, bf16[2,27,16,128]{3,2,1,0:T(8,128)(2,1)S(1)} %collective-permute-done.14.refs_3_, ...), custom_call_target="tpu_custom_call" | custom-call | tf_op jit(solution)/shard_map/pallas_call | solution.py:391
  (32 shorter events, 0.1 us)
Async XLA Ops:
  0.6 31.3 %copy-start.6 = (s32[1,27,4]{1,2,0:T(4,128)S(1)}, s32[1,27,4]{1,2,0:T(4,128)}, u32[]{:S(2)}) copy-start(s32[1,27,4]{1,2,0:T(4,128)} %param.14) | copy-start | bytes 1300
  0.6 1.0 copy-start
  1.7 0.7 copy-start.4
  2.4 0.7 copy-start.7
  3.0 28.9 %copy-start.1 = (bf16[1024,256]{1,0:T(8,128)(2,1)S(1)}, bf16[1024,256]{1,0:T(8,128)(2,1)}, u32[]{:S(2)}) copy-start(bf16[1024,256]{1,0:T(8,128)(2,1)} %param.8) | copy-start | bytes 1572868
  3.0 28.9 %copy-start.2 = (s32[1,27,4,128]{3,2,1,0:T(4,128)S(1)}, s32[1,27,4,128]{3,2,1,0:T(4,128)}, u32[]{:S(2)}) copy-start(s32[1,27,4,128]{3,2,1,0:T(4,128)} %param.15) | copy-start | bytes 165892
  3.7 5.1 %collective-permute-start = (bf16[6,128,256]{2,1,0:T(8,128)(2,1)S(1)}, bf16[6,128,256]{2,1,0:T(8,128)(2,1)S(1)}, u32[]{:S(2)}, u32[]{:S(2)}) collective-permute-start(bf16[6,128,256]{2,1,0:T(8,128)(2,1)S(1)} %get-tuple-element.21), channel_id=1, source_target_pairs={{0,128},{1,129},{2,130},{3,131},{4,132},{5,133},{6,134},{7,135},{8... | collective-permute-start | bytes 1179656 | tf_op jit(solution)/shard_map/ppermute | solution.py:75
  8.0 6.8 %collective-permute-start.3 = (bf16[27,32,128]{2,1,0:T(8,128)(2,1)S(1)}, bf16[27,32,128]{2,1,0:T(8,128)(2,1)S(1)}, u32[]{:S(2)}, u32[]{:S(2)}) collective-permute-start(bf16[27,32,128]{2,1,0:T(8,128)(2,1)S(1)} %constant_dynamic-slice_fusion), channel_id=1, source_target_pairs={{0,1},{1,2},{2,3},{3,0},{4,5},{5,6},{6,7},{7,4},{8,9},{9,10},{10,1... | collective-permute-start | bytes 663560 | tf_op jit(solution)/shard_map/ppermute | solution.py:321
  8.8 18.5 %collective-permute-start.2 = (bf16[5,128,256]{2,1,0:T(8,128)(2,1)S(1)}, bf16[5,128,256]{2,1,0:T(8,128)(2,1)S(1)}, u32[]{:S(2)}, u32[]{:S(2)}) collective-permute-start(bf16[5,128,256]{2,1,0:T(8,128)(2,1)S(1)} %get-tuple-element.39), channel_id=1, source_target_pairs={{2,4},{3,5},{130,132},{131,133},{4,2},{5,3},{132,130},{133,131},{6... | collective-permute-start | bytes 983048 | tf_op jit(solution)/shard_map/ppermute | solution.py:84
  9.5 20.0 %collective-permute-start.1 = (bf16[5,128,256]{2,1,0:T(8,128)(2,1)S(1)}, bf16[5,128,256]{2,1,0:T(8,128)(2,1)S(1)}, u32[]{:S(2)}, u32[]{:S(2)}) collective-permute-start(bf16[5,128,256]{2,1,0:T(8,128)(2,1)S(1)} %get-tuple-element.40), channel_id=1, source_target_pairs={{0,2},{1,3},{128,130},{129,131},{2,0},{3,1},{130,128},{131,129},{4... | collective-permute-start | bytes 983048 | tf_op jit(solution)/shard_map/ppermute | solution.py:84
  14.8 12.5 %collective-permute-start.6 = (bf16[27,32,128]{2,1,0:T(8,128)(2,1)S(1)}, bf16[27,32,128]{2,1,0:T(8,128)(2,1)S(1)}, u32[]{:S(2)}, u32[]{:S(2)}) collective-permute-start(bf16[27,32,128]{2,1,0:T(8,128)(2,1)S(1)} %collective-permute-done.3), channel_id=1, source_target_pairs={{0,12},{1,13},{2,14},{3,15},{4,0},{5,1},{6,2},{7,3},{8,4},{9,5},{1... | collective-permute-start | bytes 663560 | tf_op jit(solution)/shard_map/ppermute | solution.py:75
  17.5 12.0 %collective-permute-start.5 = (bf16[27,32,128]{2,1,0:T(8,128)(2,1)S(1)}, bf16[27,32,128]{2,1,0:T(8,128)(2,1)S(1)}, u32[]{:S(2)}, u32[]{:S(2)}) collective-permute-start(bf16[27,32,128]{2,1,0:T(8,128)(2,1)S(1)} %collective-permute-done.3), channel_id=1, source_target_pairs={{0,8},{1,9},{2,10},{3,11},{4,12},{5,13},{6,14},{7,15},{8,0},{9,1},... | collective-permute-start | bytes 663560 | tf_op jit(solution)/shard_map/ppermute | solution.py:75
  17.9 13.2 %collective-permute-start.4 = (bf16[27,32,128]{2,1,0:T(8,128)(2,1)S(1)}, bf16[27,32,128]{2,1,0:T(8,128)(2,1)S(1)}, u32[]{:S(2)}, u32[]{:S(2)}) collective-permute-start(bf16[27,32,128]{2,1,0:T(8,128)(2,1)S(1)} %collective-permute-done.3), channel_id=1, source_target_pairs={{0,4},{1,5},{2,6},{3,7},{4,8},{5,9},{6,10},{7,11},{8,12},{9,13},{1... | collective-permute-start | bytes 663560 | tf_op jit(solution)/shard_map/ppermute | solution.py:75
  31.2 3.7 %collective-permute-start.7 = (bf16[4,27,32,128]{3,2,1,0:T(8,128)(2,1)S(1)}, bf16[4,27,32,128]{3,2,1,0:T(8,128)(2,1)S(1)}, u32[]{:S(2)}, u32[]{:S(2)}) collective-permute-start(bf16[4,27,32,128]{3,2,1,0:T(8,128)(2,1)S(1)} %pad_maximum_fusion.near), channel_id=1, source_target_pairs={{0,128},{1,129},{2,130},{3,131},{4,132},{5,133},{6,134},{7,135},{8... | collective-permute-start | bytes 2654216 | tf_op jit(solution)/shard_map/ppermute | solution.py:75
  31.9 3.0 %copy-start.3 = (bf16[27,256,128]{2,1,0:T(8,128)(2,1)S(1)}, bf16[27,256,128]{2,1,0:T(8,128)(2,1)}, u32[]{:S(2)}) copy-start(bf16[27,256,128]{2,1,0:T(8,128)(2,1)} %own.3) | copy-start | bytes 5308420
  31.9 3.0 %copy-start.9 = (bf16[1024,256]{1,0:T(8,128)(2,1)S(1)}, bf16[1024,256]{1,0:T(8,128)(2,1)}, u32[]{:S(2)}) copy-start(bf16[1024,256]{1,0:T(8,128)(2,1)} %param.10) | copy-start | bytes 1572868
  31.9 3.0 %copy-start.10 = (s32[1,27,4]{1,2,0:T(4,128)S(1)}, s32[1,27,4]{1,2,0:T(4,128)}, u32[]{:S(2)}) copy-start(s32[1,27,4]{1,2,0:T(4,128)} %param.13) | copy-start | bytes 1300
  41.7 6.0 %collective-permute-start.8 = (bf16[16,27,16,128]{3,2,1,0:T(8,128)(2,1)S(1)}, bf16[16,27,16,128]{3,2,1,0:T(8,128)(2,1)S(1)}, u32[]{:S(2)}, u32[]{:S(2)}) collective-permute-start(bf16[16,27,16,128]{3,2,1,0:T(8,128)(2,1)S(1)} %get-tuple-element.34), channel_id=1, source_target_pairs={{0,128},{1,129},{2,130},{3,131},{4,132},{5,133},{6,134},{7,135},{8... | collective-permute-start | bytes 5308424 | tf_op jit(solution)/shard_map/ppermute | solution.py:75
  79.1 40.1 %copy-start.5 = (s32[1,4,4]{2,1,0:T(4,128)S(1)}, s32[1,4,4]{2,1,0:T(4,128)}, u32[]{:S(2)}) copy-start(s32[1,4,4]{2,1,0:T(4,128)} %face.3) | copy-start | bytes 196
  79.1 40.1 %copy-start.8 = (s32[1,4,1]{1,2,0:T(1,128)S(1)}, s32[1,4,1]{1,2,0:T(1,128)}, u32[]{:S(2)}) copy-start(s32[1,4,1]{1,2,0:T(1,128)} %param.12) | copy-start | bytes 52
  79.1 23.0 %collective-permute-start.9 = (bf16[5,128,256]{2,1,0:T(8,128)(2,1)S(1)}, bf16[5,128,256]{2,1,0:T(8,128)(2,1)S(1)}, u32[]{:S(2)}, u32[]{:S(2)}) collective-permute-start(bf16[5,128,256]{2,1,0:T(8,128)(2,1)S(1)} %get-tuple-element.35), channel_id=1, source_target_pairs={{0,2},{1,3},{128,130},{129,131},{2,0},{3,1},{130,128},{131,129},{4... | collective-permute-start | bytes 983048 | tf_op jit(solution)/shard_map/ppermute | solution.py:84
  81.6 16.2 %all-to-all-start.1 = ((bf16[8,4,16,128]{3,2,1,0:T(8,128)(2,1)}), bf16[8,4,16,128]{3,2,1,0:T(8,128)(2,1)S(1)}, u32[]{:S(2)}, u32[]{:S(2)}) async-start(bf16[8,4,16,128]{3,2,1,0:T(8,128)(2,1)} %shard_map.108), calls=%async_computation.1 | async-start | bytes 262144 | tf_op jit(solution)/shard_map/all_to_all | solution.py:304
  89.7 12.3 %collective-permute-start.10 = (bf16[5,128,256]{2,1,0:T(8,128)(2,1)S(1)}, bf16[5,128,256]{2,1,0:T(8,128)(2,1)S(1)}, u32[]{:S(2)}, u32[]{:S(2)}) collective-permute-start(bf16[5,128,256]{2,1,0:T(8,128)(2,1)S(1)} %get-tuple-element.37), channel_id=1, source_target_pairs={{2,4},{3,5},{130,132},{131,133},{4,2},{5,3},{132,130},{133,131},{6... | collective-permute-start | bytes 983048 | tf_op jit(solution)/shard_map/ppermute | solution.py:84
  98.5 12.8 %all-to-all-start.2 = ((bf16[16,4,16,128]{3,2,1,0:T(8,128)(2,1)}), bf16[16,4,16,128]{3,2,1,0:T(8,128)(2,1)S(1)}, u32[]{:S(2)}, u32[]{:S(2)}) async-start(bf16[16,4,16,128]{3,2,1,0:T(8,128)(2,1)} %shard_map.109), calls=%async_computation.2 | async-start | bytes 524288 | tf_op jit(solution)/shard_map/all_to_all | solution.py:304
  102.1 17.1 %collective-permute-start.11 = (bf16[6,128,256]{2,1,0:T(8,128)(2,1)S(1)}, bf16[6,128,256]{2,1,0:T(8,128)(2,1)S(1)}, u32[]{:S(2)}, u32[]{:S(2)}) collective-permute-start(bf16[6,128,256]{2,1,0:T(8,128)(2,1)S(1)} %slice_dynamic-update-slice_fusion), channel_id=1, source_target_pairs={{0,128},{1,129},{2,130},{3,131},{4,132},{5,133},{6,134},{7,135},{8... | collective-permute-start | bytes 1179656 | tf_op jit(solution)/shard_map/ppermute | solution.py:75
  111.3 9.5 %collective-permute-start.14 = (bf16[2,27,16,128]{3,2,1,0:T(8,128)(2,1)S(1)}, bf16[2,27,16,128]{3,2,1,0:T(8,128)(2,1)S(1)}, u32[]{:S(2)}, u32[]{:S(2)}) collective-permute-start(bf16[2,27,16,128]{3,2,1,0:T(8,128)(2,1)S(1)} %slice.24.refs_0_), channel_id=1, source_target_pairs={{0,12},{1,13},{2,14},{3,15},{4,0},{5,1},{6,2},{7,3},{8,4},{9,5},{1... | collective-permute-start | bytes 663560 | tf_op jit(solution)/shard_map/ppermute | solution.py:75
  113.6 7.3 %collective-permute-start.13 = (bf16[2,27,16,128]{3,2,1,0:T(8,128)(2,1)S(1)}, bf16[2,27,16,128]{3,2,1,0:T(8,128)(2,1)S(1)}, u32[]{:S(2)}, u32[]{:S(2)}) collective-permute-start(bf16[2,27,16,128]{3,2,1,0:T(8,128)(2,1)S(1)} %slice.24.refs_0_), channel_id=1, source_target_pairs={{0,8},{1,9},{2,10},{3,11},{4,12},{5,13},{6,14},{7,15},{8,0},{9,1},... | collective-permute-start | bytes 663560 | tf_op jit(solution)/shard_map/ppermute | solution.py:75
  113.6 12.2 %collective-permute-start.12 = (bf16[2,27,16,128]{3,2,1,0:T(8,128)(2,1)S(1)}, bf16[2,27,16,128]{3,2,1,0:T(8,128)(2,1)S(1)}, u32[]{:S(2)}, u32[]{:S(2)}) collective-permute-start(bf16[2,27,16,128]{3,2,1,0:T(8,128)(2,1)S(1)} %slice.24.refs_0_), channel_id=1, source_target_pairs={{0,4},{1,5},{2,6},{3,7},{4,8},{5,9},{6,10},{7,11},{8,12},{9,13},{1... | collective-permute-start | bytes 663560 | tf_op jit(solution)/shard_map/ppermute | solution.py:75
  114.3 13.8 %collective-permute-start.15 = (bf16[2,27,16,128]{3,2,1,0:T(8,128)(2,1)S(1)}, bf16[2,27,16,128]{3,2,1,0:T(8,128)(2,1)S(1)}, u32[]{:S(2)}, u32[]{:S(2)}) collective-permute-start(bf16[2,27,16,128]{3,2,1,0:T(8,128)(2,1)S(1)} %slice.24.refs_0_), channel_id=1, source_target_pairs={{0,128},{1,129},{2,130},{3,131},{4,132},{5,133},{6,134},{7,135},{8... | collective-permute-start | bytes 663560 | tf_op jit(solution)/shard_map/ppermute | solution.py:75
  120.9 7.2 %collective-permute-start.17 = (bf16[2,27,16,128]{3,2,1,0:T(8,128)(2,1)S(1)}, bf16[2,27,16,128]{3,2,1,0:T(8,128)(2,1)S(1)}, u32[]{:S(2)}, u32[]{:S(2)}) collective-permute-start(bf16[2,27,16,128]{3,2,1,0:T(8,128)(2,1)S(1)} %collective-permute-done.13.refs_2_), channel_id=1, source_target_pairs={{0,128},{1,129},{2,130},{3,131},{4,132},{5,133},{6,134},{7,135},{8... | collective-permute-start | bytes 663560 | tf_op jit(solution)/shard_map/ppermute | solution.py:75
  125.8 3.4 %collective-permute-start.16 = (bf16[2,27,16,128]{3,2,1,0:T(8,128)(2,1)S(1)}, bf16[2,27,16,128]{3,2,1,0:T(8,128)(2,1)S(1)}, u32[]{:S(2)}, u32[]{:S(2)}) collective-permute-start(bf16[2,27,16,128]{3,2,1,0:T(8,128)(2,1)S(1)} %collective-permute-done.12.refs_1_), channel_id=1, source_target_pairs={{0,128},{1,129},{2,130},{3,131},{4,132},{5,133},{6,134},{7,135},{8... | collective-permute-start | bytes 663560 | tf_op jit(solution)/shard_map/ppermute | solution.py:75
  128.0 1.5 %collective-permute-start.18 = (bf16[2,27,16,128]{3,2,1,0:T(8,128)(2,1)S(1)}, bf16[2,27,16,128]{3,2,1,0:T(8,128)(2,1)S(1)}, u32[]{:S(2)}, u32[]{:S(2)}) collective-permute-start(bf16[2,27,16,128]{3,2,1,0:T(8,128)(2,1)S(1)} %collective-permute-done.14.refs_3_), channel_id=1, source_target_pairs={{0,128},{1,129},{2,130},{3,131},{4,132},{5,133},{6,134},{7,135},{8... | collective-permute-start | bytes 663560 | tf_op jit(solution)/shard_map/ppermute | solution.py:75

commit v6 on v5

--- a/solution.py
+++ b/solution.py
@@ -352,10 +352,11 @@
         pl.CostEstimate(flops=5_000_000_000, bytes_accessed=12_000_000, transcendentals=0),
     )
     got = shift(send, core=1)
+    paired = (keep.astype(F32) + got.astype(F32)).astype(BF)
     local, back_x, to_first, to_second = call(
         backward_kernel,
         pairs
-        + [("v", grad)]
+        + [("v", tie(grad, paired))]
         + [("v", v) for v in (weight, near, other)],
         [shape_of(NB, ROWS, C, dtype=F32), six, five, five],
         [
@@ -364,7 +365,6 @@
         ],
         pl.CostEstimate(flops=5_000_000_000, bytes_accessed=10_000_000, transcendentals=0),
     )
-    paired = (tie(keep, to_first).astype(F32) + got.astype(F32)).astype(BF)
     spread = exchange(paired, lambda c, x, y, z: (c, z))
     first = swap_y(tie(to_first, spread), 0)
     second = swap_y(tie(to_second, spread), 1)

time: 133 us -> 135 us (1.015)
  blocking collectives: 30.9 us -> 0 us
  waiting for transfers between devices: 27.4 us -> 42.7 us
  starting transfers between devices: 47.1 us -> 56.4 us
  local copies, waits for them, and re-layouts: 3.4 us -> 10.5 us
    all_to_all x1 -> x0, blocking collectives: 30.9 us -> none  [exchange(): lax.all_to_all(value, ALL, split_axis=0, concat_axis=0, axis_index_groups...]
    all_to_all x2 -> x3, waiting for transfers between devices: 13.1 us -> 24.8 us  [exchange(): lax.all_to_all(value, ALL, split_axis=0, concat_axis=0, axis_index_groups...]
    all_to_all x2 -> x3, starting transfers between devices: 11.7 us -> 19.5 us  [exchange(): lax.all_to_all(value, ALL, split_axis=0, concat_axis=0, axis_index_groups...]
    unnamed x22 -> x40, local copies, waits for them, and re-layouts: 2.41 us -> 9.49 us
    ppermute x14, waiting for transfers between devices: 12.1 us -> 15.7 us  [shift(): return lax.ppermute(value, ALL, torus_perm(move))]
    ppermute x4, starting transfers between devices: 8.28 us -> 10.7 us  [swap_y(): return lax.ppermute(value, ALL, pairs)]
  transfers between devices with their start and end apart: 21 -> 22, of which waited for: 8 -> 10; matrix products, arithmetic and copies ran while one was open for 1% -> 1% of each run, Pallas kernels for 9% -> 9%
where the time goes in v6:
time: 135 us; the launch traced here: 134 us
  starting transfers between devices  56.4 us (42%)
  waiting for transfers between devices  42.7 us (32%)
  Pallas kernels  22 us (16%)
  local copies, waits for them, and re-layouts  10.5 us (8%)
  other arithmetic  1.78 us (1%)
    ppermute x14, starting transfers between devices, shift(): return lax.ppermute(value, ALL, torus_perm(move))  25.5 us
    all_to_all x3, waiting for transfers between devices, exchange(): lax.all_to_all(value, ALL, split_axis=0, concat_axis=0, axis_index_groups...  24.8 us
    all_to_all x3, starting transfers between devices, exchange(): lax.all_to_all(value, ALL, split_axis=0, concat_axis=0, axis_index_groups...  19.5 us
    pallas_call x7, Pallas kernels, call(): pl.pallas_call(kernel, out_shape=[out for _, out in outs], in_specs=[plac...  19.2 us
    ppermute x14, waiting for transfers between devices, shift(): return lax.ppermute(value, ALL, torus_perm(move))  15.7 us
    ppermute x4, starting transfers between devices, swap_y(): return lax.ppermute(value, ALL, pairs)  10.7 us
    unnamed x40, local copies, waits for them, and re-layouts  9.49 us
    pallas_call x1, Pallas kernels, body(): pl.pallas_call(functools.partial(final_kernel, scale), grid=(3,), out_sha...  2.73 us
  transfers between devices with their start and end apart: 22, of which 10 were waited for; matrix products, arithmetic and copies ran while one was open for 1% of the time, Pallas kernels for 9%

profile of v6, /device:TPU:1, one launch (start us, length us, event | category | flops | bytes accessed | tf_op | source)
XLA Modules:
  0.0 134.3 jit_solution(12745315655819431802)
XLA Ops:
  0.7 1.0 copy-done
  1.7 0.7 copy-done.7
  2.4 0.7 copy-done.10
  3.0 0.7 shard_map.103
  3.7 3.3 %collective-permute-start = (bf16[6,128,256]{2,1,0:T(8,128)(2,1)S(1)}, bf16[6,128,256]{2,1,0:T(8,128)(2,1)S(1)}, u32[]{:S(2)}, u32[]{:S(2)}) collective-permute-start(bf16[6,128,256]{2,1,0:T(8,128)(2,1)S(1)} %get-tuple-element.21), channel_id=1, source_target_pairs={{0,128},{1,129},{2,130},{3,131},{4,132},{5,133},{6,134},{7,135},{8... | collective-permute-start | bytes 1179656 | tf_op jit(solution)/shard_map/ppermute | solution.py:75
  7.0 1.0 constant_dynamic-slice_fusion
  8.0 0.8 collective-permute-start.3
  8.8 0.7 collective-permute-start.2
  9.5 5.3 %collective-permute-start.1 = (bf16[5,128,256]{2,1,0:T(8,128)(2,1)S(1)}, bf16[5,128,256]{2,1,0:T(8,128)(2,1)S(1)}, u32[]{:S(2)}, u32[]{:S(2)}) collective-permute-start(bf16[5,128,256]{2,1,0:T(8,128)(2,1)S(1)} %get-tuple-element.40), channel_id=1, source_target_pairs={{0,2},{1,3},{128,130},{129,131},{2,0},{3,1},{130,128},{131,129},{4... | collective-permute-start | bytes 983048 | tf_op jit(solution)/shard_map/ppermute | solution.py:84
  14.8 2.7 %collective-permute-start.6 = (bf16[27,32,128]{2,1,0:T(8,128)(2,1)S(1)}, bf16[27,32,128]{2,1,0:T(8,128)(2,1)S(1)}, u32[]{:S(2)}, u32[]{:S(2)}) collective-permute-start(bf16[27,32,128]{2,1,0:T(8,128)(2,1)S(1)} %collective-permute-done.3), channel_id=1, source_target_pairs={{0,12},{1,13},{2,14},{3,15},{4,0},{5,1},{6,2},{7,3},{8,4},{9,5},{1... | collective-permute-start | bytes 663560 | tf_op jit(solution)/shard_map/ppermute | solution.py:75
  17.5 0.3 collective-permute-start.5
  17.9 0.4 collective-permute-start.4
  18.3 9.0 %collective-permute-done.6 = bf16[27,32,128]{2,1,0:T(8,128)(2,1)S(1)} collective-permute-done((bf16[27,32,128]{2,1,0:T(8,128)(2,1)S(1)}, bf16[27,32,128]{2,1,0:T(8,128)(2,1)S(1)}, u32[]{:S(2)}, u32[]{:S(2)}) %collective-permute-start.6) | collective-permute-done | bytes 221216 | tf_op jit(solution)/shard_map/ppermute | solution.py:75
  27.3 2.2 %collective-permute-done.1.first = bf16[5,128,256]{2,1,0:T(8,128)(2,1)S(1)} collective-permute-done((bf16[5,128,256]{2,1,0:T(8,128)(2,1)S(1)}, bf16[5,128,256]{2,1,0:T(8,128)(2,1)S(1)}, u32[]{:S(2)}, u32[]{:S(2)}) %collective-permute-start.1) | collective-permute-done | bytes 327712 | tf_op jit(solution)/shard_map/ppermute | solution.py:84
  29.6 1.5 %collective-permute-done.4 = bf16[27,32,128]{2,1,0:T(8,128)(2,1)S(1)} collective-permute-done((bf16[27,32,128]{2,1,0:T(8,128)(2,1)S(1)}, bf16[27,32,128]{2,1,0:T(8,128)(2,1)S(1)}, u32[]{:S(2)}, u32[]{:S(2)}) %collective-permute-start.4) | collective-permute-done | bytes 221216 | tf_op jit(solution)/shard_map/ppermute | solution.py:75
  31.2 0.9 collective-permute-start.7
  32.1 3.0 %shard_map.104.rows = bf16[27,512,256]{2,1,0:T(8,128)(2,1)S(1)} custom-call(s32[1,4,27]{2,1,0:T(4,128)S(1)} %bitcast.17, s32[27,4,128]{2,1,0:T(4,128)S(1)} %bitcast.15, bf16[8,128,256]{2,1,0:T(8,128)(2,1)S(1)} %bitcast.14, bf16[6,128,256]{2,1,0:T(8,128)(2,1)S(1)} %collective-permute-done.from_x, bf16[5,128,256]{2,1,0:T(8,128)(2,1)S(1)} %collective-permute-done.1.first, ...), custom_call_target="tpu_custom_call" | custom-call | flops 2000000000 | bytes 9000000 | tf_op jit(solution)/shard_map/pallas_call | solution.py:32
  35.2 6.7 %shard_map.105 = (bf16[8,128,256]{2,1,0:T(8,128)(2,1)}, bf16[8,128,256]{2,1,0:T(8,128)(2,1)S(1)}, bf16[16,27,16,128]{3,2,1,0:T(8,128)(2,1)S(1)}, bf16[16,27,16,128]{3,2,1,0:T(8,128)(2,1)S(1)}) custom-call(s32[1,4,27]{2,1,0:T(4,128)S(1)} %bitcast.22, bf16[27,512,256]{2,1,0:T(8,128)(2,1)S(1)} %shard_map.104.rows, bf16[27,256,128]{2,1,0:T(8,128)(2,1)S(1)} %copy-done.5, ...), custom_call_target="tpu_custom_call" | custom-call | flops 5000000000 | bytes 12000000 | tf_op jit(solution)/shard_map/pallas_call | solution.py:32
  42.0 0.8 copy-done.18
  42.8 3.6 %collective-permute-done.8 = bf16[16,27,16,128]{3,2,1,0:T(8,128)(2,1)S(1)} collective-permute-done((bf16[16,27,16,128]{3,2,1,0:T(8,128)(2,1)S(1)}, bf16[16,27,16,128]{3,2,1,0:T(8,128)(2,1)S(1)}, u32[]{:S(2)}, u32[]{:S(2)}) %collective-permute-start.8) | collective-permute-done | bytes 1769504 | tf_op jit(solution)/shard_map/ppermute | solution.py:75
  46.4 1.7 %add_convert_fusion = bf16[16,27,16,128]{3,2,1,0:T(8,128)(2,1)} fusion(bf16[16,27,16,128]{3,2,1,0:T(8,128)(2,1)S(1)} %collective-permute-done.8, bf16[16,27,16,128]{3,2,1,0:T(8,128)(2,1)S(1)} %get-tuple-element.29), kind=kLoop, calls=%fused_computation | loop fusion | flops 3538944 | bytes 5308416 | tf_op jit(solution)/shard_map/convert_element_type | solution.py:355
  48.1 7.7 %all-to-all-start = ((bf16[16,27,16,128]{3,2,1,0:T(8,128)(2,1)}), bf16[16,27,16,128]{3,2,1,0:T(8,128)(2,1)S(1)}, u32[]{:S(2)}, u32[]{:S(2)}) async-start(bf16[16,27,16,128]{3,2,1,0:T(8,128)(2,1)} %add_convert_fusion), calls=%async_computation | async-start | bytes 3538944 | tf_op jit(solution)/shard_map/all_to_all | solution.py:304
  55.8 1.2 copy-done.3
  56.9 1.5 %copy-done.6 = bf16[27,256,128]{2,1,0:T(8,128)(2,1)S(1)} copy-done((bf16[27,256,128]{2,1,0:T(8,128)(2,1)S(1)}, bf16[27,256,128]{2,1,0:T(8,128)(2,1)}, u32[]{:S(2)}) %copy-start.6) | copy-done | bytes 1769496
  58.4 1.2 copy-done.13
  59.6 1.0 copy-done.19
  60.6 5.6 %shard_map.106 = (f32[8,128,256]{2,1,0:T(8,128)S(1)}, bf16[6,128,256]{2,1,0:T(8,128)(2,1)S(1)}, bf16[5,128,256]{2,1,0:T(8,128)(2,1)S(1)}, bf16[5,128,256]{2,1,0:T(8,128)(2,1)S(1)}) custom-call(s32[1,4,27]{2,1,0:T(4,128)S(1)} %bitcast.23, s32[1,4,27]{2,1,0:T(4,128)S(1)} %bitcast.18, s32[27,4,128]{2,1,0:T(4,128)S(1)} %bitcast.16, ...), custom_call_target="tpu_custom_call" | custom-call | flops 5000000000 | bytes 10000000 | tf_op jit(solution)/shard_map/pallas_call | solution.py:32
  66.2 0.7 copy-done.15
  66.9 0.7 copy-done.16
  67.7 11.3 %all-to-all-done.spread = bf16[16,27,16,128]{3,2,1,0:T(8,128)(2,1)S(1)} async-done(((bf16[16,27,16,128]{3,2,1,0:T(8,128)(2,1)}), bf16[16,27,16,128]{3,2,1,0:T(8,128)(2,1)S(1)}, u32[]{:S(2)}, u32[]{:S(2)}) %all-to-all-start) | async-done | bytes 1769504 | tf_op jit(solution)/shard_map/all_to_all | solution.py:304
  79.0 4.0 %collective-permute-start.9 = (bf16[5,128,256]{2,1,0:T(8,128)(2,1)}, bf16[5,128,256]{2,1,0:T(8,128)(2,1)S(1)}, u32[]{:S(2)}, u32[]{:S(2)}) collective-permute-start(bf16[5,128,256]{2,1,0:T(8,128)(2,1)} %copy-done.16), channel_id=1, source_target_pairs={{0,2},{1,3},{128,130},{129,131},{2,0},{3,1},{130,128},{131,129},{4... | collective-permute-start | bytes 983048 | tf_op jit(solution)/shard_map/ppermute | solution.py:84
  83.0 0.9 shard_map.108
  83.9 8.3 %all-to-all-start.1 = ((bf16[8,4,16,128]{3,2,1,0:T(8,128)(2,1)}), bf16[8,4,16,128]{3,2,1,0:T(8,128)(2,1)S(1)}, u32[]{:S(2)}, u32[]{:S(2)}) async-start(bf16[8,4,16,128]{3,2,1,0:T(8,128)(2,1)} %shard_map.108), calls=%async_computation.1 | async-start | bytes 262144 | tf_op jit(solution)/shard_map/all_to_all | solution.py:304
  92.2 0.7 collective-permute-start.10
  92.9 7.3 %all-to-all-done.1.spread = bf16[8,4,16,128]{3,2,1,0:T(8,128)(2,1)S(1)} async-done(((bf16[8,4,16,128]{3,2,1,0:T(8,128)(2,1)}), bf16[8,4,16,128]{3,2,1,0:T(8,128)(2,1)S(1)}, u32[]{:S(2)}, u32[]{:S(2)}) %all-to-all-start.1) | async-done | bytes 131104 | tf_op jit(solution)/shard_map/all_to_all | solution.py:304
  100.1 0.7 shard_map.109
  100.9 3.5 %all-to-all-start.2 = ((bf16[16,4,16,128]{3,2,1,0:T(8,128)(2,1)}), bf16[16,4,16,128]{3,2,1,0:T(8,128)(2,1)S(1)}, u32[]{:S(2)}, u32[]{:S(2)}) async-start(bf16[16,4,16,128]{3,2,1,0:T(8,128)(2,1)} %shard_map.109), calls=%async_computation.2 | async-start | bytes 524288 | tf_op jit(solution)/shard_map/all_to_all | solution.py:304
  104.5 3.0 %collective-permute-start.11 = (bf16[6,128,256]{2,1,0:T(8,128)(2,1)S(1)}, bf16[6,128,256]{2,1,0:T(8,128)(2,1)S(1)}, u32[]{:S(2)}, u32[]{:S(2)}) collective-permute-start(bf16[6,128,256]{2,1,0:T(8,128)(2,1)S(1)} %slice_dynamic-update-slice_fusion), channel_id=1, source_target_pairs={{0,128},{1,129},{2,130},{3,131},{4,132},{5,133},{6,134},{7,135},{8... | collective-permute-start | bytes 1179656 | tf_op jit(solution)/shard_map/ppermute | solution.py:75
  107.5 6.2 %all-to-all-done.2 = bf16[16,4,16,128]{3,2,1,0:T(8,128)(2,1)S(1)} async-done(((bf16[16,4,16,128]{3,2,1,0:T(8,128)(2,1)}), bf16[16,4,16,128]{3,2,1,0:T(8,128)(2,1)S(1)}, u32[]{:S(2)}, u32[]{:S(2)}) %all-to-all-start.2) | async-done | bytes 262176 | tf_op jit(solution)/shard_map/all_to_all | solution.py:304
  113.7 2.6 %collective-permute-start.14 = (bf16[2,27,16,128]{3,2,1,0:T(8,128)(2,1)S(1)}, bf16[2,27,16,128]{3,2,1,0:T(8,128)(2,1)S(1)}, u32[]{:S(2)}, u32[]{:S(2)}) collective-permute-start(bf16[2,27,16,128]{3,2,1,0:T(8,128)(2,1)S(1)} %slice.24.refs_0_), channel_id=1, source_target_pairs={{0,12},{1,13},{2,14},{3,15},{4,0},{5,1},{6,2},{7,3},{8,4},{9,5},{1... | collective-permute-start | bytes 663560 | tf_op jit(solution)/shard_map/ppermute | solution.py:75
  116.3 0.7 collective-permute-start.12
  117.0 4.4 %collective-permute-start.15 = (bf16[2,27,16,128]{3,2,1,0:T(8,128)(2,1)S(1)}, bf16[2,27,16,128]{3,2,1,0:T(8,128)(2,1)S(1)}, u32[]{:S(2)}, u32[]{:S(2)}) collective-permute-start(bf16[2,27,16,128]{3,2,1,0:T(8,128)(2,1)S(1)} %slice.24.refs_0_), channel_id=1, source_target_pairs={{0,128},{1,129},{2,130},{3,131},{4,132},{5,133},{6,134},{7,135},{8... | collective-permute-start | bytes 663560 | tf_op jit(solution)/shard_map/ppermute | solution.py:75
  121.4 1.7 %shard_map.107 = bf16[8,128,256]{2,1,0:T(8,128)(2,1)} custom-call(s32[1,4,4]{2,1,0:T(4,128)S(1)} %copy-done.8, s32[1,1,4]{2,1,0:T(1,128)S(1)} %bitcast.20, f32[8,128,256]{2,1,0:T(8,128)S(1)} %get-tuple-element.32.local, bf16[6,128,256]{2,1,0:T(8,128)(2,1)S(1)} %collective-permute-done.11.from_x, bf16[5,128,256]{2,1,0:T(8,128)(2,1)S(1)} %collective-permute-done.9.first, ...), custom_call_target="tpu_custom_call" | custom-call | tf_op jit(solution)/shard_map/pallas_call | solution.py:32
  123.1 5.1 %collective-permute-start.17 = (bf16[2,27,16,128]{3,2,1,0:T(8,128)(2,1)S(1)}, bf16[2,27,16,128]{3,2,1,0:T(8,128)(2,1)S(1)}, u32[]{:S(2)}, u32[]{:S(2)}) collective-permute-start(bf16[2,27,16,128]{3,2,1,0:T(8,128)(2,1)S(1)} %collective-permute-done.13.refs_2_), channel_id=1, source_target_pairs={{0,128},{1,129},{2,130},{3,131},{4,132},{5,133},{6,134},{7,135},{8... | collective-permute-start | bytes 663560 | tf_op jit(solution)/shard_map/ppermute | solution.py:75
  128.2 1.9 %collective-permute-start.16 = (bf16[2,27,16,128]{3,2,1,0:T(8,128)(2,1)S(1)}, bf16[2,27,16,128]{3,2,1,0:T(8,128)(2,1)S(1)}, u32[]{:S(2)}, u32[]{:S(2)}) collective-permute-start(bf16[2,27,16,128]{3,2,1,0:T(8,128)(2,1)S(1)} %collective-permute-done.12.refs_1_), channel_id=1, source_target_pairs={{0,128},{1,129},{2,130},{3,131},{4,132},{5,133},{6,134},{7,135},{8... | collective-permute-start | bytes 663560 | tf_op jit(solution)/shard_map/ppermute | solution.py:75
  130.1 1.1 collective-permute-done.16.refs_5_
  131.2 0.4 collective-permute-done.18.refs_7_
  131.6 2.7 %shard_map.110 = f32[27,256,128]{2,1,0:T(8,128)} custom-call(bf16[2,27,16,128]{3,2,1,0:T(8,128)(2,1)S(1)} %slice.24.refs_0_, bf16[2,27,16,128]{3,2,1,0:T(8,128)(2,1)S(1)} %collective-permute-done.12.refs_1_, bf16[2,27,16,128]{3,2,1,0:T(8,128)(2,1)S(1)} %collective-permute-done.13.refs_2_, bf16[2,27,16,128]{3,2,1,0:T(8,128)(2,1)S(1)} %collective-permute-done.14.refs_3_, ...), custom_call_target="tpu_custom_call" | custom-call | tf_op jit(solution)/shard_map/pallas_call | solution.py:391
  (51 shorter events, 0.4 us)
Async XLA Ops:
  0.6 31.4 %copy-start.9 = (s32[1,27,4]{1,2,0:T(4,128)S(1)}, s32[1,27,4]{1,2,0:T(4,128)}, u32[]{:S(2)}) copy-start(s32[1,27,4]{1,2,0:T(4,128)} %param.14) | copy-start | bytes 1300
  0.6 1.0 copy-start
  1.7 0.7 copy-start.7
  2.4 0.7 copy-start.10
  3.0 29.1 %copy-start.1 = (bf16[1024,256]{1,0:T(8,128)(2,1)S(1)}, bf16[1024,256]{1,0:T(8,128)(2,1)}, u32[]{:S(2)}) copy-start(bf16[1024,256]{1,0:T(8,128)(2,1)} %param.8) | copy-start | bytes 1572868
  3.0 29.1 %copy-start.4 = (s32[1,27,4,128]{3,2,1,0:T(4,128)S(1)}, s32[1,27,4,128]{3,2,1,0:T(4,128)}, u32[]{:S(2)}) copy-start(s32[1,27,4,128]{3,2,1,0:T(4,128)} %param.15) | copy-start | bytes 165892
  3.7 5.1 %collective-permute-start = (bf16[6,128,256]{2,1,0:T(8,128)(2,1)S(1)}, bf16[6,128,256]{2,1,0:T(8,128)(2,1)S(1)}, u32[]{:S(2)}, u32[]{:S(2)}) collective-permute-start(bf16[6,128,256]{2,1,0:T(8,128)(2,1)S(1)} %get-tuple-element.21), channel_id=1, source_target_pairs={{0,128},{1,129},{2,130},{3,131},{4,132},{5,133},{6,134},{7,135},{8... | collective-permute-start | bytes 1179656 | tf_op jit(solution)/shard_map/ppermute | solution.py:75
  8.0 6.8 %collective-permute-start.3 = (bf16[27,32,128]{2,1,0:T(8,128)(2,1)S(1)}, bf16[27,32,128]{2,1,0:T(8,128)(2,1)S(1)}, u32[]{:S(2)}, u32[]{:S(2)}) collective-permute-start(bf16[27,32,128]{2,1,0:T(8,128)(2,1)S(1)} %constant_dynamic-slice_fusion), channel_id=1, source_target_pairs={{0,1},{1,2},{2,3},{3,0},{4,5},{5,6},{6,7},{7,4},{8,9},{9,10},{10,1... | collective-permute-start | bytes 663560 | tf_op jit(solution)/shard_map/ppermute | solution.py:321
  8.8 18.5 %collective-permute-start.2 = (bf16[5,128,256]{2,1,0:T(8,128)(2,1)S(1)}, bf16[5,128,256]{2,1,0:T(8,128)(2,1)S(1)}, u32[]{:S(2)}, u32[]{:S(2)}) collective-permute-start(bf16[5,128,256]{2,1,0:T(8,128)(2,1)S(1)} %get-tuple-element.39), channel_id=1, source_target_pairs={{2,4},{3,5},{130,132},{131,133},{4,2},{5,3},{132,130},{133,131},{6... | collective-permute-start | bytes 983048 | tf_op jit(solution)/shard_map/ppermute | solution.py:84
  9.5 20.0 %collective-permute-start.1 = (bf16[5,128,256]{2,1,0:T(8,128)(2,1)S(1)}, bf16[5,128,256]{2,1,0:T(8,128)(2,1)S(1)}, u32[]{:S(2)}, u32[]{:S(2)}) collective-permute-start(bf16[5,128,256]{2,1,0:T(8,128)(2,1)S(1)} %get-tuple-element.40), channel_id=1, source_target_pairs={{0,2},{1,3},{128,130},{129,131},{2,0},{3,1},{130,128},{131,129},{4... | collective-permute-start | bytes 983048 | tf_op jit(solution)/shard_map/ppermute | solution.py:84
  14.8 12.5 %collective-permute-start.6 = (bf16[27,32,128]{2,1,0:T(8,128)(2,1)S(1)}, bf16[27,32,128]{2,1,0:T(8,128)(2,1)S(1)}, u32[]{:S(2)}, u32[]{:S(2)}) collective-permute-start(bf16[27,32,128]{2,1,0:T(8,128)(2,1)S(1)} %collective-permute-done.3), channel_id=1, source_target_pairs={{0,12},{1,13},{2,14},{3,15},{4,0},{5,1},{6,2},{7,3},{8,4},{9,5},{1... | collective-permute-start | bytes 663560 | tf_op jit(solution)/shard_map/ppermute | solution.py:75
  17.5 12.0 %collective-permute-start.5 = (bf16[27,32,128]{2,1,0:T(8,128)(2,1)S(1)}, bf16[27,32,128]{2,1,0:T(8,128)(2,1)S(1)}, u32[]{:S(2)}, u32[]{:S(2)}) collective-permute-start(bf16[27,32,128]{2,1,0:T(8,128)(2,1)S(1)} %collective-permute-done.3), channel_id=1, source_target_pairs={{0,8},{1,9},{2,10},{3,11},{4,12},{5,13},{6,14},{7,15},{8,0},{9,1},... | collective-permute-start | bytes 663560 | tf_op jit(solution)/shard_map/ppermute | solution.py:75
  17.9 13.2 %collective-permute-start.4 = (bf16[27,32,128]{2,1,0:T(8,128)(2,1)S(1)}, bf16[27,32,128]{2,1,0:T(8,128)(2,1)S(1)}, u32[]{:S(2)}, u32[]{:S(2)}) collective-permute-start(bf16[27,32,128]{2,1,0:T(8,128)(2,1)S(1)} %collective-permute-done.3), channel_id=1, source_target_pairs={{0,4},{1,5},{2,6},{3,7},{4,8},{5,9},{6,10},{7,11},{8,12},{9,13},{1... | collective-permute-start | bytes 663560 | tf_op jit(solution)/shard_map/ppermute | solution.py:75
  31.2 4.0 %copy-start.2 = (bf16[4,27,32,128]{3,2,1,0:T(8,128)(2,1)}, bf16[4,27,32,128]{3,2,1,0:T(8,128)(2,1)S(1)}, u32[]{:S(2)}) copy-start(bf16[4,27,32,128]{3,2,1,0:T(8,128)(2,1)S(1)} %pad_maximum_fusion.near) | copy-start | bytes 2654212
  31.2 3.9 %collective-permute-start.7 = (bf16[4,27,32,128]{3,2,1,0:T(8,128)(2,1)S(1)}, bf16[4,27,32,128]{3,2,1,0:T(8,128)(2,1)S(1)}, u32[]{:S(2)}, u32[]{:S(2)}) collective-permute-start(bf16[4,27,32,128]{3,2,1,0:T(8,128)(2,1)S(1)} %pad_maximum_fusion.near), channel_id=1, source_target_pairs={{0,128},{1,129},{2,130},{3,131},{4,132},{5,133},{6,134},{7,135},{8... | collective-permute-start | bytes 2654216 | tf_op jit(solution)/shard_map/ppermute | solution.py:75
  32.1 3.1 %copy-start.5 = (bf16[27,256,128]{2,1,0:T(8,128)(2,1)S(1)}, bf16[27,256,128]{2,1,0:T(8,128)(2,1)}, u32[]{:S(2)}) copy-start(bf16[27,256,128]{2,1,0:T(8,128)(2,1)} %own.3) | copy-start | bytes 5308420
  32.1 3.1 %copy-start.14 = (bf16[1024,256]{1,0:T(8,128)(2,1)S(1)}, bf16[1024,256]{1,0:T(8,128)(2,1)}, u32[]{:S(2)}) copy-start(bf16[1024,256]{1,0:T(8,128)(2,1)} %param.10) | copy-start | bytes 1572868
  32.1 3.1 %copy-start.17 = (s32[1,27,4]{1,2,0:T(4,128)S(1)}, s32[1,27,4]{1,2,0:T(4,128)}, u32[]{:S(2)}) copy-start(s32[1,27,4]{1,2,0:T(4,128)} %param.13) | copy-start | bytes 1300
  35.1 6.8 %copy-start.12 = (bf16[4,27,32,128]{3,2,1,0:T(8,128)(2,1)}, bf16[4,27,32,128]{3,2,1,0:T(8,128)(2,1)S(1)}, u32[]{:S(2)}) copy-start(bf16[4,27,32,128]{3,2,1,0:T(8,128)(2,1)S(1)} %collective-permute-done.7.other) | copy-start | bytes 2654212
  41.9 0.8 copy-start.18
  42.7 3.7 %collective-permute-start.8 = (bf16[16,27,16,128]{3,2,1,0:T(8,128)(2,1)S(1)}, bf16[16,27,16,128]{3,2,1,0:T(8,128)(2,1)S(1)}, u32[]{:S(2)}, u32[]{:S(2)}) collective-permute-start(bf16[16,27,16,128]{3,2,1,0:T(8,128)(2,1)S(1)} %get-tuple-element.30), channel_id=1, source_target_pairs={{0,128},{1,129},{2,130},{3,131},{4,132},{5,133},{6,134},{7,135},{8... | collective-permute-start | bytes 5308424 | tf_op jit(solution)/shard_map/ppermute | solution.py:75
  48.1 30.9 %all-to-all-start = ((bf16[16,27,16,128]{3,2,1,0:T(8,128)(2,1)}), bf16[16,27,16,128]{3,2,1,0:T(8,128)(2,1)S(1)}, u32[]{:S(2)}, u32[]{:S(2)}) async-start(bf16[16,27,16,128]{3,2,1,0:T(8,128)(2,1)} %add_convert_fusion), calls=%async_computation | async-start | bytes 3538944 | tf_op jit(solution)/shard_map/all_to_all | solution.py:304
  55.8 1.2 copy-start.3
  56.9 1.5 %copy-start.6 = (bf16[27,256,128]{2,1,0:T(8,128)(2,1)S(1)}, bf16[27,256,128]{2,1,0:T(8,128)(2,1)}, u32[]{:S(2)}) copy-start(bf16[27,256,128]{2,1,0:T(8,128)(2,1)} %own.3) | copy-start | bytes 5308420
  58.4 1.2 copy-start.13
  59.6 1.0 copy-start.19
  66.2 0.7 copy-start.15
  66.9 0.7 copy-start.16
  79.0 42.4 %copy-start.8 = (s32[1,4,4]{2,1,0:T(4,128)S(1)}, s32[1,4,4]{2,1,0:T(4,128)}, u32[]{:S(2)}) copy-start(s32[1,4,4]{2,1,0:T(4,128)} %face.3) | copy-start | bytes 196
  79.0 42.4 %copy-start.11 = (s32[1,4,1]{1,2,0:T(1,128)S(1)}, s32[1,4,1]{1,2,0:T(1,128)}, u32[]{:S(2)}) copy-start(s32[1,4,1]{1,2,0:T(1,128)} %param.12) | copy-start | bytes 52
  79.0 25.4 %collective-permute-start.9 = (bf16[5,128,256]{2,1,0:T(8,128)(2,1)}, bf16[5,128,256]{2,1,0:T(8,128)(2,1)S(1)}, u32[]{:S(2)}, u32[]{:S(2)}) collective-permute-start(bf16[5,128,256]{2,1,0:T(8,128)(2,1)} %copy-done.16), channel_id=1, source_target_pairs={{0,2},{1,3},{128,130},{129,131},{2,0},{3,1},{130,128},{131,129},{4... | collective-permute-start | bytes 983048 | tf_op jit(solution)/shard_map/ppermute | solution.py:84
  83.9 16.2 %all-to-all-start.1 = ((bf16[8,4,16,128]{3,2,1,0:T(8,128)(2,1)}), bf16[8,4,16,128]{3,2,1,0:T(8,128)(2,1)S(1)}, u32[]{:S(2)}, u32[]{:S(2)}) async-start(bf16[8,4,16,128]{3,2,1,0:T(8,128)(2,1)} %shard_map.108), calls=%async_computation.1 | async-start | bytes 262144 | tf_op jit(solution)/shard_map/all_to_all | solution.py:304
  92.2 12.2 %collective-permute-start.10 = (bf16[5,128,256]{2,1,0:T(8,128)(2,1)}, bf16[5,128,256]{2,1,0:T(8,128)(2,1)S(1)}, u32[]{:S(2)}, u32[]{:S(2)}) collective-permute-start(bf16[5,128,256]{2,1,0:T(8,128)(2,1)} %copy-done.15), channel_id=1, source_target_pairs={{2,4},{3,5},{130,132},{131,133},{4,2},{5,3},{132,130},{133,131},{6... | collective-permute-start | bytes 983048 | tf_op jit(solution)/shard_map/ppermute | solution.py:84
  100.9 12.8 %all-to-all-start.2 = ((bf16[16,4,16,128]{3,2,1,0:T(8,128)(2,1)}), bf16[16,4,16,128]{3,2,1,0:T(8,128)(2,1)S(1)}, u32[]{:S(2)}, u32[]{:S(2)}) async-start(bf16[16,4,16,128]{3,2,1,0:T(8,128)(2,1)} %shard_map.109), calls=%async_computation.2 | async-start | bytes 524288 | tf_op jit(solution)/shard_map/all_to_all | solution.py:304
  104.5 16.9 %collective-permute-start.11 = (bf16[6,128,256]{2,1,0:T(8,128)(2,1)S(1)}, bf16[6,128,256]{2,1,0:T(8,128)(2,1)S(1)}, u32[]{:S(2)}, u32[]{:S(2)}) collective-permute-start(bf16[6,128,256]{2,1,0:T(8,128)(2,1)S(1)} %slice_dynamic-update-slice_fusion), channel_id=1, source_target_pairs={{0,128},{1,129},{2,130},{3,131},{4,132},{5,133},{6,134},{7,135},{8... | collective-permute-start | bytes 1179656 | tf_op jit(solution)/shard_map/ppermute | solution.py:75
  113.7 9.4 %collective-permute-start.14 = (bf16[2,27,16,128]{3,2,1,0:T(8,128)(2,1)S(1)}, bf16[2,27,16,128]{3,2,1,0:T(8,128)(2,1)S(1)}, u32[]{:S(2)}, u32[]{:S(2)}) collective-permute-start(bf16[2,27,16,128]{3,2,1,0:T(8,128)(2,1)S(1)} %slice.24.refs_0_), channel_id=1, source_target_pairs={{0,12},{1,13},{2,14},{3,15},{4,0},{5,1},{6,2},{7,3},{8,4},{9,5},{1... | collective-permute-start | bytes 663560 | tf_op jit(solution)/shard_map/ppermute | solution.py:75
  116.3 6.8 %collective-permute-start.13 = (bf16[2,27,16,128]{3,2,1,0:T(8,128)(2,1)S(1)}, bf16[2,27,16,128]{3,2,1,0:T(8,128)(2,1)S(1)}, u32[]{:S(2)}, u32[]{:S(2)}) collective-permute-start(bf16[2,27,16,128]{3,2,1,0:T(8,128)(2,1)S(1)} %slice.24.refs_0_), channel_id=1, source_target_pairs={{0,8},{1,9},{2,10},{3,11},{4,12},{5,13},{6,14},{7,15},{8,0},{9,1},... | collective-permute-start | bytes 663560 | tf_op jit(solution)/shard_map/ppermute | solution.py:75
  116.3 11.9 %collective-permute-start.12 = (bf16[2,27,16,128]{3,2,1,0:T(8,128)(2,1)S(1)}, bf16[2,27,16,128]{3,2,1,0:T(8,128)(2,1)S(1)}, u32[]{:S(2)}, u32[]{:S(2)}) collective-permute-start(bf16[2,27,16,128]{3,2,1,0:T(8,128)(2,1)S(1)} %slice.24.refs_0_), channel_id=1, source_target_pairs={{0,4},{1,5},{2,6},{3,7},{4,8},{5,9},{6,10},{7,11},{8,12},{9,13},{1... | collective-permute-start | bytes 663560 | tf_op jit(solution)/shard_map/ppermute | solution.py:75
  117.0 13.1 %collective-permute-start.15 = (bf16[2,27,16,128]{3,2,1,0:T(8,128)(2,1)S(1)}, bf16[2,27,16,128]{3,2,1,0:T(8,128)(2,1)S(1)}, u32[]{:S(2)}, u32[]{:S(2)}) collective-permute-start(bf16[2,27,16,128]{3,2,1,0:T(8,128)(2,1)S(1)} %slice.24.refs_0_), channel_id=1, source_target_pairs={{0,128},{1,129},{2,130},{3,131},{4,132},{5,133},{6,134},{7,135},{8... | collective-permute-start | bytes 663560 | tf_op jit(solution)/shard_map/ppermute | solution.py:75
  123.1 7.0 %collective-permute-start.17 = (bf16[2,27,16,128]{3,2,1,0:T(8,128)(2,1)S(1)}, bf16[2,27,16,128]{3,2,1,0:T(8,128)(2,1)S(1)}, u32[]{:S(2)}, u32[]{:S(2)}) collective-permute-start(bf16[2,27,16,128]{3,2,1,0:T(8,128)(2,1)S(1)} %collective-permute-done.13.refs_2_), channel_id=1, source_target_pairs={{0,128},{1,129},{2,130},{3,131},{4,132},{5,133},{6,134},{7,135},{8... | collective-permute-start | bytes 663560 | tf_op jit(solution)/shard_map/ppermute | solution.py:75
  128.2 3.0 %collective-permute-start.16 = (bf16[2,27,16,128]{3,2,1,0:T(8,128)(2,1)S(1)}, bf16[2,27,16,128]{3,2,1,0:T(8,128)(2,1)S(1)}, u32[]{:S(2)}, u32[]{:S(2)}) collective-permute-start(bf16[2,27,16,128]{3,2,1,0:T(8,128)(2,1)S(1)} %collective-permute-done.12.refs_1_), channel_id=1, source_target_pairs={{0,128},{1,129},{2,130},{3,131},{4,132},{5,133},{6,134},{7,135},{8... | collective-permute-start | bytes 663560 | tf_op jit(solution)/shard_map/ppermute | solution.py:75
  130.1 1.5 %collective-permute-start.18 = (bf16[2,27,16,128]{3,2,1,0:T(8,128)(2,1)S(1)}, bf16[2,27,16,128]{3,2,1,0:T(8,128)(2,1)S(1)}, u32[]{:S(2)}, u32[]{:S(2)}) collective-permute-start(bf16[2,27,16,128]{3,2,1,0:T(8,128)(2,1)S(1)} %collective-permute-done.14.refs_3_), channel_id=1, source_target_pairs={{0,128},{1,129},{2,130},{3,131},{4,132},{5,133},{6,134},{7,135},{8... | collective-permute-start | bytes 663560 | tf_op jit(solution)/shard_map/ppermute | solution.py:75
